TPU v7x, 32 devices: a whole 2x2x4 slice. The times are simulated.
32 devices in a mesh: groups: 2 (over y), tm: 4 (over z), space: 2 (over x), pair: 2 (over core).
Axes of the slice: x: 2, y: 2, z: 4, core: 2. Of those that a mesh axis runs over, the one named last changes fastest.
Arguments:
- link_field: float32 [4, 4, 16, 16, 4, 256], P(None, None, 'tm', 'space', 'pair', 'groups'), parts along dimension 5, may hold values from -1 to 1, as said below
Outputs:
- rotated_links: float32 [3, 4, 16, 16, 4, 256], P(None, None, 'tm', 'space', 'pair', 'groups'), parts along dimension 5
There are 2 independent parts, one for each index of `groups`. A program takes and returns all parts, laid end to end along the dimension named above; each array names one. Nothing has to cross between parts.
Inputs may be any that keep to these rules, and one draw needn't show every extreme that they name: `link_field`: every link is a unit quaternion: its four components' squares sum to one.
All inputs are finite; a program needn't handle non-finite values.
Results may differ from a plain program's by a relative error of at most 0.0001.
Values sent between devices are 32-bit elements; how exact they have to be, the bound alone decides.
No kernel may reach another device: no remote copies, remote signals or barrier semaphores. Data moves between devices by JAX's collectives and lax.ppermute only.
A program may use at most 64 MiB of HBM per device.

v0:
```python
import jax
import jax.numpy as jnp
from jax import lax
from jax.sharding import PartitionSpec as P

SWEEPS = 2


smear_weight = 0.1


def with_halo(x, sides, width):
    for axis, dim in sides:
        size, length = (lax.axis_size(axis), x.shape[dim])
        up = [(i, (i + 1) % size) for i in range(size)]
        down = [(j, i) for i, j in up]
        last = lax.slice_in_dim(x, length - width, length, axis=dim)
        first = lax.slice_in_dim(x, 0, width, axis=dim)
        before = lax.ppermute(last, axis, up)
        after = lax.ppermute(first, axis, down)
        x = jnp.concatenate([before, x, after], axis=dim)
    return x


def carried_in(part, axis, combine, identity):
    place = lax.axis_index(axis)
    gathered = lax.all_gather(part, axis)
    state = jnp.zeros_like(part) + jnp.asarray(identity, part.dtype)

    def one(lap, state):
        return combine(state, lax.dynamic_index_in_dim(gathered, lap, 0, False))

    return lax.fori_loop(0, place, one, state)


def shifted_2(value, axis, steps):
    count = lax.axis_size(axis)
    pairs = [(source, (source + steps) % count) for source in range(count)]
    return lax.ppermute(value, axis, pairs)


def quat_mul(former, latter):
    return jnp.stack(
        [
            former[0] * latter[0]
            - former[1] * latter[1]
            - former[2] * latter[2]
            - former[3] * latter[3],
            former[0] * latter[1]
            + former[1] * latter[0]
            + former[2] * latter[3]
            - former[3] * latter[2],
            former[0] * latter[2]
            - former[1] * latter[3]
            + former[2] * latter[0]
            + former[3] * latter[1],
            former[0] * latter[3]
            + former[1] * latter[2]
            - former[2] * latter[1]
            + former[3] * latter[0],
        ]
    )


def quat_conj(quat_field):
    return jnp.concatenate([quat_field[:1], -quat_field[1:]], axis=0)


def unit_step(direction):
    return tuple((1 if slot == direction else 0 for slot in range(4)))


def shifted(quat_field, offset):
    cropped = quat_field[
        :,
        1 + offset[0] : quat_field.shape[1] - 1 + offset[0],
        1 + offset[1] : quat_field.shape[2] - 1 + offset[1],
        1 + offset[2] : quat_field.shape[3] - 1 + offset[2],
        :,
    ]
    if offset[3] != 0:
        cropped = jnp.roll(cropped, -offset[3], axis=-1)
    return cropped


def smear_padded(padded):
    anchor = (0, 0, 0, 0)
    results = []
    for lead_dir in range(4):
        current = shifted(padded[lead_dir], anchor)
        staple_sum = jnp.zeros_like(current)
        forward = unit_step(lead_dir)
        for side_dir in range(4):
            if side_dir == lead_dir:
                continue
            across = unit_step(side_dir)
            backward = tuple((-value for value in across))
            diagonal = tuple((backward[slot] + forward[slot] for slot in range(4)))
            upper_path = quat_mul(
                quat_mul(shifted(padded[side_dir], anchor), shifted(padded[lead_dir], across)),
                quat_conj(shifted(padded[side_dir], forward)),
            )
            lower_path = quat_mul(
                quat_mul(
                    quat_conj(shifted(padded[side_dir], backward)),
                    shifted(padded[lead_dir], backward),
                ),
                shifted(padded[side_dir], diagonal),
            )
            staple_sum = staple_sum + upper_path + lower_path
        combined = current + smear_weight * staple_sum
        results.append(combined / jnp.sqrt(jnp.sum(combined * combined, axis=0, keepdims=True)))
    return jnp.stack(results)


def on_device(link_field):
    smeared = link_field
    for sweep_index in range(SWEEPS):
        padded = with_halo(smeared, (("tm", 2), ("space", 3), ("pair", 4)), 1)
        smeared = smear_padded(padded)
    temporal = smeared[0]
    local_prefix = lax.associative_scan(quat_mul, temporal, axis=1)
    slab_total = local_prefix[:, -1]
    identity = jnp.concatenate(
        [jnp.ones_like(slab_total[:1]), jnp.zeros_like(slab_total[1:])], axis=0
    )
    carry_in = carried_in(slab_total, "tm", quat_mul, identity)
    inclusive = quat_mul(carry_in[:, None], local_prefix)
    gauge_field = jnp.concatenate([carry_in[:, None], inclusive[:, :-1]], axis=1)
    next_first = shifted_2(gauge_field[:, :, :1], "space", -1)
    next_second = shifted_2(gauge_field[:, :, :, :1], "pair", -1)
    neighbours = [
        jnp.concatenate([gauge_field[:, :, 1:], next_first], axis=2),
        jnp.concatenate([gauge_field[:, :, :, 1:], next_second], axis=3),
        jnp.roll(gauge_field, -1, axis=4),
    ]
    rotated = []
    for spatial in range(1, 4):
        rotated.append(
            quat_mul(quat_mul(gauge_field, smeared[spatial]), quat_conj(neighbours[spatial - 1]))
        )
    return jnp.stack(rotated)


def solution(mesh):
    in_specs = (P(None, None, "tm", "space", "pair", "groups"),)
    out_specs = P(None, None, "tm", "space", "pair", "groups")
    return jax.shard_map(
        on_device, mesh=mesh, in_specs=in_specs, out_specs=out_specs, check_vma=False
    )
```

profile of v0, /device:TPU:0, one launch (start us, length us, event | category | flops | bytes accessed | tf_op | source)
XLA Modules:
  0.0 103.2 jit_solution(4547737255178541874)
XLA Ops:
  0.0 1.0 fusion.192
  1.0 3.1 %collective-permute-start = (f32[4,4,1,8,2,128]{5,3,4,2,1,0:T(8,128)S(1)}, f32[4,4,1,8,2,128]{5,3,4,2,1,0:T(8,128)S(1)}, u32[]{:S(2)}, u32[]{:S(2)}) collective-permute-start(f32[4,4,1,8,2,128]{5,3,4,2,1,0:T(8,128)S(1)} %copy.80), channel_id=1, source_target_pairs={{0,4},{4,8},{8,12},{12,0},{1,5},{5,9},{9,13},{13,1},{2,6},{6,10},{... | collective-permute-start | bytes 393224 | tf_op jit(solution)/shard_map/ppermute | solution.py:19
  4.1 2.1 %collective-permute-start.1 = (f32[4,4,1,8,2,128]{5,3,4,2,1,0:T(8,128)S(1)}, f32[4,4,1,8,2,128]{5,3,4,2,1,0:T(8,128)S(1)}, u32[]{:S(2)}, u32[]{:S(2)}) collective-permute-start(f32[4,4,1,8,2,128]{5,3,4,2,1,0:T(8,128)S(1)} %copy.81), channel_id=1, source_target_pairs={{4,0},{8,4},{12,8},{0,12},{5,1},{9,5},{13,9},{1,13},{6,2},{10,6},{... | collective-permute-start | bytes 393224 | tf_op jit(solution)/shard_map/ppermute | solution.py:20
  6.2 4.2 %collective-permute-done = f32[4,4,1,8,2,128]{5,3,4,2,1,0:T(8,128)S(1)} collective-permute-done((f32[4,4,1,8,2,128]{5,3,4,2,1,0:T(8,128)S(1)}, f32[4,4,1,8,2,128]{5,3,4,2,1,0:T(8,128)S(1)}, u32[]{:S(2)}, u32[]{:S(2)}) %collective-permute-start) | collective-permute-done | bytes 131104 | tf_op jit(solution)/shard_map/ppermute | solution.py:19
  10.5 1.1 %constant_dynamic-update-slice_fusion.1 = f32[4,4,6,8,2,128]{5,3,4,2,1,0:T(8,128)S(1)} fusion(f32[4,4,6,8,2,128]{5,3,4,2,1,0:T(8,128)S(1)} %constant_dynamic-update-slice_fusion.2, f32[4,4,4,8,2,128]{5,4,3,2,1,0:T(2,128)} %param.3), kind=kLoop, calls=%fused_computation.850 | loop fusion | bytes 1048576
  12.1 1.6 %collective-permute-start.3 = (f32[4,4,6,1,2,128]{5,3,4,2,1,0:T(1,128)S(1)}, f32[4,4,6,1,2,128]{5,3,4,2,1,0:T(1,128)S(1)}, u32[]{:S(2)}, u32[]{:S(2)}) collective-permute-start(f32[4,4,6,1,2,128]{5,3,4,2,1,0:T(1,128)S(1)} %get-tuple-element.572), channel_id=1, source_target_pairs={{2,0},{0,2},{3,1},{1,3},{6,4},{4,6},{7,5},{5,7},{10,8},{8,10},{11,... | collective-permute-start | bytes 294920 | tf_op jit(solution)/shard_map/ppermute | solution.py:20
  14.2 3.3 %collective-permute-done.3 = f32[4,4,6,1,2,128]{5,3,4,2,1,0:T(1,128)S(1)} collective-permute-done((f32[4,4,6,1,2,128]{5,3,4,2,1,0:T(1,128)S(1)}, f32[4,4,6,1,2,128]{5,3,4,2,1,0:T(1,128)S(1)}, u32[]{:S(2)}, u32[]{:S(2)}) %collective-permute-start.3) | collective-permute-done | bytes 98336 | tf_op jit(solution)/shard_map/ppermute | solution.py:20
  17.5 1.1 %collective-permute-done.2 = f32[4,4,6,1,2,128]{5,3,4,2,1,0:T(1,128)S(1)} collective-permute-done((f32[4,4,6,1,2,128]{5,3,4,2,1,0:T(1,128)S(1)}, f32[4,4,6,1,2,128]{5,3,4,2,1,0:T(1,128)S(1)}, u32[]{:S(2)}, u32[]{:S(2)}) %collective-permute-start.2) | collective-permute-done | bytes 98336 | tf_op jit(solution)/shard_map/ppermute | solution.py:19
  20.3 1.0 collective-permute-done.5
  28.6 3.1 %collective-permute-start.7 = (f32[4,4,1,8,2,128]{5,3,4,2,1,0:T(8,128)S(1)}, f32[4,4,1,8,2,128]{5,3,4,2,1,0:T(8,128)S(1)}, u32[]{:S(2)}, u32[]{:S(2)}) collective-permute-start(f32[4,4,1,8,2,128]{5,3,4,2,1,0:T(8,128)S(1)} %get-tuple-element.574), channel_id=1, source_target_pairs={{4,0},{8,4},{12,8},{0,12},{5,1},{9,5},{13,9},{1,13},{6,2},{10,6},{... | collective-permute-start | bytes 393224 | tf_op jit(solution)/shard_map/ppermute | solution.py:20
  31.7 3.9 %collective-permute-done.7 = f32[4,4,1,8,2,128]{5,3,4,2,1,0:T(8,128)S(1)} collective-permute-done((f32[4,4,1,8,2,128]{5,3,4,2,1,0:T(8,128)S(1)}, f32[4,4,1,8,2,128]{5,3,4,2,1,0:T(8,128)S(1)}, u32[]{:S(2)}, u32[]{:S(2)}) %collective-permute-start.7) | collective-permute-done | bytes 131104 | tf_op jit(solution)/shard_map/ppermute | solution.py:20
  35.6 3.2 %collective-permute-done.6 = f32[4,4,1,8,2,128]{5,3,4,2,1,0:T(8,128)S(1)} collective-permute-done((f32[4,4,1,8,2,128]{5,3,4,2,1,0:T(8,128)S(1)}, f32[4,4,1,8,2,128]{5,3,4,2,1,0:T(8,128)S(1)}, u32[]{:S(2)}, u32[]{:S(2)}) %collective-permute-start.6) | collective-permute-done | bytes 131104 | tf_op jit(solution)/shard_map/ppermute | solution.py:19
  38.9 1.1 %collective-permute-start.9 = (f32[4,4,6,1,2,128]{5,3,4,2,1,0:T(1,128)S(1)}, f32[4,4,6,1,2,128]{5,3,4,2,1,0:T(1,128)S(1)}, u32[]{:S(2)}, u32[]{:S(2)}) collective-permute-start(f32[4,4,6,1,2,128]{5,3,4,2,1,0:T(1,128)S(1)} %get-tuple-element.532), channel_id=1, source_target_pairs={{2,0},{0,2},{3,1},{1,3},{6,4},{4,6},{7,5},{5,7},{10,8},{8,10},{11,... | collective-permute-start | bytes 294920 | tf_op jit(solution)/shard_map/ppermute | solution.py:20
  40.1 1.0 collective-permute-start.8
  41.0 2.8 %collective-permute-done.9 = f32[4,4,6,1,2,128]{5,3,4,2,1,0:T(1,128)S(1)} collective-permute-done((f32[4,4,6,1,2,128]{5,3,4,2,1,0:T(1,128)S(1)}, f32[4,4,6,1,2,128]{5,3,4,2,1,0:T(1,128)S(1)}, u32[]{:S(2)}, u32[]{:S(2)}) %collective-permute-start.9) | collective-permute-done | bytes 98336 | tf_op jit(solution)/shard_map/ppermute | solution.py:20
  43.8 1.1 %collective-permute-done.8 = f32[4,4,6,1,2,128]{5,3,4,2,1,0:T(1,128)S(1)} collective-permute-done((f32[4,4,6,1,2,128]{5,3,4,2,1,0:T(1,128)S(1)}, f32[4,4,6,1,2,128]{5,3,4,2,1,0:T(1,128)S(1)}, u32[]{:S(2)}, u32[]{:S(2)}) %collective-permute-start.8) | collective-permute-done | bytes 98336 | tf_op jit(solution)/shard_map/ppermute | solution.py:19
  46.7 1.0 collective-permute-done.11
  61.2 8.2 %pad.16 = f32[4,4,8,2,128]{4,2,3,1,0:T(8,128)} pad(f32[4,2,8,2,128]{4,2,3,1,0:T(8,128)} %copy-done.15, f32[]{:T(128)} %constant.20.clone.1), padding=0_0_0x1_0_1x0_0_0x0_0_0x0_0_0 | pad | bytes 196612 | tf_op jit(solution)/shard_map/pad | solution.py:122
  69.4 1.4 %maximum_maximum_fusion = f32[4,2,8,2,128]{4,2,3,1,0:T(8,128)} fusion(f32[1,1,8,2,128]{4,2,3,1,0:T(8,128)S(1)} %get-tuple-element.685, f32[1,1,8,2,128]{4,2,3,1,0:T(8,128)S(1)} %get-tuple-element.684, f32[1,1,8,2,128]{4,2,3,1,0:T(8,128)} %get-tuple-element.683, f32[1,1,8,2,128]{4,2,3,1,0:T(8,128)} %get-tuple-element.682, f32[4,1,8,2,128]{4,2,3,1,0:T(8,128)} %slice.2660), kind=kLoop, calls=%fused_computation.322 | loop fusion | flops 65536 | bytes 131072 | tf_op jit(solution)/shard_map/concatenate | solution.py:122
  70.8 8.3 %pad.15 = f32[4,4,8,2,128]{4,2,3,1,0:T(8,128)} pad(f32[4,2,8,2,128]{4,2,3,1,0:T(8,128)} %maximum_maximum_fusion, f32[]{:T(128)} %constant.20.clone.1), padding=0_0_0x0_1_1x0_0_0x0_0_0x0_0_0 | pad | bytes 196612 | tf_op jit(solution)/shard_map/pad | solution.py:122
  79.9 14.3 %all-gather = f32[16,1,8,2,128]{4,2,3,1,0:T(8,128)} all-gather(f32[4,1,8,2,128]{4,2,3,1,0:T(8,128)S(1)} %slice_add_fusion.11), channel_id=2, replica_groups=mesh['groups'=2,'tm'=4,'space'=2,'pair'=2] {'tm'}, dimensions={0}, use_global_device_ids=true | all-gather | bytes 163840 | tf_op jit(solution)/shard_map/all_gather | solution.py:27
  98.1 1.1 %collective-permute-start.12 = (f32[4,4,1,2,128]{4,2,3,1,0:T(1,128)S(1)}, f32[4,4,1,2,128]{4,2,3,1,0:T(1,128)S(1)}, u32[]{:S(2)}, u32[]{:S(2)}) collective-permute-start(f32[4,4,1,2,128]{4,2,3,1,0:T(1,128)S(1)} %slice.2807), channel_id=1, source_target_pairs={{0,2},{2,0},{1,3},{3,1},{4,6},{6,4},{5,7},{7,5},{8,10},{10,8},{9,1... | collective-permute-start | bytes 49160 | tf_op jit(solution)/shard_map/ppermute | solution.py:39
  100.1 1.7 %collective-permute-done.12 = f32[4,4,1,2,128]{4,2,3,1,0:T(1,128)S(1)} collective-permute-done((f32[4,4,1,2,128]{4,2,3,1,0:T(1,128)S(1)}, f32[4,4,1,2,128]{4,2,3,1,0:T(1,128)S(1)}, u32[]{:S(2)}, u32[]{:S(2)}) %collective-permute-start.12) | collective-permute-done | bytes 16416 | tf_op jit(solution)/shard_map/ppermute | solution.py:39
  102.2 0.9 copy.36
  (297 shorter events, 30.1 us)
Async XLA Ops:
  1.0 9.4 %collective-permute-start = (f32[4,4,1,8,2,128]{5,3,4,2,1,0:T(8,128)S(1)}, f32[4,4,1,8,2,128]{5,3,4,2,1,0:T(8,128)S(1)}, u32[]{:S(2)}, u32[]{:S(2)}) collective-permute-start(f32[4,4,1,8,2,128]{5,3,4,2,1,0:T(8,128)S(1)} %copy.80), channel_id=1, source_target_pairs={{0,4},{4,8},{8,12},{12,0},{1,5},{5,9},{9,13},{13,1},{2,6},{6,10},{... | collective-permute-start | bytes 393224 | tf_op jit(solution)/shard_map/ppermute | solution.py:19
  4.1 7.8 %collective-permute-start.1 = (f32[4,4,1,8,2,128]{5,3,4,2,1,0:T(8,128)S(1)}, f32[4,4,1,8,2,128]{5,3,4,2,1,0:T(8,128)S(1)}, u32[]{:S(2)}, u32[]{:S(2)}) collective-permute-start(f32[4,4,1,8,2,128]{5,3,4,2,1,0:T(8,128)S(1)} %copy.81), channel_id=1, source_target_pairs={{4,0},{8,4},{12,8},{0,12},{5,1},{9,5},{13,9},{1,13},{6,2},{10,6},{... | collective-permute-start | bytes 393224 | tf_op jit(solution)/shard_map/ppermute | solution.py:20
  12.1 5.4 %collective-permute-start.3 = (f32[4,4,6,1,2,128]{5,3,4,2,1,0:T(1,128)S(1)}, f32[4,4,6,1,2,128]{5,3,4,2,1,0:T(1,128)S(1)}, u32[]{:S(2)}, u32[]{:S(2)}) collective-permute-start(f32[4,4,6,1,2,128]{5,3,4,2,1,0:T(1,128)S(1)} %get-tuple-element.572), channel_id=1, source_target_pairs={{2,0},{0,2},{3,1},{1,3},{6,4},{4,6},{7,5},{5,7},{10,8},{8,10},{11,... | collective-permute-start | bytes 294920 | tf_op jit(solution)/shard_map/ppermute | solution.py:20
  13.6 4.9 %collective-permute-start.2 = (f32[4,4,6,1,2,128]{5,3,4,2,1,0:T(1,128)S(1)}, f32[4,4,6,1,2,128]{5,3,4,2,1,0:T(1,128)S(1)}, u32[]{:S(2)}, u32[]{:S(2)}) collective-permute-start(f32[4,4,6,1,2,128]{5,3,4,2,1,0:T(1,128)S(1)} %get-tuple-element.571), channel_id=1, source_target_pairs={{0,2},{2,0},{1,3},{3,1},{4,6},{6,4},{5,7},{7,5},{8,10},{10,8},{9,1... | collective-permute-start | bytes 294920 | tf_op jit(solution)/shard_map/ppermute | solution.py:19
  19.4 1.9 %collective-permute-start.5 = (f32[4,4,6,10,1,128]{5,1,4,3,2,0:T(4,128)S(1)}, f32[4,4,6,10,1,128]{5,1,4,3,2,0:T(4,128)S(1)}, u32[]{:S(2)}, u32[]{:S(2)}) collective-permute-start(f32[4,4,6,10,1,128]{5,1,4,3,2,0:T(4,128)S(1)} %copy.23), channel_id=1, source_target_pairs={{1,0},{0,1},{3,2},{2,3},{5,4},{4,5},{7,6},{6,7},{9,8},{8,9},{11,10... | collective-permute-start | bytes 1474568 | tf_op jit(solution)/shard_map/ppermute | solution.py:20
  19.8 2.2 %collective-permute-start.4 = (f32[4,4,6,10,1,128]{5,1,4,3,2,0:T(4,128)S(1)}, f32[4,4,6,10,1,128]{5,1,4,3,2,0:T(4,128)S(1)}, u32[]{:S(2)}, u32[]{:S(2)}) collective-permute-start(f32[4,4,6,10,1,128]{5,1,4,3,2,0:T(4,128)S(1)} %copy.22), channel_id=1, source_target_pairs={{0,1},{1,0},{2,3},{3,2},{4,5},{5,4},{6,7},{7,6},{8,9},{9,8},{10,11... | collective-permute-start | bytes 1474568 | tf_op jit(solution)/shard_map/ppermute | solution.py:19
  28.6 7.0 %collective-permute-start.7 = (f32[4,4,1,8,2,128]{5,3,4,2,1,0:T(8,128)S(1)}, f32[4,4,1,8,2,128]{5,3,4,2,1,0:T(8,128)S(1)}, u32[]{:S(2)}, u32[]{:S(2)}) collective-permute-start(f32[4,4,1,8,2,128]{5,3,4,2,1,0:T(8,128)S(1)} %get-tuple-element.574), channel_id=1, source_target_pairs={{4,0},{8,4},{12,8},{0,12},{5,1},{9,5},{13,9},{1,13},{6,2},{10,6},{... | collective-permute-start | bytes 393224 | tf_op jit(solution)/shard_map/ppermute | solution.py:20
  31.7 7.1 %collective-permute-start.6 = (f32[4,4,1,8,2,128]{5,3,4,2,1,0:T(8,128)S(1)}, f32[4,4,1,8,2,128]{5,3,4,2,1,0:T(8,128)S(1)}, u32[]{:S(2)}, u32[]{:S(2)}) collective-permute-start(f32[4,4,1,8,2,128]{5,3,4,2,1,0:T(8,128)S(1)} %get-tuple-element.573), channel_id=1, source_target_pairs={{0,4},{4,8},{8,12},{12,0},{1,5},{5,9},{9,13},{13,1},{2,6},{6,10},{... | collective-permute-start | bytes 393224 | tf_op jit(solution)/shard_map/ppermute | solution.py:19
  38.9 4.9 %collective-permute-start.9 = (f32[4,4,6,1,2,128]{5,3,4,2,1,0:T(1,128)S(1)}, f32[4,4,6,1,2,128]{5,3,4,2,1,0:T(1,128)S(1)}, u32[]{:S(2)}, u32[]{:S(2)}) collective-permute-start(f32[4,4,6,1,2,128]{5,3,4,2,1,0:T(1,128)S(1)} %get-tuple-element.532), channel_id=1, source_target_pairs={{2,0},{0,2},{3,1},{1,3},{6,4},{4,6},{7,5},{5,7},{10,8},{8,10},{11,... | collective-permute-start | bytes 294920 | tf_op jit(solution)/shard_map/ppermute | solution.py:20
  40.1 4.8 %collective-permute-start.8 = (f32[4,4,6,1,2,128]{5,3,4,2,1,0:T(1,128)S(1)}, f32[4,4,6,1,2,128]{5,3,4,2,1,0:T(1,128)S(1)}, u32[]{:S(2)}, u32[]{:S(2)}) collective-permute-start(f32[4,4,6,1,2,128]{5,3,4,2,1,0:T(1,128)S(1)} %get-tuple-element.531), channel_id=1, source_target_pairs={{0,2},{2,0},{1,3},{3,1},{4,6},{6,4},{5,7},{7,5},{8,10},{10,8},{9,1... | collective-permute-start | bytes 294920 | tf_op jit(solution)/shard_map/ppermute | solution.py:19
  45.7 1.9 %collective-permute-start.11 = (f32[4,4,6,10,1,128]{5,1,4,3,2,0:T(4,128)S(1)}, f32[4,4,6,10,1,128]{5,1,4,3,2,0:T(4,128)S(1)}, u32[]{:S(2)}, u32[]{:S(2)}) collective-permute-start(f32[4,4,6,10,1,128]{5,1,4,3,2,0:T(4,128)S(1)} %copy.27), channel_id=1, source_target_pairs={{1,0},{0,1},{3,2},{2,3},{5,4},{4,5},{7,6},{6,7},{9,8},{8,9},{11,10... | collective-permute-start | bytes 1474568 | tf_op jit(solution)/shard_map/ppermute | solution.py:20
  46.1 2.2 %collective-permute-start.10 = (f32[4,4,6,10,1,128]{5,1,4,3,2,0:T(4,128)S(1)}, f32[4,4,6,10,1,128]{5,1,4,3,2,0:T(4,128)S(1)}, u32[]{:S(2)}, u32[]{:S(2)}) collective-permute-start(f32[4,4,6,10,1,128]{5,1,4,3,2,0:T(4,128)S(1)} %copy.26), channel_id=1, source_target_pairs={{0,1},{1,0},{2,3},{3,2},{4,5},{5,4},{6,7},{7,6},{8,9},{9,8},{10,11... | collective-permute-start | bytes 1474568 | tf_op jit(solution)/shard_map/ppermute | solution.py:19
  51.6 5.0 %copy-start.1 = (f32[4,4,8,2,1]{4,2,3,1,0:T(8,128)}, f32[4,4,8,2,1]{4,2,3,1,0:T(8,128)S(1)}, u32[]{:S(2)}) copy-start(f32[4,4,8,2,1]{4,2,3,1,0:T(8,128)S(1)} %get-tuple-element.521) | copy-start | bytes 3076
  52.4 4.2 %copy-start.3 = (f32[4,4,8,2,127]{4,2,3,1,0:T(8,128)}, f32[4,4,8,2,127]{4,2,3,1,0:T(8,128)S(1)}, u32[]{:S(2)}) copy-start(f32[4,4,8,2,127]{4,2,3,1,0:T(8,128)S(1)} %get-tuple-element.518) | copy-start | bytes 390148
  55.3 2.3 %copy-start.5 = (f32[3,4,8,2,128]{4,2,3,1,0:T(8,128)}, f32[3,4,8,2,128]{4,2,3,1,0:T(8,128)S(1)}, u32[]{:S(2)}) copy-start(f32[3,4,8,2,128]{4,2,3,1,0:T(8,128)S(1)} %get-tuple-element.500) | copy-start | bytes 294916
  57.5 36.6 %copy-start = (f32[4,8,2,128]{3,2,1,0:T(2,128)S(1)}, f32[4,8,2,128]{3,2,1,0:T(2,128)}, u32[]{:S(2)}) copy-start(f32[4,8,2,128]{3,2,1,0:T(2,128)} %constant.16.clone.1) | copy-start | bytes 98308
  97.1 2.1 %copy-start.11 = (f32[3,4,8,2,128]{4,2,3,1,0:T(8,128)S(1)}, f32[3,4,8,2,128]{4,2,3,1,0:T(8,128)}, u32[]{:S(2)}) copy-start(f32[3,4,8,2,128]{4,2,3,1,0:T(8,128)} %get-tuple-element.496) | copy-start | bytes 294916
  97.1 4.9 %collective-permute-start.13 = (f32[4,4,8,1,128]{4,2,3,1,0:T(8,128)S(1)}, f32[4,4,8,1,128]{4,2,3,1,0:T(8,128)S(1)}, u32[]{:S(2)}, u32[]{:S(2)}) collective-permute-start(f32[4,4,8,1,128]{4,2,3,1,0:T(8,128)S(1)} %get-tuple-element.690), channel_id=1, source_target_pairs={{0,1},{1,0},{2,3},{3,2},{4,5},{5,4},{6,7},{7,6},{8,9},{9,8},{10,11... | collective-permute-start | bytes 196616 | tf_op jit(solution)/shard_map/ppermute | solution.py:39
  97.6 2.0 %copy-start.26 = (f32[1,4,8,2,128]{4,2,3,1,0:T(8,128)S(1)}, f32[1,4,8,2,128]{4,2,3,1,0:T(8,128)}, u32[]{:S(2)}) copy-start(f32[1,4,8,2,128]{4,2,3,1,0:T(8,128)} %get-tuple-element.58) | copy-start | bytes 98308
  97.6 2.0 %copy-start.27 = (f32[1,4,8,2,128]{4,2,3,1,0:T(8,128)S(1)}, f32[1,4,8,2,128]{4,2,3,1,0:T(8,128)}, u32[]{:S(2)}) copy-start(f32[1,4,8,2,128]{4,2,3,1,0:T(8,128)} %get-tuple-element.59) | copy-start | bytes 98308
  97.6 2.0 %copy-start.28 = (f32[1,4,8,2,128]{4,2,3,1,0:T(8,128)S(1)}, f32[1,4,8,2,128]{4,2,3,1,0:T(8,128)}, u32[]{:S(2)}) copy-start(f32[1,4,8,2,128]{4,2,3,1,0:T(8,128)} %get-tuple-element.60) | copy-start | bytes 98308
  97.6 2.0 %copy-start.29 = (f32[1,4,8,2,128]{4,2,3,1,0:T(8,128)S(1)}, f32[1,4,8,2,128]{4,2,3,1,0:T(8,128)}, u32[]{:S(2)}) copy-start(f32[1,4,8,2,128]{4,2,3,1,0:T(8,128)} %get-tuple-element.61) | copy-start | bytes 98308
  97.6 2.0 %copy-start.30 = (f32[1,4,8,2,128]{4,2,3,1,0:T(8,128)S(1)}, f32[1,4,8,2,128]{4,2,3,1,0:T(8,128)}, u32[]{:S(2)}) copy-start(f32[1,4,8,2,128]{4,2,3,1,0:T(8,128)} %get-tuple-element.62) | copy-start | bytes 98308
  98.1 3.8 %collective-permute-start.12 = (f32[4,4,1,2,128]{4,2,3,1,0:T(1,128)S(1)}, f32[4,4,1,2,128]{4,2,3,1,0:T(1,128)S(1)}, u32[]{:S(2)}, u32[]{:S(2)}) collective-permute-start(f32[4,4,1,2,128]{4,2,3,1,0:T(1,128)S(1)} %slice.2807), channel_id=1, source_target_pairs={{0,2},{2,0},{1,3},{3,1},{4,6},{6,4},{5,7},{7,5},{8,10},{10,8},{9,1... | collective-permute-start | bytes 49160 | tf_op jit(solution)/shard_map/ppermute | solution.py:39
  (24 other events, 28.7 us)
where the time goes:
time: 104 us; the launch traced here: 103 us
  local copies, waits for them, and re-layouts  30.3 us (29%)
  waiting for transfers between devices  24.8 us (24%)
  other arithmetic  17.3 us (17%)
  starting transfers between devices  14.9 us (14%)
  blocking collectives  14.3 us (14%)
  between operations  1.58 us (2%)
    pad x2, local copies, waits for them, and re-layouts, on_device(): local_prefix = lax.associative_scan(quat_mul, temporal, axis=1)  16.5 us
    all_gather x1, blocking collectives, carried_in(): gathered = lax.all_gather(part, axis)  14.3 us
    ppermute x6, waiting for transfers between devices, with_halo(): after = lax.ppermute(first, axis, down)  12.3 us
    ppermute x6, waiting for transfers between devices, with_halo(): before = lax.ppermute(last, axis, up)  10.8 us
    ppermute x6, starting transfers between devices, with_halo(): after = lax.ppermute(first, axis, down)  8.01 us
    sub x55, other arithmetic, quat_mul(): former[0] * latter[0] - former[1] * latter[1] - former[2] * latter[2]  6.27 us
    ppermute x6, starting transfers between devices, with_halo(): before = lax.ppermute(last, axis, up)  5.7 us
    slice x12, local copies, waits for them, and re-layouts, shifted(): cropped = jnp.roll(cropped, -offset[3], axis=-1)  5.42 us
  transfers between devices with their start and end apart: 14, of which 13 were waited for; matrix products, arithmetic and copies ran while one was open for 3% of the time, Pallas kernels for 0%

commit v1 on v0

v1 whole, which is shorter than its diff:
```python
import jax
import jax.numpy as jnp
from jax import lax
from jax.experimental import pallas as pl
from jax.experimental.pallas import tpu as pltpu
from jax.sharding import PartitionSpec as P

SWEEPS = 2
smear_weight = 0.1
VMEM = pl.BlockSpec(memory_space=pltpu.VMEM)
F32 = jnp.float32
BASE = 8


def mul(a, b):
    return (
        a[0] * b[0] - a[1] * b[1] - a[2] * b[2] - a[3] * b[3],
        a[0] * b[1] + a[1] * b[0] + a[2] * b[3] - a[3] * b[2],
        a[0] * b[2] - a[1] * b[3] + a[2] * b[0] + a[3] * b[1],
        a[0] * b[3] + a[1] * b[2] - a[2] * b[1] + a[3] * b[0],
    )


def mul_cr(a, b):
    return (
        a[0] * b[0] + a[1] * b[1] + a[2] * b[2] + a[3] * b[3],
        a[1] * b[0] - a[0] * b[1] - a[2] * b[3] + a[3] * b[2],
        a[2] * b[0] - a[0] * b[2] + a[1] * b[3] - a[3] * b[1],
        a[3] * b[0] - a[0] * b[3] - a[1] * b[2] + a[2] * b[1],
    )


def mul_cl(a, b):
    return (
        a[0] * b[0] + a[1] * b[1] + a[2] * b[2] + a[3] * b[3],
        a[0] * b[1] - a[1] * b[0] - a[2] * b[3] + a[3] * b[2],
        a[0] * b[2] + a[1] * b[3] - a[2] * b[0] - a[3] * b[1],
        a[0] * b[3] - a[1] * b[2] + a[2] * b[1] - a[3] * b[0],
    )


def add(a, b):
    return tuple(x + y for x, y in zip(a, b))


def zroll(a, amount):
    return tuple(pltpu.roll(x, amount % 128, 1) for x in a)


def fill_scratch(own, par, t_below, t_above, xh, corner, t_shared, x_shared, eo, ep):
    tl = own.shape[2]
    for d in range(4):
        eo[d, :, 1 : tl + 1, BASE : BASE + 16, :] = own[d]
        ep[d, :, 1 : tl + 1, BASE : BASE + 16, :] = par[d]
    eo[:, :, 0, BASE : BASE + 16, :] = t_below[...]
    eo[1:4, :, tl + 1, BASE : BASE + 16, :] = t_above[...]
    for slot, d in enumerate((0, 2, 3)):
        eo[d, :, 1 : tl + 1, BASE + 16 : BASE + 18, :] = xh[slot]
    for d in range(4):
        eo[d, :, 1 : tl + 1, BASE - 2 : BASE, :] = xh[3 + d]
    ep[0, :, 0, BASE : BASE + 16, :] = t_shared[0]
    ep[2, :, tl + 1, BASE : BASE + 16, :] = t_shared[1]
    ep[2, :, 1 : tl + 1, BASE + 16 : BASE + 18, :] = x_shared[0]
    ep[1, :, 1 : tl + 1, BASE - 2 : BASE, :] = x_shared[1]
    eo[0, :, 0, BASE + 16 : BASE + 18, :] = corner[0]
    eo[1, :, tl + 1, BASE - 2 : BASE, :] = corner[1]


def smear_site(eo, ep, t, y):
    def ld(d, dt=0, dx=0, dy=0):
        yy = y + dy
        ref = eo if 0 <= yy < 2 else ep
        start = BASE + 2 * dx + yy % 2
        return tuple(ref[d, c, t + 1 + dt, pl.ds(start, 8, stride=2), :] for c in range(4))

    def step(m):
        return {0: dict(dt=1), 1: dict(dx=1), 2: dict(dy=1)}[m]

    def back(n):
        return {0: dict(dt=-1), 1: dict(dx=-1), 2: dict(dy=-1)}[n]

    total = [None] * 4

    def acc(m, q):
        total[m] = q if total[m] is None else add(total[m], q)

    here = [ld(d) for d in range(4)]
    for m in range(3):
        for n in range(m + 1, 3):
            um, un = here[m], here[n]
            um_n = ld(m, **step(n))
            un_m = ld(n, **step(m))
            acc(m, mul_cr(mul(un, um_n), un_m))
            acc(n, mul_cr(mul(um, un_m), um_n))
            acc(m, mul(mul_cl(ld(n, **back(n)), ld(m, **back(n))), ld(n, **back(n), **step(m))))
            acc(n, mul(mul_cl(ld(m, **back(m)), ld(n, **back(m))), ld(m, **back(m), **step(n))))
    uz = here[3]
    for m in range(3):
        um = here[m]
        um_z = zroll(um, -1)
        uz_m = ld(3, **step(m))
        a = mul(um, uz_m)
        acc(m, mul_cr(mul(uz, um_z), uz_m))
        acc(3, mul_cr(a, um_z))
        acc(m, zroll(mul_cl(uz, a), 1))
        low = ld(m, **back(m))
        acc(3, mul(mul_cl(low, ld(3, **back(m))), zroll(low, -1)))
    out = []
    for m in range(4):
        comb = tuple(h + smear_weight * s for h, s in zip(here[m], total[m]))
        norm = comb[0] * comb[0] + comb[1] * comb[1] + comb[2] * comb[2] + comb[3] * comb[3]
        inv = lax.rsqrt(norm)
        out.append(tuple(x * inv for x in comb))
    return out


def boundary(out, t_up, t_dn, xs):
    tl = out.shape[2]
    t_up[...] = out[:, :, tl - 1]
    t_dn[...] = out[1:4, :, 0]
    for slot, d in enumerate((0, 2, 3)):
        xs[slot] = out[d, :, :, 0:2, :]
    for d in range(4):
        xs[3 + d] = out[d, :, :, 14:16, :]


def sweep_kernel(own, par, t_below, t_above, xh, corner, t_shared, x_shared, out, t_up, t_dn, xs, eo, ep):
    tl = own.shape[2]
    fill_scratch(own, par, t_below, t_above, xh, corner, t_shared, x_shared, eo, ep)

    def body(t, carry):
        for y in range(2):
            new = smear_site(eo, ep, t, y)
            for d in range(4):
                for c in range(4):
                    out[d, c, t, pl.ds(y, 8, stride=2), :] = new[d][c]
        return carry

    lax.fori_loop(0, tl, body, 0)
    boundary(out, t_up, t_dn, xs)


def last_kernel(own, par, t_below, t_above, xh, corner, t_shared, x_shared, out, prefix, slab, eo, ep):
    tl = own.shape[2]
    fill_scratch(own, par, t_below, t_above, xh, corner, t_shared, x_shared, eo, ep)

    def body(t, carry):
        new_carry = []
        for y in range(2):
            rows = pl.ds(y, 8, stride=2)
            new = smear_site(eo, ep, t, y)
            for d in range(1, 4):
                for c in range(4):
                    out[d - 1, c, t, rows, :] = new[d][c]
            for c in range(4):
                prefix[c, t, rows, :] = carry[y][c]
            new_carry.append(mul(carry[y], new[0]))
        return tuple(new_carry)

    one = jnp.ones((8, 128), F32)
    zero = jnp.zeros((8, 128), F32)
    ident = (one, zero, zero, zero)
    final = lax.fori_loop(0, tl, body, (ident, ident))
    for y in range(2):
        for c in range(4):
            slab[c, pl.ds(y, 8, stride=2), :] = final[y][c]


def carry_kernel(n, prefix, slab_list, gauge, gx, gy):
    tl = prefix.shape[1]
    place = lax.axis_index("tm")
    for half in range(2):
        rows = pl.ds(half * 8, 8)
        state = None
        for j in reversed(range(n - 1)):
            q = tuple(slab_list[j][c, rows, :] for c in range(4))
            there = place >= j + 1
            q = tuple(jnp.where(there, v, 1.0 if c == 0 else 0.0) for c, v in enumerate(q))
            state = q if state is None else mul(state, q)
        for t in range(tl):
            g = mul(state, tuple(prefix[c, t, rows, :] for c in range(4)))
            for c in range(4):
                gauge[c, t, rows, :] = g[c]
    gx[...] = gauge[:, :, 0:2, :]
    for c in range(4):
        for t in range(tl):
            gy[c, t] = gauge[c, t, pl.ds(0, 8, stride=2), :]


def rotate_kernel(gauge, nx, ny, links, out, ext):
    tl = gauge.shape[1]
    ext[:, :, 0:16, :] = gauge[...]
    ext[:, :, 16:18, :] = nx[...]
    for t in range(tl):
        for y in range(2):
            rows = pl.ds(y, 8, stride=2)
            g = tuple(gauge[c, t, rows, :] for c in range(4))
            g1 = tuple(ext[c, t, pl.ds(2 + y, 8, stride=2), :] for c in range(4))
            if y == 0:
                g2 = tuple(gauge[c, t, pl.ds(1, 8, stride=2), :] for c in range(4))
            else:
                g2 = tuple(ny[c, t] for c in range(4))
            g3 = zroll(g, -1)
            for d, other in enumerate((g1, g2, g3)):
                u = tuple(links[d, c, t, rows, :] for c in range(4))
                r = mul_cr(mul(g, u), other)
                for c in range(4):
                    out[d, c, t, rows, :] = r[c]


def call(kernel, outs, scratch, *args):
    single = isinstance(outs[0], int)
    shapes = [jax.ShapeDtypeStruct(s, F32) for s in ([outs] if single else outs)]
    return pl.pallas_call(
        kernel,
        out_shape=shapes[0] if single else shapes,
        in_specs=[VMEM] * len(args),
        out_specs=VMEM if single else [VMEM] * len(shapes),
        scratch_shapes=[pltpu.VMEM(s, F32) for s in scratch],
        compiler_params=pltpu.CompilerParams(vmem_limit_bytes=40 * 2**20),
    )(*args)


def rotated_by(x, axis, steps):
    n = lax.axis_size(axis)
    return lax.ppermute(x, axis, [(i, (i + steps) % n) for i in range(n)])


def x_exchange(xs, cut):
    if lax.axis_size("space") == 2:
        return rotated_by(xs, "space", 1)
    return jnp.concatenate(
        [rotated_by(xs[:cut], "space", -1), rotated_by(xs[cut:], "space", 1)]
    )


def halo(own, t_up, t_dn, xs):
    t_below = rotated_by(t_up, "tm", 1)
    t_above = rotated_by(t_dn, "tm", -1)
    xh = x_exchange(xs, 3)
    par = rotated_by(own, "pair", 1)
    x_shared = rotated_by(jnp.stack([xh[1], xh[4]]), "pair", 1)
    corner = x_exchange(jnp.stack([t_below[0, :, :2], t_above[0, :, -2:]]), 1)
    t_shared = rotated_by(jnp.stack([t_below[0], t_above[1]]), "pair", 1)
    return par, t_below, t_above, xh, corner, t_shared, x_shared


def on_device(link_field):
    tl, xl, yl, z = link_field.shape[2:]
    rows = xl * yl
    links = link_field.reshape(4, 4, tl, rows, z)
    scratch = [(4, 4, tl + 2, 32, z)] * 2
    edges = [(4, 4, rows, z), (3, 4, rows, z), (7, 4, tl, 2, z)]
    t_up, t_dn, xs = call(boundary, edges, [], links)
    for _ in range(SWEEPS - 1):
        got = halo(links, t_up, t_dn, xs)
        links, t_up, t_dn, xs = call(
            sweep_kernel,
            [(4, 4, tl, rows, z)] + edges,
            scratch,
            links,
            *got,
        )
    got = halo(links, t_up, t_dn, xs)
    smeared, prefix, slab = call(
        last_kernel, [(3, 4, tl, rows, z), (4, tl, rows, z), (4, rows, z)], scratch, links, *got
    )
    n = lax.axis_size("tm")
    slabs = [rotated_by(slab, "tm", k) for k in range(1, n)]
    gauge, gx, gy = call(
        lambda p, *rest: carry_kernel(n, p, rest[: n - 1], *rest[n - 1 :]),
        [(4, tl, rows, z), (4, tl, 2, z), (4, tl, xl, z)],
        [],
        prefix,
        *slabs,
    )
    nx = rotated_by(gx, "space", -1)
    ny = rotated_by(gy, "pair", -1)
    out = call(
        rotate_kernel, (3, 4, tl, rows, z), [(4, tl, 24, z)], gauge, nx, ny, smeared
    )
    return out.reshape(3, 4, tl, xl, yl, z)


def solution(mesh):
    spec = P(None, None, "tm", "space", "pair", "groups")
    return jax.shard_map(on_device, mesh=mesh, in_specs=(spec,), out_specs=spec, check_vma=False)
```

time: 104 us -> 47.3 us (0.45)
  local copies, waits for them, and re-layouts: 30.3 us -> 1.08 us
  other arithmetic: 17.3 us -> 0.07 us
  blocking collectives: 14.3 us -> 0 us
  Pallas kernels: 0 us -> 5.03 us
  between operations: 1.58 us -> 0.17 us
    pad x2 -> x0, local copies, waits for them, and re-layouts: 16.5 us -> none  [on_device(): local_prefix = lax.associative_scan(quat_mul, temporal, axis=1)]
    all_gather x1 -> x0, blocking collectives: 14.3 us -> none  [carried_in(): gathered = lax.all_gather(part, axis)]
    slice x26 -> x10, local copies, waits for them, and re-layouts: 8.97 us -> 0.04 us  [the longest x4 0.01 us: halo(): corner = x_exchange(jnp.stack([t_below[0, :, :2], t_above[0, :, -2:]]), 1)]
    sub x108 -> x0, other arithmetic: 8.14 us -> none  [the longest x55 6.27 us: quat_mul(): former[0] * latter[0] - former[1] * latter[1] - former[2] * latter[2]]
    pallas_call x0 -> x5, Pallas kernels: none -> 5.03 us  [call(): pl.pallas_call(kernel, out_shape=shapes[0] if single else shapes, in_spec...]
    concatenate x18 -> x0, other arithmetic: 4.21 us -> none  [the longest x4 1.63 us: with_halo(): x = jnp.concatenate([before, x, after], axis=dim)]
    neg x17 -> x0, other arithmetic: 3.09 us -> none  [quat_conj(): return jnp.concatenate([quat_field[:1], -quat_field[1:]], axis=0)]
    unnamed x72 -> x2, local copies, waits for them, and re-layouts: 2.56 us -> 1.04 us
  transfers between devices with their start and end apart: 14 -> 19, of which waited for: 13 -> 10; matrix products, arithmetic and copies ran while one was open for 3% -> 0% of each run, Pallas kernels for 0% -> 0%
where the time goes in v1:
time: 47.3 us; the launch traced here: 47.2 us
  waiting for transfers between devices  25 us (53%)
  starting transfers between devices  15.9 us (34%)
  Pallas kernels  5.03 us (11%)
  local copies, waits for them, and re-layouts  1.08 us (2%)
    ppermute x19, waiting for transfers between devices, rotated_by(): return lax.ppermute(x, axis, [(i, (i + steps) % n) for i in range(n)])  25 us
    ppermute x19, starting transfers between devices, rotated_by(): return lax.ppermute(x, axis, [(i, (i + steps) % n) for i in range(n)])  15.9 us
    pallas_call x5, Pallas kernels, call(): pl.pallas_call(kernel, out_shape=shapes[0] if single else shapes, in_spec...  5.03 us
    unnamed x2, local copies, waits for them, and re-layouts  1.04 us
  transfers between devices with their start and end apart: 19, of which 10 were waited for; matrix products, arithmetic and copies ran while one was open for 0% of the time, Pallas kernels for 0%

profile of v1, /device:TPU:0, one launch (start us, length us, event | category | flops | bytes accessed | tf_op | source)
XLA Modules:
  0.0 47.2 jit_solution(9976946902795811213)
XLA Ops:
  0.0 1.0 %copy-done = f32[4,4,4,8,2,128]{5,4,3,2,1,0:T(2,128)S(1)} copy-done((f32[4,4,4,8,2,128]{5,4,3,2,1,0:T(2,128)S(1)}, f32[4,4,4,8,2,128]{5,4,3,2,1,0:T(2,128)}, u32[]{:S(2)}) %copy-start) | copy-done | bytes 524312
  1.1 3.0 %collective-permute-start.3 = (f32[7,4,4,2,128]{4,3,2,1,0:T(2,128)S(1)}, f32[7,4,4,2,128]{4,3,2,1,0:T(2,128)S(1)}, u32[]{:S(2)}, u32[]{:S(2)}) collective-permute-start(f32[7,4,4,2,128]{4,3,2,1,0:T(2,128)S(1)} %get-tuple-element.20), channel_id=1, source_target_pairs={{0,2},{2,0},{1,3},{3,1},{4,6},{6,4},{5,7},{7,5},{8,10},{10,8},{9,1... | collective-permute-start | bytes 344072 | tf_op jit(solution)/shard_map/ppermute | solution.py:226
  4.1 3.6 %collective-permute-start.2 = (f32[3,4,16,128]{3,2,1,0:T(8,128)S(1)}, f32[3,4,16,128]{3,2,1,0:T(8,128)S(1)}, u32[]{:S(2)}, u32[]{:S(2)}) collective-permute-start(f32[3,4,16,128]{3,2,1,0:T(8,128)S(1)} %get-tuple-element.19), channel_id=1, source_target_pairs={{0,12},{4,0},{8,4},{12,8},{1,13},{5,1},{9,5},{13,9},{2,14},{6,2},{... | collective-permute-start | bytes 294920 | tf_op jit(solution)/shard_map/ppermute | solution.py:226
  7.7 3.2 %collective-permute-done.2.t_above = f32[3,4,16,128]{3,2,1,0:T(8,128)S(1)} collective-permute-done((f32[3,4,16,128]{3,2,1,0:T(8,128)S(1)}, f32[3,4,16,128]{3,2,1,0:T(8,128)S(1)}, u32[]{:S(2)}, u32[]{:S(2)}) %collective-permute-start.2) | collective-permute-done | bytes 98336 | tf_op jit(solution)/shard_map/ppermute | solution.py:226
  11.0 4.4 %collective-permute-done.1.t_below = f32[4,4,16,128]{3,2,1,0:T(8,128)S(1)} collective-permute-done((f32[4,4,16,128]{3,2,1,0:T(8,128)S(1)}, f32[4,4,16,128]{3,2,1,0:T(8,128)S(1)}, u32[]{:S(2)}, u32[]{:S(2)}) %collective-permute-start.1) | collective-permute-done | bytes 131104 | tf_op jit(solution)/shard_map/ppermute | solution.py:226
  15.5 0.6 %collective-permute-start.4 = (f32[2,4,2,128]{3,2,1,0:T(2,128)S(1)}, f32[2,4,2,128]{3,2,1,0:T(2,128)S(1)}, u32[]{:S(2)}, u32[]{:S(2)}) collective-permute-start(f32[2,4,2,128]{3,2,1,0:T(2,128)S(1)} %pad_maximum_fusion.4), channel_id=1, source_target_pairs={{0,2},{2,0},{1,3},{3,1},{4,6},{6,4},{5,7},{7,5},{8,10},{10,8},{9,1... | collective-permute-start | bytes 24584 | tf_op jit(solution)/shard_map/ppermute | solution.py:226
  16.1 3.1 %collective-permute-done.4.corner = f32[2,4,2,128]{3,2,1,0:T(2,128)S(1)} collective-permute-done((f32[2,4,2,128]{3,2,1,0:T(2,128)S(1)}, f32[2,4,2,128]{3,2,1,0:T(2,128)S(1)}, u32[]{:S(2)}, u32[]{:S(2)}) %collective-permute-start.4) | collective-permute-done | bytes 8224 | tf_op jit(solution)/shard_map/ppermute | solution.py:226
  19.3 2.0 %shard_map.18 = (f32[4,4,4,16,128]{4,3,2,1,0:T(8,128)S(1)}, f32[4,4,16,128]{3,2,1,0:T(8,128)S(1)}, f32[3,4,16,128]{3,2,1,0:T(8,128)S(1)}, f32[7,4,4,2,128]{4,3,2,1,0:T(2,128)S(1)}) custom-call(f32[4,4,4,16,128]{4,3,2,1,0:T(8,128)S(1)} %bitcast.4, f32[4,4,4,16,128]{4,3,2,1,0:T(8,128)S(1)} %collective-permute-done.par, ...), custom_call_target="tpu_custom_call" | custom-call | tf_op jit(solution)/shard_map/pallas_call | solution.py:214
  21.3 0.6 %collective-permute-start.10 = (f32[7,4,4,2,128]{4,3,2,1,0:T(2,128)S(1)}, f32[7,4,4,2,128]{4,3,2,1,0:T(2,128)S(1)}, u32[]{:S(2)}, u32[]{:S(2)}) collective-permute-start(f32[7,4,4,2,128]{4,3,2,1,0:T(2,128)S(1)} %get-tuple-element.24), channel_id=1, source_target_pairs={{0,2},{2,0},{1,3},{3,1},{4,6},{6,4},{5,7},{7,5},{8,10},{10,8},{9,1... | collective-permute-start | bytes 344072 | tf_op jit(solution)/shard_map/ppermute | solution.py:226
  21.9 0.8 %collective-permute-start.9 = (f32[3,4,16,128]{3,2,1,0:T(8,128)S(1)}, f32[3,4,16,128]{3,2,1,0:T(8,128)S(1)}, u32[]{:S(2)}, u32[]{:S(2)}) collective-permute-start(f32[3,4,16,128]{3,2,1,0:T(8,128)S(1)} %get-tuple-element.23), channel_id=1, source_target_pairs={{0,12},{4,0},{8,4},{12,8},{1,13},{5,1},{9,5},{13,9},{2,14},{6,2},{... | collective-permute-start | bytes 294920 | tf_op jit(solution)/shard_map/ppermute | solution.py:226
  22.6 1.3 %collective-permute-start.8 = (f32[4,4,16,128]{3,2,1,0:T(8,128)S(1)}, f32[4,4,16,128]{3,2,1,0:T(8,128)S(1)}, u32[]{:S(2)}, u32[]{:S(2)}) collective-permute-start(f32[4,4,16,128]{3,2,1,0:T(8,128)S(1)} %get-tuple-element.22), channel_id=1, source_target_pairs={{0,4},{4,8},{8,12},{12,0},{1,5},{5,9},{9,13},{13,1},{2,6},{6,10},{... | collective-permute-start | bytes 393224 | tf_op jit(solution)/shard_map/ppermute | solution.py:226
  23.9 4.0 %collective-permute-done.9.t_above = f32[3,4,16,128]{3,2,1,0:T(8,128)S(1)} collective-permute-done((f32[3,4,16,128]{3,2,1,0:T(8,128)S(1)}, f32[3,4,16,128]{3,2,1,0:T(8,128)S(1)}, u32[]{:S(2)}, u32[]{:S(2)}) %collective-permute-start.9) | collective-permute-done | bytes 98336 | tf_op jit(solution)/shard_map/ppermute | solution.py:226
  28.0 1.4 %collective-permute-done.8.t_below = f32[4,4,16,128]{3,2,1,0:T(8,128)S(1)} collective-permute-done((f32[4,4,16,128]{3,2,1,0:T(8,128)S(1)}, f32[4,4,16,128]{3,2,1,0:T(8,128)S(1)}, u32[]{:S(2)}, u32[]{:S(2)}) %collective-permute-start.8) | collective-permute-done | bytes 131104 | tf_op jit(solution)/shard_map/ppermute | solution.py:226
  29.5 1.6 %collective-permute-start.11 = (f32[2,4,2,128]{3,2,1,0:T(2,128)S(1)}, f32[2,4,2,128]{3,2,1,0:T(2,128)S(1)}, u32[]{:S(2)}, u32[]{:S(2)}) collective-permute-start(f32[2,4,2,128]{3,2,1,0:T(2,128)S(1)} %pad_maximum_fusion.5), channel_id=1, source_target_pairs={{0,2},{2,0},{1,3},{3,1},{4,6},{6,4},{5,7},{7,5},{8,10},{10,8},{9,1... | collective-permute-start | bytes 24584 | tf_op jit(solution)/shard_map/ppermute | solution.py:226
  31.1 2.2 %collective-permute-done.11.corner = f32[2,4,2,128]{3,2,1,0:T(2,128)S(1)} collective-permute-done((f32[2,4,2,128]{3,2,1,0:T(2,128)S(1)}, f32[2,4,2,128]{3,2,1,0:T(2,128)S(1)}, u32[]{:S(2)}, u32[]{:S(2)}) %collective-permute-start.11) | collective-permute-done | bytes 8224 | tf_op jit(solution)/shard_map/ppermute | solution.py:226
  33.2 2.0 %shard_map.19 = (f32[3,4,4,16,128]{4,3,2,1,0:T(8,128)S(1)}, f32[4,4,16,128]{3,2,1,0:T(8,128)S(1)}, f32[4,16,128]{2,1,0:T(8,128)S(1)}) custom-call(f32[4,4,4,16,128]{4,3,2,1,0:T(8,128)S(1)} %get-tuple-element.21.own, f32[4,4,4,16,128]{4,3,2,1,0:T(8,128)S(1)} %collective-permute-done.7.par, f32[4,4,16,128]{3,2,1,0:T(8,128)S(1)} %collective-permute-done.8.t_below, ...), custom_call_target="tpu_custom_call" | custom-call | tf_op jit(solution)/shard_map/pallas_call | solution.py:214
  35.2 1.0 %collective-permute-start.16 = (f32[4,16,128]{2,1,0:T(8,128)S(1)}, f32[4,16,128]{2,1,0:T(8,128)S(1)}, u32[]{:S(2)}, u32[]{:S(2)}) collective-permute-start(f32[4,16,128]{2,1,0:T(8,128)S(1)} %get-tuple-element.26), channel_id=1, source_target_pairs={{0,12},{4,0},{8,4},{12,8},{1,13},{5,1},{9,5},{13,9},{2,14},{6,2},{... | collective-permute-start | bytes 98312 | tf_op jit(solution)/shard_map/ppermute | solution.py:226
  36.6 1.2 %collective-permute-start.14 = (f32[4,16,128]{2,1,0:T(8,128)S(1)}, f32[4,16,128]{2,1,0:T(8,128)S(1)}, u32[]{:S(2)}, u32[]{:S(2)}) collective-permute-start(f32[4,16,128]{2,1,0:T(8,128)S(1)} %get-tuple-element.26), channel_id=1, source_target_pairs={{0,4},{4,8},{8,12},{12,0},{1,5},{5,9},{9,13},{13,1},{2,6},{6,10},{... | collective-permute-start | bytes 98312 | tf_op jit(solution)/shard_map/ppermute | solution.py:226
  37.8 1.4 %collective-permute-done.16.rest_2_ = f32[4,16,128]{2,1,0:T(8,128)S(1)} collective-permute-done((f32[4,16,128]{2,1,0:T(8,128)S(1)}, f32[4,16,128]{2,1,0:T(8,128)S(1)}, u32[]{:S(2)}, u32[]{:S(2)}) %collective-permute-start.16) | collective-permute-done | bytes 32800 | tf_op jit(solution)/shard_map/ppermute | solution.py:226
  39.2 1.9 %collective-permute-done.15.rest_1_ = f32[4,16,128]{2,1,0:T(8,128)S(1)} collective-permute-done((f32[4,16,128]{2,1,0:T(8,128)S(1)}, f32[4,16,128]{2,1,0:T(8,128)S(1)}, u32[]{:S(2)}, u32[]{:S(2)}) %collective-permute-start.15) | collective-permute-done | bytes 32800 | tf_op jit(solution)/shard_map/ppermute | solution.py:226
  41.0 1.3 %collective-permute-done.14.rest_0_ = f32[4,16,128]{2,1,0:T(8,128)S(1)} collective-permute-done((f32[4,16,128]{2,1,0:T(8,128)S(1)}, f32[4,16,128]{2,1,0:T(8,128)S(1)}, u32[]{:S(2)}, u32[]{:S(2)}) %collective-permute-start.14) | collective-permute-done | bytes 32800 | tf_op jit(solution)/shard_map/ppermute | solution.py:226
  42.4 1.6 %collective-permute-start.17 = (f32[4,4,2,128]{3,2,1,0:T(2,128)S(1)}, f32[4,4,2,128]{3,2,1,0:T(2,128)S(1)}, u32[]{:S(2)}, u32[]{:S(2)}) collective-permute-start(f32[4,4,2,128]{3,2,1,0:T(2,128)S(1)} %get-tuple-element.28), channel_id=1, source_target_pairs={{0,2},{2,0},{1,3},{3,1},{4,6},{6,4},{5,7},{7,5},{8,10},{10,8},{9,1... | collective-permute-start | bytes 49160 | tf_op jit(solution)/shard_map/ppermute | solution.py:226
  44.0 2.2 %collective-permute-done.17.nx = f32[4,4,2,128]{3,2,1,0:T(2,128)S(1)} collective-permute-done((f32[4,4,2,128]{3,2,1,0:T(2,128)S(1)}, f32[4,4,2,128]{3,2,1,0:T(2,128)S(1)}, u32[]{:S(2)}, u32[]{:S(2)}) %collective-permute-start.17) | collective-permute-done | bytes 16416 | tf_op jit(solution)/shard_map/ppermute | solution.py:226
  46.2 0.9 %shard_map.21 = f32[3,4,4,16,128]{4,3,2,1,0:T(8,128)} custom-call(f32[4,4,16,128]{3,2,1,0:T(8,128)S(1)} %get-tuple-element.27.gauge, f32[4,4,2,128]{3,2,1,0:T(2,128)S(1)} %collective-permute-done.17.nx, f32[4,4,8,128]{3,2,1,0:T(8,128)S(1)} %collective-permute-done.18.ny, f32[3,4,4,16,128]{4,3,2,1,0:T(8,128)S(1)} %get-tuple-element.30.links), custom_call_target="tpu_custom_call" | custom-call | tf_op jit(solution)/shard_map/pallas_call | solution.py:214
  (37 shorter events, 1.0 us)
Async XLA Ops:
  0.0 1.0 %copy-start = (f32[4,4,4,8,2,128]{5,4,3,2,1,0:T(2,128)S(1)}, f32[4,4,4,8,2,128]{5,4,3,2,1,0:T(2,128)}, u32[]{:S(2)}) copy-start(f32[4,4,4,8,2,128]{5,4,3,2,1,0:T(2,128)} %param.1) | copy-start | bytes 1572868
  1.1 9.8 %collective-permute-start.3 = (f32[7,4,4,2,128]{4,3,2,1,0:T(2,128)S(1)}, f32[7,4,4,2,128]{4,3,2,1,0:T(2,128)S(1)}, u32[]{:S(2)}, u32[]{:S(2)}) collective-permute-start(f32[7,4,4,2,128]{4,3,2,1,0:T(2,128)S(1)} %get-tuple-element.20), channel_id=1, source_target_pairs={{0,2},{2,0},{1,3},{3,1},{4,6},{6,4},{5,7},{7,5},{8,10},{10,8},{9,1... | collective-permute-start | bytes 344072 | tf_op jit(solution)/shard_map/ppermute | solution.py:226
  4.1 6.8 %collective-permute-start.2 = (f32[3,4,16,128]{3,2,1,0:T(8,128)S(1)}, f32[3,4,16,128]{3,2,1,0:T(8,128)S(1)}, u32[]{:S(2)}, u32[]{:S(2)}) collective-permute-start(f32[3,4,16,128]{3,2,1,0:T(8,128)S(1)} %get-tuple-element.19), channel_id=1, source_target_pairs={{0,12},{4,0},{8,4},{12,8},{1,13},{5,1},{9,5},{13,9},{2,14},{6,2},{... | collective-permute-start | bytes 294920 | tf_op jit(solution)/shard_map/ppermute | solution.py:226
  7.7 11.6 %collective-permute-start = (f32[4,4,4,16,128]{4,3,2,1,0:T(8,128)S(1)}, f32[4,4,4,16,128]{4,3,2,1,0:T(8,128)S(1)}, u32[]{:S(2)}, u32[]{:S(2)}) collective-permute-start(f32[4,4,4,16,128]{4,3,2,1,0:T(8,128)S(1)} %bitcast.3), channel_id=1, source_target_pairs={{0,1},{1,0},{2,3},{3,2},{4,5},{5,4},{6,7},{7,6},{8,9},{9,8},{10,11... | collective-permute-start | bytes 1572872 | tf_op jit(solution)/shard_map/ppermute | solution.py:226
  7.7 7.7 %collective-permute-start.1 = (f32[4,4,16,128]{3,2,1,0:T(8,128)S(1)}, f32[4,4,16,128]{3,2,1,0:T(8,128)S(1)}, u32[]{:S(2)}, u32[]{:S(2)}) collective-permute-start(f32[4,4,16,128]{3,2,1,0:T(8,128)S(1)} %get-tuple-element.18), channel_id=1, source_target_pairs={{0,4},{4,8},{8,12},{12,0},{1,5},{5,9},{9,13},{13,1},{2,6},{6,10},{... | collective-permute-start | bytes 393224 | tf_op jit(solution)/shard_map/ppermute | solution.py:226
  10.9 8.3 %collective-permute-start.6 = (f32[2,4,4,2,128]{4,3,2,1,0:T(2,128)S(1)}, f32[2,4,4,2,128]{4,3,2,1,0:T(2,128)S(1)}, u32[]{:S(2)}, u32[]{:S(2)}) collective-permute-start(f32[2,4,4,2,128]{4,3,2,1,0:T(2,128)S(1)} %pad_maximum_fusion.2), channel_id=1, source_target_pairs={{0,1},{1,0},{2,3},{3,2},{4,5},{5,4},{6,7},{7,6},{8,9},{9,8},{10,11... | collective-permute-start | bytes 98312 | tf_op jit(solution)/shard_map/ppermute | solution.py:226
  15.4 3.8 %collective-permute-start.5 = (f32[2,4,16,128]{3,2,1,0:T(8,128)S(1)}, f32[2,4,16,128]{3,2,1,0:T(8,128)S(1)}, u32[]{:S(2)}, u32[]{:S(2)}) collective-permute-start(f32[2,4,16,128]{3,2,1,0:T(8,128)S(1)} %pad_maximum_fusion), channel_id=1, source_target_pairs={{0,1},{1,0},{2,3},{3,2},{4,5},{5,4},{6,7},{7,6},{8,9},{9,8},{10,11... | collective-permute-start | bytes 196616 | tf_op jit(solution)/shard_map/ppermute | solution.py:226
  15.5 3.7 %collective-permute-start.4 = (f32[2,4,2,128]{3,2,1,0:T(2,128)S(1)}, f32[2,4,2,128]{3,2,1,0:T(2,128)S(1)}, u32[]{:S(2)}, u32[]{:S(2)}) collective-permute-start(f32[2,4,2,128]{3,2,1,0:T(2,128)S(1)} %pad_maximum_fusion.4), channel_id=1, source_target_pairs={{0,2},{2,0},{1,3},{3,1},{4,6},{6,4},{5,7},{7,5},{8,10},{10,8},{9,1... | collective-permute-start | bytes 24584 | tf_op jit(solution)/shard_map/ppermute | solution.py:226
  21.3 6.6 %collective-permute-start.10 = (f32[7,4,4,2,128]{4,3,2,1,0:T(2,128)S(1)}, f32[7,4,4,2,128]{4,3,2,1,0:T(2,128)S(1)}, u32[]{:S(2)}, u32[]{:S(2)}) collective-permute-start(f32[7,4,4,2,128]{4,3,2,1,0:T(2,128)S(1)} %get-tuple-element.24), channel_id=1, source_target_pairs={{0,2},{2,0},{1,3},{3,1},{4,6},{6,4},{5,7},{7,5},{8,10},{10,8},{9,1... | collective-permute-start | bytes 344072 | tf_op jit(solution)/shard_map/ppermute | solution.py:226
  21.9 6.0 %collective-permute-start.9 = (f32[3,4,16,128]{3,2,1,0:T(8,128)S(1)}, f32[3,4,16,128]{3,2,1,0:T(8,128)S(1)}, u32[]{:S(2)}, u32[]{:S(2)}) collective-permute-start(f32[3,4,16,128]{3,2,1,0:T(8,128)S(1)} %get-tuple-element.23), channel_id=1, source_target_pairs={{0,12},{4,0},{8,4},{12,8},{1,13},{5,1},{9,5},{13,9},{2,14},{6,2},{... | collective-permute-start | bytes 294920 | tf_op jit(solution)/shard_map/ppermute | solution.py:226
  22.6 6.8 %collective-permute-start.8 = (f32[4,4,16,128]{3,2,1,0:T(8,128)S(1)}, f32[4,4,16,128]{3,2,1,0:T(8,128)S(1)}, u32[]{:S(2)}, u32[]{:S(2)}) collective-permute-start(f32[4,4,16,128]{3,2,1,0:T(8,128)S(1)} %get-tuple-element.22), channel_id=1, source_target_pairs={{0,4},{4,8},{8,12},{12,0},{1,5},{5,9},{9,13},{13,1},{2,6},{6,10},{... | collective-permute-start | bytes 393224 | tf_op jit(solution)/shard_map/ppermute | solution.py:226
  23.9 9.3 %collective-permute-start.7 = (f32[4,4,4,16,128]{4,3,2,1,0:T(8,128)S(1)}, f32[4,4,4,16,128]{4,3,2,1,0:T(8,128)S(1)}, u32[]{:S(2)}, u32[]{:S(2)}) collective-permute-start(f32[4,4,4,16,128]{4,3,2,1,0:T(8,128)S(1)} %get-tuple-element.21.own), channel_id=1, source_target_pairs={{0,1},{1,0},{2,3},{3,2},{4,5},{5,4},{6,7},{7,6},{8,9},{9,8},{10,11... | collective-permute-start | bytes 1572872 | tf_op jit(solution)/shard_map/ppermute | solution.py:226
  27.9 5.3 %collective-permute-start.13 = (f32[2,4,4,2,128]{4,3,2,1,0:T(2,128)S(1)}, f32[2,4,4,2,128]{4,3,2,1,0:T(2,128)S(1)}, u32[]{:S(2)}, u32[]{:S(2)}) collective-permute-start(f32[2,4,4,2,128]{4,3,2,1,0:T(2,128)S(1)} %pad_maximum_fusion.3), channel_id=1, source_target_pairs={{0,1},{1,0},{2,3},{3,2},{4,5},{5,4},{6,7},{7,6},{8,9},{9,8},{10,11... | collective-permute-start | bytes 98312 | tf_op jit(solution)/shard_map/ppermute | solution.py:226
  29.4 3.8 %collective-permute-start.12 = (f32[2,4,16,128]{3,2,1,0:T(8,128)S(1)}, f32[2,4,16,128]{3,2,1,0:T(8,128)S(1)}, u32[]{:S(2)}, u32[]{:S(2)}) collective-permute-start(f32[2,4,16,128]{3,2,1,0:T(8,128)S(1)} %pad_maximum_fusion.1), channel_id=1, source_target_pairs={{0,1},{1,0},{2,3},{3,2},{4,5},{5,4},{6,7},{7,6},{8,9},{9,8},{10,11... | collective-permute-start | bytes 196616 | tf_op jit(solution)/shard_map/ppermute | solution.py:226
  29.5 3.7 %collective-permute-start.11 = (f32[2,4,2,128]{3,2,1,0:T(2,128)S(1)}, f32[2,4,2,128]{3,2,1,0:T(2,128)S(1)}, u32[]{:S(2)}, u32[]{:S(2)}) collective-permute-start(f32[2,4,2,128]{3,2,1,0:T(2,128)S(1)} %pad_maximum_fusion.5), channel_id=1, source_target_pairs={{0,2},{2,0},{1,3},{3,1},{4,6},{6,4},{5,7},{7,5},{8,10},{10,8},{9,1... | collective-permute-start | bytes 24584 | tf_op jit(solution)/shard_map/ppermute | solution.py:226
  35.2 4.0 %collective-permute-start.16 = (f32[4,16,128]{2,1,0:T(8,128)S(1)}, f32[4,16,128]{2,1,0:T(8,128)S(1)}, u32[]{:S(2)}, u32[]{:S(2)}) collective-permute-start(f32[4,16,128]{2,1,0:T(8,128)S(1)} %get-tuple-element.26), channel_id=1, source_target_pairs={{0,12},{4,0},{8,4},{12,8},{1,13},{5,1},{9,5},{13,9},{2,14},{6,2},{... | collective-permute-start | bytes 98312 | tf_op jit(solution)/shard_map/ppermute | solution.py:226
  36.2 4.8 %collective-permute-start.15 = (f32[4,16,128]{2,1,0:T(8,128)S(1)}, f32[4,16,128]{2,1,0:T(8,128)S(1)}, u32[]{:S(2)}, u32[]{:S(2)}) collective-permute-start(f32[4,16,128]{2,1,0:T(8,128)S(1)} %get-tuple-element.26), channel_id=1, source_target_pairs={{0,8},{4,12},{8,0},{12,4},{1,9},{5,13},{9,1},{13,5},{2,10},{6,14},... | collective-permute-start | bytes 98312 | tf_op jit(solution)/shard_map/ppermute | solution.py:226
  36.6 5.7 %collective-permute-start.14 = (f32[4,16,128]{2,1,0:T(8,128)S(1)}, f32[4,16,128]{2,1,0:T(8,128)S(1)}, u32[]{:S(2)}, u32[]{:S(2)}) collective-permute-start(f32[4,16,128]{2,1,0:T(8,128)S(1)} %get-tuple-element.26), channel_id=1, source_target_pairs={{0,4},{4,8},{8,12},{12,0},{1,5},{5,9},{9,13},{13,1},{2,6},{6,10},{... | collective-permute-start | bytes 98312 | tf_op jit(solution)/shard_map/ppermute | solution.py:226
  42.4 3.9 %collective-permute-start.18 = (f32[4,4,8,128]{3,2,1,0:T(8,128)S(1)}, f32[4,4,8,128]{3,2,1,0:T(8,128)S(1)}, u32[]{:S(2)}, u32[]{:S(2)}) collective-permute-start(f32[4,4,8,128]{3,2,1,0:T(8,128)S(1)} %get-tuple-element.29), channel_id=1, source_target_pairs={{0,1},{1,0},{2,3},{3,2},{4,5},{5,4},{6,7},{7,6},{8,9},{9,8},{10,11... | collective-permute-start | bytes 196616 | tf_op jit(solution)/shard_map/ppermute | solution.py:226
  42.4 3.8 %collective-permute-start.17 = (f32[4,4,2,128]{3,2,1,0:T(2,128)S(1)}, f32[4,4,2,128]{3,2,1,0:T(2,128)S(1)}, u32[]{:S(2)}, u32[]{:S(2)}) collective-permute-start(f32[4,4,2,128]{3,2,1,0:T(2,128)S(1)} %get-tuple-element.28), channel_id=1, source_target_pairs={{0,2},{2,0},{1,3},{3,1},{4,6},{6,4},{5,7},{7,5},{8,10},{10,8},{9,1... | collective-permute-start | bytes 49160 | tf_op jit(solution)/shard_map/ppermute | solution.py:226

commit v2 on v1

v2 whole, which is shorter than its diff:
```python
import jax
import jax.numpy as jnp
from jax import lax
from jax.experimental import pallas as pl
from jax.experimental.pallas import tpu as pltpu
from jax.sharding import PartitionSpec as P

smear_weight = 0.1
VMEM = pl.BlockSpec(memory_space=pltpu.VMEM)
F32 = jnp.float32
BASE = 8


def mul(a, b):
    return (
        a[0] * b[0] - a[1] * b[1] - a[2] * b[2] - a[3] * b[3],
        a[0] * b[1] + a[1] * b[0] + a[2] * b[3] - a[3] * b[2],
        a[0] * b[2] - a[1] * b[3] + a[2] * b[0] + a[3] * b[1],
        a[0] * b[3] + a[1] * b[2] - a[2] * b[1] + a[3] * b[0],
    )


def mul_cr(a, b):
    return (
        a[0] * b[0] + a[1] * b[1] + a[2] * b[2] + a[3] * b[3],
        a[1] * b[0] - a[0] * b[1] - a[2] * b[3] + a[3] * b[2],
        a[2] * b[0] - a[0] * b[2] + a[1] * b[3] - a[3] * b[1],
        a[3] * b[0] - a[0] * b[3] - a[1] * b[2] + a[2] * b[1],
    )


def mul_cl(a, b):
    return (
        a[0] * b[0] + a[1] * b[1] + a[2] * b[2] + a[3] * b[3],
        a[0] * b[1] - a[1] * b[0] - a[2] * b[3] + a[3] * b[2],
        a[0] * b[2] + a[1] * b[3] - a[2] * b[0] - a[3] * b[1],
        a[0] * b[3] - a[1] * b[2] + a[2] * b[1] - a[3] * b[0],
    )


def add(a, b):
    return tuple(x + y for x, y in zip(a, b))


def zroll(a, amount):
    return tuple(pltpu.roll(x, amount % 128, 1) for x in a)


def accessor(eo, ep, low, high):
    tl = eo.shape[2]
    cache = {}

    def ld(d, t, x, y, z=0):
        key = (d, t, x, y, z)
        if key not in cache:
            if z:
                cache[key] = zroll(ld(d, t, x, y), -z)
            else:
                mine = 0 <= y < 2
                rows = pl.ds(BASE + 2 * x + y % 2, 8, stride=2)
                if 0 <= t < tl:
                    ref = eo if mine else ep
                    cache[key] = tuple(ref[d, c, t, rows, :] for c in range(4))
                else:
                    ref = (low if t < 0 else high)[0 if mine else 1]
                    cache[key] = tuple(ref[d, c, rows, :] for c in range(4))
        return cache[key]

    return ld


def moved(s, d, k=1):
    return tuple(v + k if i == d else v for i, v in enumerate(s))


def smear_link(ld, m, s):
    total = None
    here = ld(m, *s)
    for n in range(4):
        if n == m:
            continue
        u = mul_cr(mul(ld(n, *s), ld(m, *moved(s, n))), ld(n, *moved(s, m)))
        if n == 3:
            v = zroll(mul(mul_cl(ld(n, *s), here), ld(n, *moved(s, m))), 1)
        else:
            b = moved(s, n, -1)
            v = mul(mul_cl(ld(n, *b), ld(m, *b)), ld(n, *moved(b, m)))
        total = add(u, v) if total is None else add(total, add(u, v))
    comb = tuple(h + smear_weight * w for h, w in zip(here, total))
    norm = comb[0] * comb[0] + comb[1] * comb[1] + comb[2] * comb[2] + comb[3] * comb[3]
    inv = lax.rsqrt(norm)
    return tuple(v * inv for v in comb)


def fill(own, par, xh, x_shared, eo, ep):
    for d in range(4):
        eo[d, :, :, BASE : BASE + 16, :] = own[d]
        ep[d, :, :, BASE : BASE + 16, :] = par[d]
        eo[d, :, :, BASE - 2 : BASE, :] = xh[3 + d]
    for slot, d in enumerate((0, 2, 3)):
        eo[d, :, :, BASE + 16 : BASE + 18, :] = xh[slot]
    ep[2, :, :, BASE + 16 : BASE + 18, :] = x_shared[0]
    ep[1, :, :, BASE - 2 : BASE, :] = x_shared[1]
    ep[2, :, :, BASE - 2 : BASE, :] = x_shared[2]


def interior_1(own, par, xh, x_shared, eo, ep, new):
    tl = own.shape[2]
    fill(own, par, xh, x_shared, eo, ep)
    for t in range(1, tl - 1):
        for y in range(2):
            ld = accessor(eo, ep, None, None)
            for d in range(4):
                q = smear_link(ld, d, (t, 0, y, 0))
                for c in range(4):
                    new[d, c, t, pl.ds(y, 8, stride=2), :] = q[c]


MAIN = slice(BASE, BASE + 16)
BEFORE = slice(BASE - 2, BASE)
AFTER = slice(BASE + 16, BASE + 18)


def edges_1(
    eo, ep, part, t_below, t_above, t_shared, corner, new, t_dn, t_up, xs, lo, lp, ho, hp
):
    tl = eo.shape[2]
    lo[:, :, MAIN, :] = t_below[...]
    lo[0, :, AFTER, :] = corner[0]
    lo[0:2, :, BEFORE, :] = corner[2:4]
    lp[0, :, MAIN, :] = t_shared[0]
    lp[2, :, MAIN, :] = t_shared[1]
    ho[1:4, :, MAIN, :] = t_above[...]
    ho[1, :, BEFORE, :] = corner[1]
    hp[2, :, MAIN, :] = t_shared[2]
    for t in range(1, tl - 1):
        new[:, :, t] = part[:, :, t]
    for t in (0, tl - 1):
        for y in range(2):
            ld = accessor(eo, ep, (lo, lp), (ho, hp))
            for d in range(4):
                q = smear_link(ld, d, (t, 0, y, 0))
                for c in range(4):
                    new[d, c, t, pl.ds(y, 8, stride=2), :] = q[c]
    for d in range(3):
        for c in range(4):
            t_dn[64 * d + 16 * c : 64 * d + 16 * c + 16, :] = new[d + 1, c, 0]
    q = smear_link(accessor(eo, ep, (lo, lp), None), 2, (0, 0, -1, 0))
    for c in range(4):
        t_dn[192 + 8 * c : 200 + 8 * c, :] = q[c]
    for y in range(2):
        q = smear_link(accessor(eo, ep, (lo, lp), None), 1, (0, -1, y, 0))
        for c in range(4):
            t_dn[224 + 2 * c + y : 225 + 2 * c + y, :] = q[c][0:1]
    t_up[...] = new[:, :, tl - 1]
    for slot, d in enumerate((0, 2, 3)):
        xs[slot] = new[d, :, :, 0:2, :]
    for d in range(4):
        xs[3 + d] = new[d, :, :, 14:16, :]


def interior_2(own, par, xh, x_shared, eo, ep, prefix, new):
    tl = own.shape[2]
    fill(own, par, xh, x_shared, eo, ep)
    for y in range(2):
        rows = pl.ds(y, 8, stride=2)
        one = jnp.ones((8, 128), F32)
        zero = jnp.zeros((8, 128), F32)
        state = (one, zero, zero, zero)
        for t in range(tl):
            for c in range(4):
                prefix[c, t, rows, :] = state[c]
            if t < tl - 1:
                ld = accessor(eo, ep, None, None)
                q = smear_link(ld, 0, (t, 0, y, 0))
                state = q if t == 0 else mul(state, q)
                if t > 0:
                    for d in range(1, 4):
                        q = smear_link(ld, d, (t, 0, y, 0))
                        for c in range(4):
                            new[d - 1, c, t, rows, :] = q[c]


def slab_kernel(eo, ep, t_above, prefix, slab, ho, hp):
    tl = eo.shape[2]
    for d in range(3):
        for c in range(4):
            ho[d + 1, c, MAIN, :] = t_above[64 * d + 16 * c : 64 * d + 16 * c + 16, :]
    for c in range(4):
        hp[2, c, pl.ds(BASE + 1, 8, stride=2), :] = t_above[192 + 8 * c : 200 + 8 * c, :]
        ho[1, c, BEFORE, :] = t_above[224 + 2 * c : 226 + 2 * c, :]
    for y in range(2):
        rows = pl.ds(y, 8, stride=2)
        q = smear_link(accessor(eo, ep, None, (ho, hp)), 0, (tl - 1, 0, y, 0))
        state = mul(tuple(prefix[c, tl - 1, rows, :] for c in range(4)), q)
        for c in range(4):
            slab[c, rows, :] = state[c]


def edges_2(eo, ep, part, t_above, t_below, t_shared, corner, new, lo, lp, ho):
    tl = eo.shape[2]
    lo[:, :, MAIN, :] = t_below[...]
    lo[0, :, AFTER, :] = corner[...]
    lp[0, :, MAIN, :] = t_shared[...]
    for d in range(3):
        for c in range(4):
            ho[d + 1, c, MAIN, :] = t_above[64 * d + 16 * c : 64 * d + 16 * c + 16, :]
    for t in range(1, tl - 1):
        new[:, :, t] = part[:, :, t]
    for t in (0, tl - 1):
        for y in range(2):
            ld = accessor(eo, ep, (lo, lp), (ho, None))
            for d in range(1, 4):
                q = smear_link(ld, d, (t, 0, y, 0))
                for c in range(4):
                    new[d - 1, c, t, pl.ds(y, 8, stride=2), :] = q[c]


def boundary(out, t_up, t_dn, xs):
    tl = out.shape[2]
    t_up[...] = out[:, :, tl - 1]
    t_dn[...] = out[1:4, :, 0]
    for slot, d in enumerate((0, 2, 3)):
        xs[slot] = out[d, :, :, 0:2, :]
    for d in range(4):
        xs[3 + d] = out[d, :, :, 14:16, :]


def carry_kernel(n, prefix, slab_list, gauge, gx, gy):
    tl = prefix.shape[1]
    place = lax.axis_index("tm")
    for half in range(2):
        rows = pl.ds(half * 8, 8)
        state = None
        for j in reversed(range(n - 1)):
            q = tuple(slab_list[j][c, rows, :] for c in range(4))
            there = place >= j + 1
            q = tuple(jnp.where(there, v, 1.0 if c == 0 else 0.0) for c, v in enumerate(q))
            state = q if state is None else mul(state, q)
        for t in range(tl):
            g = mul(state, tuple(prefix[c, t, rows, :] for c in range(4)))
            for c in range(4):
                gauge[c, t, rows, :] = g[c]
    gx[...] = gauge[:, :, 0:2, :]
    for c in range(4):
        for t in range(tl):
            gy[c, t] = gauge[c, t, pl.ds(0, 8, stride=2), :]


def rotate_kernel(gauge, nx, ny, links, out, ext):
    tl = gauge.shape[1]
    ext[:, :, 0:16, :] = gauge[...]
    ext[:, :, 16:18, :] = nx[...]
    for t in range(tl):
        for y in range(2):
            rows = pl.ds(y, 8, stride=2)
            g = tuple(gauge[c, t, rows, :] for c in range(4))
            g1 = tuple(ext[c, t, pl.ds(2 + y, 8, stride=2), :] for c in range(4))
            if y == 0:
                g2 = tuple(gauge[c, t, pl.ds(1, 8, stride=2), :] for c in range(4))
            else:
                g2 = tuple(ny[c, t] for c in range(4))
            g3 = zroll(g, -1)
            for d, other in enumerate((g1, g2, g3)):
                u = tuple(links[d, c, t, rows, :] for c in range(4))
                r = mul_cr(mul(g, u), other)
                for c in range(4):
                    out[d, c, t, rows, :] = r[c]


def call(kernel, outs, scratch, *args):
    single = isinstance(outs[0], int)
    shapes = [jax.ShapeDtypeStruct(s, F32) for s in ([outs] if single else outs)]
    return pl.pallas_call(
        kernel,
        out_shape=shapes[0] if single else shapes,
        in_specs=[VMEM] * len(args),
        out_specs=VMEM if single else [VMEM] * len(shapes),
        scratch_shapes=[pltpu.VMEM(s, F32) for s in scratch],
        compiler_params=pltpu.CompilerParams(vmem_limit_bytes=40 * 2**20),
    )(*args)


def rotated_by(x, axis, steps):
    n = lax.axis_size(axis)
    return lax.ppermute(x, axis, [(i, (i + steps) % n) for i in range(n)])


def x_exchange(xs, cut):
    if lax.axis_size("space") == 2:
        return rotated_by(xs, "space", 1)
    return jnp.concatenate(
        [rotated_by(xs[:cut], "space", -1), rotated_by(xs[cut:], "space", 1)]
    )


def side_halo(own, xs):
    xh = x_exchange(xs, 3)
    par = rotated_by(own, "pair", 1)
    x_shared = rotated_by(jnp.stack([xh[1], xh[4], xh[5]]), "pair", 1)
    return par, xh, x_shared


def on_device(link_field):
    tl, xl, yl, z = link_field.shape[2:]
    rows = xl * yl
    links = link_field.reshape(4, 4, tl, rows, z)
    block = (4, 4, tl, rows, z)
    ext = (4, 4, tl, 32, z)
    layer = (4, 4, 32, z)
    t_up, t_dn, xs = call(
        boundary, [(4, 4, rows, z), (3, 4, rows, z), (7, 4, tl, 2, z)], [], links
    )
    t_below = rotated_by(t_up, "tm", 1)
    t_above = rotated_by(t_dn, "tm", -1)
    sides = side_halo(links, xs)
    eo, ep, part = call(interior_1, [ext, ext, block], [], links, *sides)
    corner = x_exchange(
        jnp.stack([t_below[0, :, :2], t_above[0, :, -2:], t_below[0, :, -2:], t_below[1, :, -2:]]),
        1,
    )
    t_shared = rotated_by(jnp.stack([t_below[0], t_below[2], t_above[1]]), "pair", 1)
    links, t_dn, t_up, xs = call(
        edges_1,
        [block, (232, z), (4, 4, rows, z), (7, 4, tl, 2, z)],
        [layer] * 4,
        eo,
        ep,
        part,
        t_below,
        t_above,
        t_shared,
        corner,
    )
    t_above = rotated_by(t_dn, "tm", -1)
    t_below = rotated_by(t_up, "tm", 1)
    sides = side_halo(links, xs)
    spatial = (3, 4, tl, rows, z)
    eo, ep, prefix, part = call(
        interior_2, [ext, ext, (4, tl, rows, z), spatial], [], links, *sides
    )
    slab = call(slab_kernel, (4, rows, z), [layer] * 2, eo, ep, t_above, prefix)
    n = lax.axis_size("tm")
    slabs = [rotated_by(slab, "tm", k) for k in range(1, n)]
    corner = rotated_by(t_below[0, :, :2], "space", -1)
    t_shared = rotated_by(t_below[0], "pair", 1)
    smeared = call(
        edges_2, spatial, [layer] * 3, eo, ep, part, t_above, t_below, t_shared, corner
    )
    gauge, gx, gy = call(
        lambda p, *rest: carry_kernel(n, p, rest[: n - 1], *rest[n - 1 :]),
        [(4, tl, rows, z), (4, tl, 2, z), (4, tl, xl, z)],
        [],
        prefix,
        *slabs,
    )
    nx = rotated_by(gx, "space", -1)
    ny = rotated_by(gy, "pair", -1)
    out = call(rotate_kernel, spatial, [(4, tl, 24, z)], gauge, nx, ny, smeared)
    return out.reshape(3, 4, tl, xl, yl, z)


def solution(mesh):
    spec = P(None, None, "tm", "space", "pair", "groups")
    return jax.shard_map(on_device, mesh=mesh, in_specs=(spec,), out_specs=spec, check_vma=False)
```

time: 47.3 us -> 42.6 us (0.901)
  waiting for transfers between devices: 25 us -> 16.7 us
  starting transfers between devices: 15.9 us -> 19.4 us
    ppermute x19, waiting for transfers between devices: 25 us -> 16.7 us  [rotated_by(): return lax.ppermute(x, axis, [(i, (i + steps) % n) for i in range(n)])]
    ppermute x19, starting transfers between devices: 15.9 us -> 19.4 us  [rotated_by(): return lax.ppermute(x, axis, [(i, (i + steps) % n) for i in range(n)])]
    pallas_call x5 -> x8, Pallas kernels: 5.03 us -> 4.97 us  [call(): pl.pallas_call(kernel, out_shape=shapes[0] if single else shapes, in_spec...]
  transfers between devices with their start and end apart: 19 -> 19, of which waited for: 10 -> 9; matrix products, arithmetic and copies ran while one was open for 0% -> 0% of each run, Pallas kernels for 0% -> 7%
where the time goes in v2:
time: 42.6 us; the launch traced here: 42.5 us
  starting transfers between devices  19.4 us (46%)
  waiting for transfers between devices  16.7 us (39%)
  Pallas kernels  4.97 us (12%)
  local copies, waits for them, and re-layouts  1.08 us (3%)
    ppermute x19, starting transfers between devices, rotated_by(): return lax.ppermute(x, axis, [(i, (i + steps) % n) for i in range(n)])  19.4 us
    ppermute x19, waiting for transfers between devices, rotated_by(): return lax.ppermute(x, axis, [(i, (i + steps) % n) for i in range(n)])  16.7 us
    pallas_call x8, Pallas kernels, call(): pl.pallas_call(kernel, out_shape=shapes[0] if single else shapes, in_spec...  4.97 us
    unnamed x2, local copies, waits for them, and re-layouts  1.04 us
  transfers between devices with their start and end apart: 19, of which 9 were waited for; matrix products, arithmetic and copies ran while one was open for 0% of the time, Pallas kernels for 7%

profile of v2, /device:TPU:0, one launch (start us, length us, event | category | flops | bytes accessed | tf_op | source)
XLA Modules:
  0.0 42.5 jit_solution(10058051780071680587)
XLA Ops:
  0.0 1.0 %copy-done = f32[4,4,4,8,2,128]{5,4,3,2,1,0:T(2,128)S(1)} copy-done((f32[4,4,4,8,2,128]{5,4,3,2,1,0:T(2,128)S(1)}, f32[4,4,4,8,2,128]{5,4,3,2,1,0:T(2,128)}, u32[]{:S(2)}) %copy-start) | copy-done | bytes 524312
  1.1 3.0 %collective-permute-start.1 = (f32[7,4,4,2,128]{4,3,2,1,0:T(2,128)S(1)}, f32[7,4,4,2,128]{4,3,2,1,0:T(2,128)S(1)}, u32[]{:S(2)}, u32[]{:S(2)}) collective-permute-start(f32[7,4,4,2,128]{4,3,2,1,0:T(2,128)S(1)} %get-tuple-element.22), channel_id=1, source_target_pairs={{0,2},{2,0},{1,3},{3,1},{4,6},{6,4},{5,7},{7,5},{8,10},{10,8},{9,1... | collective-permute-start | bytes 344072 | tf_op jit(solution)/shard_map/ppermute | solution.py:286
  4.1 3.6 %collective-permute-start.4 = (f32[3,4,16,128]{3,2,1,0:T(8,128)S(1)}, f32[3,4,16,128]{3,2,1,0:T(8,128)S(1)}, u32[]{:S(2)}, u32[]{:S(2)}) collective-permute-start(f32[3,4,16,128]{3,2,1,0:T(8,128)S(1)} %get-tuple-element.27), channel_id=1, source_target_pairs={{0,12},{4,0},{8,4},{12,8},{1,13},{5,1},{9,5},{13,9},{2,14},{6,2},{... | collective-permute-start | bytes 294920 | tf_op jit(solution)/shard_map/ppermute | solution.py:286
  7.7 3.2 %collective-permute-done.4.t_above = f32[3,4,16,128]{3,2,1,0:T(8,128)S(1)} collective-permute-done((f32[3,4,16,128]{3,2,1,0:T(8,128)S(1)}, f32[3,4,16,128]{3,2,1,0:T(8,128)S(1)}, u32[]{:S(2)}, u32[]{:S(2)}) %collective-permute-start.4) | collective-permute-done | bytes 98336 | tf_op jit(solution)/shard_map/ppermute | solution.py:286
  11.1 3.4 %collective-permute-done.3.t_below = f32[4,4,16,128]{3,2,1,0:T(8,128)S(1)} collective-permute-done((f32[4,4,16,128]{3,2,1,0:T(8,128)S(1)}, f32[4,4,16,128]{3,2,1,0:T(8,128)S(1)}, u32[]{:S(2)}, u32[]{:S(2)}) %collective-permute-start.3) | collective-permute-done | bytes 131104 | tf_op jit(solution)/shard_map/ppermute | solution.py:286
  14.6 0.6 %collective-permute-start.6 = (f32[4,4,2,128]{3,2,1,0:T(2,128)S(1)}, f32[4,4,2,128]{3,2,1,0:T(2,128)S(1)}, u32[]{:S(2)}, u32[]{:S(2)}) collective-permute-start(f32[4,4,2,128]{3,2,1,0:T(2,128)S(1)} %pad_maximum_fusion.3), channel_id=1, source_target_pairs={{0,2},{2,0},{1,3},{3,1},{4,6},{6,4},{5,7},{7,5},{8,10},{10,8},{9,1... | collective-permute-start | bytes 49160 | tf_op jit(solution)/shard_map/ppermute | solution.py:286
  15.2 1.0 %shard_map.18 = (f32[4,4,4,32,128]{4,3,2,1,0:T(8,128)S(1)}, f32[4,4,4,32,128]{4,3,2,1,0:T(8,128)S(1)}, f32[4,4,4,16,128]{4,3,2,1,0:T(8,128)S(1)}) custom-call(f32[4,4,4,16,128]{4,3,2,1,0:T(8,128)S(1)} %bitcast.8, f32[4,4,4,16,128]{4,3,2,1,0:T(8,128)S(1)} %collective-permute-done.par, f32[7,4,4,2,128]{4,3,2,1,0:T(2,128)S(1)} %collective-permute-done.1.xh, ...), custom_call_target="tpu_custom_call" | custom-call | tf_op jit(solution)/shard_map/pallas_call | solution.py:274
  16.2 2.2 %collective-permute-done.6.corner = f32[4,4,2,128]{3,2,1,0:T(2,128)S(1)} collective-permute-done((f32[4,4,2,128]{3,2,1,0:T(2,128)S(1)}, f32[4,4,2,128]{3,2,1,0:T(2,128)S(1)}, u32[]{:S(2)}, u32[]{:S(2)}) %collective-permute-start.6) | collective-permute-done | bytes 16416 | tf_op jit(solution)/shard_map/ppermute | solution.py:286
  18.4 1.1 %shard_map.19 = (f32[4,4,4,16,128]{4,3,2,1,0:T(8,128)S(1)}, f32[232,128]{1,0:T(8,128)S(1)}, f32[4,4,16,128]{3,2,1,0:T(8,128)S(1)}, f32[7,4,4,2,128]{4,3,2,1,0:T(2,128)S(1)}) custom-call(f32[4,4,4,32,128]{4,3,2,1,0:T(8,128)S(1)} %get-tuple-element.23.eo, f32[4,4,4,32,128]{4,3,2,1,0:T(8,128)S(1)} %get-tuple-element.24.ep, ...), custom_call_target="tpu_custom_call" | custom-call | tf_op jit(solution)/shard_map/pallas_call | solution.py:274
  19.6 0.6 %collective-permute-start.8 = (f32[7,4,4,2,128]{4,3,2,1,0:T(2,128)S(1)}, f32[7,4,4,2,128]{4,3,2,1,0:T(2,128)S(1)}, u32[]{:S(2)}, u32[]{:S(2)}) collective-permute-start(f32[7,4,4,2,128]{4,3,2,1,0:T(2,128)S(1)} %get-tuple-element.29), channel_id=1, source_target_pairs={{0,2},{2,0},{1,3},{3,1},{4,6},{6,4},{5,7},{7,5},{8,10},{10,8},{9,1... | collective-permute-start | bytes 344072 | tf_op jit(solution)/shard_map/ppermute | solution.py:286
  20.6 3.5 %collective-permute-start.10 = (f32[232,128]{1,0:T(8,128)S(1)}, f32[232,128]{1,0:T(8,128)S(1)}, u32[]{:S(2)}, u32[]{:S(2)}) collective-permute-start(f32[232,128]{1,0:T(8,128)S(1)} %get-tuple-element.33), channel_id=1, source_target_pairs={{0,12},{4,0},{8,4},{12,8},{1,13},{5,1},{9,5},{13,9},{2,14},{6,2},{... | collective-permute-start | bytes 356360 | tf_op jit(solution)/shard_map/ppermute | solution.py:286
  24.0 1.1 %collective-permute-done.8.xh = f32[7,4,4,2,128]{4,3,2,1,0:T(2,128)S(1)} collective-permute-done((f32[7,4,4,2,128]{4,3,2,1,0:T(2,128)S(1)}, f32[7,4,4,2,128]{4,3,2,1,0:T(2,128)S(1)}, u32[]{:S(2)}, u32[]{:S(2)}) %collective-permute-start.8) | collective-permute-done | bytes 114720 | tf_op jit(solution)/shard_map/ppermute | solution.py:286
  25.3 1.2 %collective-permute-done.9.x_shared = f32[3,4,4,2,128]{4,3,2,1,0:T(2,128)S(1)} collective-permute-done((f32[3,4,4,2,128]{4,3,2,1,0:T(2,128)S(1)}, f32[3,4,4,2,128]{4,3,2,1,0:T(2,128)S(1)}, u32[]{:S(2)}, u32[]{:S(2)}) %collective-permute-start.9) | collective-permute-done | bytes 49184 | tf_op jit(solution)/shard_map/ppermute | solution.py:286
  26.5 1.1 %shard_map.20 = (f32[4,4,4,32,128]{4,3,2,1,0:T(8,128)S(1)}, f32[4,4,4,32,128]{4,3,2,1,0:T(8,128)S(1)}, f32[4,4,16,128]{3,2,1,0:T(8,128)S(1)}, f32[3,4,4,16,128]{4,3,2,1,0:T(8,128)S(1)}) custom-call(f32[4,4,4,16,128]{4,3,2,1,0:T(8,128)S(1)} %get-tuple-element.28.own, f32[4,4,4,16,128]{4,3,2,1,0:T(8,128)S(1)} %collective-permute-done.7.par, ...), custom_call_target="tpu_custom_call" | custom-call | tf_op jit(solution)/shard_map/pallas_call | solution.py:274
  27.6 0.8 %collective-permute-done.10.t_above = f32[232,128]{1,0:T(8,128)S(1)} collective-permute-done((f32[232,128]{1,0:T(8,128)S(1)}, f32[232,128]{1,0:T(8,128)S(1)}, u32[]{:S(2)}, u32[]{:S(2)}) %collective-permute-start.10) | collective-permute-done | bytes 118816 | tf_op jit(solution)/shard_map/ppermute | solution.py:286
  28.8 2.8 %collective-permute-start.12 = (f32[4,16,128]{2,1,0:T(8,128)S(1)}, f32[4,16,128]{2,1,0:T(8,128)S(1)}, u32[]{:S(2)}, u32[]{:S(2)}) collective-permute-start(f32[4,16,128]{2,1,0:T(8,128)S(1)} %shard_map.21), channel_id=1, source_target_pairs={{0,8},{4,12},{8,0},{12,4},{1,9},{5,13},{9,1},{13,5},{2,10},{6,14},... | collective-permute-start | bytes 98312 | tf_op jit(solution)/shard_map/ppermute | solution.py:286
  31.6 2.2 %collective-permute-start.13 = (f32[4,16,128]{2,1,0:T(8,128)S(1)}, f32[4,16,128]{2,1,0:T(8,128)S(1)}, u32[]{:S(2)}, u32[]{:S(2)}) collective-permute-start(f32[4,16,128]{2,1,0:T(8,128)S(1)} %shard_map.21), channel_id=1, source_target_pairs={{0,12},{4,0},{8,4},{12,8},{1,13},{5,1},{9,5},{13,9},{2,14},{6,2},{... | collective-permute-start | bytes 98312 | tf_op jit(solution)/shard_map/ppermute | solution.py:286
  33.9 0.7 %collective-permute-done.11.rest_0_ = f32[4,16,128]{2,1,0:T(8,128)S(1)} collective-permute-done((f32[4,16,128]{2,1,0:T(8,128)S(1)}, f32[4,16,128]{2,1,0:T(8,128)S(1)}, u32[]{:S(2)}, u32[]{:S(2)}) %collective-permute-start.11) | collective-permute-done | bytes 32800 | tf_op jit(solution)/shard_map/ppermute | solution.py:286
  34.5 1.0 %collective-permute-done.13.rest_2_ = f32[4,16,128]{2,1,0:T(8,128)S(1)} collective-permute-done((f32[4,16,128]{2,1,0:T(8,128)S(1)}, f32[4,16,128]{2,1,0:T(8,128)S(1)}, u32[]{:S(2)}, u32[]{:S(2)}) %collective-permute-start.13) | collective-permute-done | bytes 32800 | tf_op jit(solution)/shard_map/ppermute | solution.py:286
  35.7 1.6 %collective-permute-start.14 = (f32[4,4,2,128]{3,2,1,0:T(2,128)S(1)}, f32[4,4,2,128]{3,2,1,0:T(2,128)S(1)}, u32[]{:S(2)}, u32[]{:S(2)}) collective-permute-start(f32[4,4,2,128]{3,2,1,0:T(2,128)S(1)} %get-tuple-element.35), channel_id=1, source_target_pairs={{0,2},{2,0},{1,3},{3,1},{4,6},{6,4},{5,7},{7,5},{8,10},{10,8},{9,1... | collective-permute-start | bytes 49160 | tf_op jit(solution)/shard_map/ppermute | solution.py:286
  37.2 0.5 %collective-permute-start.18 = (f32[4,2,128]{2,1,0:T(2,128)S(1)}, f32[4,2,128]{2,1,0:T(2,128)S(1)}, u32[]{:S(2)}, u32[]{:S(2)}) collective-permute-start(f32[4,2,128]{2,1,0:T(2,128)S(1)} %slice_bitcast_fusion.1), channel_id=1, source_target_pairs={{0,2},{2,0},{1,3},{3,1},{4,6},{6,4},{5,7},{7,5},{8,10},{10,8},{9,1... | collective-permute-start | bytes 12296 | tf_op jit(solution)/shard_map/ppermute | solution.py:286
  37.8 3.1 %collective-permute-done.18.corner = f32[4,2,128]{2,1,0:T(2,128)S(1)} collective-permute-done((f32[4,2,128]{2,1,0:T(2,128)S(1)}, f32[4,2,128]{2,1,0:T(2,128)S(1)}, u32[]{:S(2)}, u32[]{:S(2)}) %collective-permute-start.18) | collective-permute-done | bytes 4128 | tf_op jit(solution)/shard_map/ppermute | solution.py:286
  40.9 0.6 %shard_map.23.links = f32[3,4,4,16,128]{4,3,2,1,0:T(8,128)S(1)} custom-call(f32[4,4,4,32,128]{4,3,2,1,0:T(8,128)S(1)} %get-tuple-element.31.eo, f32[4,4,4,32,128]{4,3,2,1,0:T(8,128)S(1)} %get-tuple-element.32.ep, f32[3,4,4,16,128]{4,3,2,1,0:T(8,128)S(1)} %get-tuple-element.37.part, f32[232,128]{1,0:T(8,128)S(1)} %collective-permute-done.10.t_above, ...), custom_call_target="tpu_custom_call" | custom-call | tf_op jit(solution)/shard_map/pallas_call | solution.py:274
  41.5 0.9 %shard_map.24 = f32[3,4,4,16,128]{4,3,2,1,0:T(8,128)} custom-call(f32[4,4,16,128]{3,2,1,0:T(8,128)S(1)} %get-tuple-element.34.gauge, f32[4,4,2,128]{3,2,1,0:T(2,128)S(1)} %collective-permute-done.14.nx, f32[4,4,8,128]{3,2,1,0:T(8,128)S(1)} %collective-permute-done.15.ny, f32[3,4,4,16,128]{4,3,2,1,0:T(8,128)S(1)} %shard_map.23.links), custom_call_target="tpu_custom_call" | custom-call | tf_op jit(solution)/shard_map/pallas_call | solution.py:274
  (39 shorter events, 1.4 us)
Async XLA Ops:
  0.0 1.0 %copy-start = (f32[4,4,4,8,2,128]{5,4,3,2,1,0:T(2,128)S(1)}, f32[4,4,4,8,2,128]{5,4,3,2,1,0:T(2,128)}, u32[]{:S(2)}) copy-start(f32[4,4,4,8,2,128]{5,4,3,2,1,0:T(2,128)} %param.1) | copy-start | bytes 1572868
  1.1 9.9 %collective-permute-start.1 = (f32[7,4,4,2,128]{4,3,2,1,0:T(2,128)S(1)}, f32[7,4,4,2,128]{4,3,2,1,0:T(2,128)S(1)}, u32[]{:S(2)}, u32[]{:S(2)}) collective-permute-start(f32[7,4,4,2,128]{4,3,2,1,0:T(2,128)S(1)} %get-tuple-element.22), channel_id=1, source_target_pairs={{0,2},{2,0},{1,3},{3,1},{4,6},{6,4},{5,7},{7,5},{8,10},{10,8},{9,1... | collective-permute-start | bytes 344072 | tf_op jit(solution)/shard_map/ppermute | solution.py:286
  4.1 6.8 %collective-permute-start.4 = (f32[3,4,16,128]{3,2,1,0:T(8,128)S(1)}, f32[3,4,16,128]{3,2,1,0:T(8,128)S(1)}, u32[]{:S(2)}, u32[]{:S(2)}) collective-permute-start(f32[3,4,16,128]{3,2,1,0:T(8,128)S(1)} %get-tuple-element.27), channel_id=1, source_target_pairs={{0,12},{4,0},{8,4},{12,8},{1,13},{5,1},{9,5},{13,9},{2,14},{6,2},{... | collective-permute-start | bytes 294920 | tf_op jit(solution)/shard_map/ppermute | solution.py:286
  7.7 6.8 %collective-permute-start.3 = (f32[4,4,16,128]{3,2,1,0:T(8,128)S(1)}, f32[4,4,16,128]{3,2,1,0:T(8,128)S(1)}, u32[]{:S(2)}, u32[]{:S(2)}) collective-permute-start(f32[4,4,16,128]{3,2,1,0:T(8,128)S(1)} %get-tuple-element.26), channel_id=1, source_target_pairs={{0,4},{4,8},{8,12},{12,0},{1,5},{5,9},{9,13},{13,1},{2,6},{6,10},{... | collective-permute-start | bytes 393224 | tf_op jit(solution)/shard_map/ppermute | solution.py:286
  7.7 7.5 %collective-permute-start = (f32[4,4,4,16,128]{4,3,2,1,0:T(8,128)S(1)}, f32[4,4,4,16,128]{4,3,2,1,0:T(8,128)S(1)}, u32[]{:S(2)}, u32[]{:S(2)}) collective-permute-start(f32[4,4,4,16,128]{4,3,2,1,0:T(8,128)S(1)} %bitcast.7), channel_id=1, source_target_pairs={{0,1},{1,0},{2,3},{3,2},{4,5},{5,4},{6,7},{7,6},{8,9},{9,8},{10,11... | collective-permute-start | bytes 1572872 | tf_op jit(solution)/shard_map/ppermute | solution.py:286
  11.0 4.2 %collective-permute-start.2 = (f32[3,4,4,2,128]{4,3,2,1,0:T(2,128)S(1)}, f32[3,4,4,2,128]{4,3,2,1,0:T(2,128)S(1)}, u32[]{:S(2)}, u32[]{:S(2)}) collective-permute-start(f32[3,4,4,2,128]{4,3,2,1,0:T(2,128)S(1)} %pad_maximum_fusion.1), channel_id=1, source_target_pairs={{0,1},{1,0},{2,3},{3,2},{4,5},{5,4},{6,7},{7,6},{8,9},{9,8},{10,11... | collective-permute-start | bytes 147464 | tf_op jit(solution)/shard_map/ppermute | solution.py:286
  14.5 3.9 %collective-permute-start.5 = (f32[3,4,16,128]{3,2,1,0:T(8,128)S(1)}, f32[3,4,16,128]{3,2,1,0:T(8,128)S(1)}, u32[]{:S(2)}, u32[]{:S(2)}) collective-permute-start(f32[3,4,16,128]{3,2,1,0:T(8,128)S(1)} %pad_maximum_fusion), channel_id=1, source_target_pairs={{0,1},{1,0},{2,3},{3,2},{4,5},{5,4},{6,7},{7,6},{8,9},{9,8},{10,11... | collective-permute-start | bytes 294920 | tf_op jit(solution)/shard_map/ppermute | solution.py:286
  14.6 3.8 %collective-permute-start.6 = (f32[4,4,2,128]{3,2,1,0:T(2,128)S(1)}, f32[4,4,2,128]{3,2,1,0:T(2,128)S(1)}, u32[]{:S(2)}, u32[]{:S(2)}) collective-permute-start(f32[4,4,2,128]{3,2,1,0:T(2,128)S(1)} %pad_maximum_fusion.3), channel_id=1, source_target_pairs={{0,2},{2,0},{1,3},{3,1},{4,6},{6,4},{5,7},{7,5},{8,10},{10,8},{9,1... | collective-permute-start | bytes 49160 | tf_op jit(solution)/shard_map/ppermute | solution.py:286
  19.5 7.0 %collective-permute-start.7 = (f32[4,4,4,16,128]{4,3,2,1,0:T(8,128)S(1)}, f32[4,4,4,16,128]{4,3,2,1,0:T(8,128)S(1)}, u32[]{:S(2)}, u32[]{:S(2)}) collective-permute-start(f32[4,4,4,16,128]{4,3,2,1,0:T(8,128)S(1)} %get-tuple-element.28.own), channel_id=1, source_target_pairs={{0,1},{1,0},{2,3},{3,2},{4,5},{5,4},{6,7},{7,6},{8,9},{9,8},{10,11... | collective-permute-start | bytes 1572872 | tf_op jit(solution)/shard_map/ppermute | solution.py:286
  19.6 5.6 %collective-permute-start.8 = (f32[7,4,4,2,128]{4,3,2,1,0:T(2,128)S(1)}, f32[7,4,4,2,128]{4,3,2,1,0:T(2,128)S(1)}, u32[]{:S(2)}, u32[]{:S(2)}) collective-permute-start(f32[7,4,4,2,128]{4,3,2,1,0:T(2,128)S(1)} %get-tuple-element.29), channel_id=1, source_target_pairs={{0,2},{2,0},{1,3},{3,1},{4,6},{6,4},{5,7},{7,5},{8,10},{10,8},{9,1... | collective-permute-start | bytes 344072 | tf_op jit(solution)/shard_map/ppermute | solution.py:286
  20.2 13.6 %collective-permute-start.16 = (f32[4,4,16,128]{3,2,1,0:T(8,128)S(1)}, f32[4,4,16,128]{3,2,1,0:T(8,128)S(1)}, u32[]{:S(2)}, u32[]{:S(2)}) collective-permute-start(f32[4,4,16,128]{3,2,1,0:T(8,128)S(1)} %get-tuple-element.38), channel_id=1, source_target_pairs={{0,4},{4,8},{8,12},{12,0},{1,5},{5,9},{9,13},{13,1},{2,6},{6,10},{... | collective-permute-start | bytes 393224 | tf_op jit(solution)/shard_map/ppermute | solution.py:286
  20.6 7.8 %collective-permute-start.10 = (f32[232,128]{1,0:T(8,128)S(1)}, f32[232,128]{1,0:T(8,128)S(1)}, u32[]{:S(2)}, u32[]{:S(2)}) collective-permute-start(f32[232,128]{1,0:T(8,128)S(1)} %get-tuple-element.33), channel_id=1, source_target_pairs={{0,12},{4,0},{8,4},{12,8},{1,13},{5,1},{9,5},{13,9},{2,14},{6,2},{... | collective-permute-start | bytes 356360 | tf_op jit(solution)/shard_map/ppermute | solution.py:286
  25.2 1.3 %collective-permute-start.9 = (f32[3,4,4,2,128]{4,3,2,1,0:T(2,128)S(1)}, f32[3,4,4,2,128]{4,3,2,1,0:T(2,128)S(1)}, u32[]{:S(2)}, u32[]{:S(2)}) collective-permute-start(f32[3,4,4,2,128]{4,3,2,1,0:T(2,128)S(1)} %pad_maximum_fusion.2), channel_id=1, source_target_pairs={{0,1},{1,0},{2,3},{3,2},{4,5},{5,4},{6,7},{7,6},{8,9},{9,8},{10,11... | collective-permute-start | bytes 147464 | tf_op jit(solution)/shard_map/ppermute | solution.py:286
  28.5 6.0 %collective-permute-start.11 = (f32[4,16,128]{2,1,0:T(8,128)S(1)}, f32[4,16,128]{2,1,0:T(8,128)S(1)}, u32[]{:S(2)}, u32[]{:S(2)}) collective-permute-start(f32[4,16,128]{2,1,0:T(8,128)S(1)} %shard_map.21), channel_id=1, source_target_pairs={{0,4},{4,8},{8,12},{12,0},{1,5},{5,9},{9,13},{13,1},{2,6},{6,10},{... | collective-permute-start | bytes 98312 | tf_op jit(solution)/shard_map/ppermute | solution.py:286
  28.8 5.7 %collective-permute-start.12 = (f32[4,16,128]{2,1,0:T(8,128)S(1)}, f32[4,16,128]{2,1,0:T(8,128)S(1)}, u32[]{:S(2)}, u32[]{:S(2)}) collective-permute-start(f32[4,16,128]{2,1,0:T(8,128)S(1)} %shard_map.21), channel_id=1, source_target_pairs={{0,8},{4,12},{8,0},{12,4},{1,9},{5,13},{9,1},{13,5},{2,10},{6,14},... | collective-permute-start | bytes 98312 | tf_op jit(solution)/shard_map/ppermute | solution.py:286
  31.6 3.9 %collective-permute-start.13 = (f32[4,16,128]{2,1,0:T(8,128)S(1)}, f32[4,16,128]{2,1,0:T(8,128)S(1)}, u32[]{:S(2)}, u32[]{:S(2)}) collective-permute-start(f32[4,16,128]{2,1,0:T(8,128)S(1)} %shard_map.21), channel_id=1, source_target_pairs={{0,12},{4,0},{8,4},{12,8},{1,13},{5,1},{9,5},{13,9},{2,14},{6,2},{... | collective-permute-start | bytes 98312 | tf_op jit(solution)/shard_map/ppermute | solution.py:286
  33.9 7.0 %collective-permute-start.17 = (f32[4,16,128]{2,1,0:T(8,128)S(1)}, f32[4,16,128]{2,1,0:T(8,128)S(1)}, u32[]{:S(2)}, u32[]{:S(2)}) collective-permute-start(f32[4,16,128]{2,1,0:T(8,128)S(1)} %slice_bitcast_fusion), channel_id=1, source_target_pairs={{0,1},{1,0},{2,3},{3,2},{4,5},{5,4},{6,7},{7,6},{8,9},{9,8},{10,11... | collective-permute-start | bytes 98312 | tf_op jit(solution)/shard_map/ppermute | solution.py:286
  35.6 5.9 %collective-permute-start.15 = (f32[4,4,8,128]{3,2,1,0:T(8,128)S(1)}, f32[4,4,8,128]{3,2,1,0:T(8,128)S(1)}, u32[]{:S(2)}, u32[]{:S(2)}) collective-permute-start(f32[4,4,8,128]{3,2,1,0:T(8,128)S(1)} %get-tuple-element.36), channel_id=1, source_target_pairs={{0,1},{1,0},{2,3},{3,2},{4,5},{5,4},{6,7},{7,6},{8,9},{9,8},{10,11... | collective-permute-start | bytes 196616 | tf_op jit(solution)/shard_map/ppermute | solution.py:286
  35.7 5.8 %collective-permute-start.14 = (f32[4,4,2,128]{3,2,1,0:T(2,128)S(1)}, f32[4,4,2,128]{3,2,1,0:T(2,128)S(1)}, u32[]{:S(2)}, u32[]{:S(2)}) collective-permute-start(f32[4,4,2,128]{3,2,1,0:T(2,128)S(1)} %get-tuple-element.35), channel_id=1, source_target_pairs={{0,2},{2,0},{1,3},{3,1},{4,6},{6,4},{5,7},{7,5},{8,10},{10,8},{9,1... | collective-permute-start | bytes 49160 | tf_op jit(solution)/shard_map/ppermute | solution.py:286
  37.2 3.6 %collective-permute-start.18 = (f32[4,2,128]{2,1,0:T(2,128)S(1)}, f32[4,2,128]{2,1,0:T(2,128)S(1)}, u32[]{:S(2)}, u32[]{:S(2)}) collective-permute-start(f32[4,2,128]{2,1,0:T(2,128)S(1)} %slice_bitcast_fusion.1), channel_id=1, source_target_pairs={{0,2},{2,0},{1,3},{3,1},{4,6},{6,4},{5,7},{7,5},{8,10},{10,8},{9,1... | collective-permute-start | bytes 12296 | tf_op jit(solution)/shard_map/ppermute | solution.py:286

commit v3 on v2

v3 whole, which is shorter than its diff:
```python
import jax
import jax.numpy as jnp
from jax import lax
from jax.experimental import pallas as pl
from jax.experimental.pallas import tpu as pltpu
from jax.sharding import PartitionSpec as P

smear_weight = 0.1
LONG = 20_000_000_000
VMEM = pl.BlockSpec(memory_space=pltpu.VMEM)
F32 = jnp.float32
BASE = 8


def mul(a, b):
    return (
        a[0] * b[0] - a[1] * b[1] - a[2] * b[2] - a[3] * b[3],
        a[0] * b[1] + a[1] * b[0] + a[2] * b[3] - a[3] * b[2],
        a[0] * b[2] - a[1] * b[3] + a[2] * b[0] + a[3] * b[1],
        a[0] * b[3] + a[1] * b[2] - a[2] * b[1] + a[3] * b[0],
    )


def mul_cr(a, b):
    return (
        a[0] * b[0] + a[1] * b[1] + a[2] * b[2] + a[3] * b[3],
        a[1] * b[0] - a[0] * b[1] - a[2] * b[3] + a[3] * b[2],
        a[2] * b[0] - a[0] * b[2] + a[1] * b[3] - a[3] * b[1],
        a[3] * b[0] - a[0] * b[3] - a[1] * b[2] + a[2] * b[1],
    )


def mul_cl(a, b):
    return (
        a[0] * b[0] + a[1] * b[1] + a[2] * b[2] + a[3] * b[3],
        a[0] * b[1] - a[1] * b[0] - a[2] * b[3] + a[3] * b[2],
        a[0] * b[2] + a[1] * b[3] - a[2] * b[0] - a[3] * b[1],
        a[0] * b[3] - a[1] * b[2] + a[2] * b[1] - a[3] * b[0],
    )


def add(a, b):
    return tuple(x + y for x, y in zip(a, b))


def zroll(a, amount):
    return tuple(pltpu.roll(x, amount % 128, 1) for x in a)


def accessor(eo, ep, low, high):
    tl = eo.shape[2]
    cache = {}

    def ld(d, t, x, y, z=0):
        key = (d, t, x, y, z)
        if key not in cache:
            if z:
                cache[key] = zroll(ld(d, t, x, y), -z)
            else:
                mine = 0 <= y < 2
                rows = pl.ds(BASE + 2 * x + y % 2, 8, stride=2)
                if 0 <= t < tl:
                    ref = eo if mine else ep
                    cache[key] = tuple(ref[d, c, t, rows, :] for c in range(4))
                else:
                    ref = (low if t < 0 else high)[0 if mine else 1]
                    cache[key] = tuple(ref[d, c, rows, :] for c in range(4))
        return cache[key]

    return ld


def moved(s, d, k=1):
    return tuple(v + k if i == d else v for i, v in enumerate(s))


def lower(ld, m, n, s):
    b = moved(s, n, -1)
    return mul(mul_cl(ld(n, *b), ld(m, *b)), ld(n, *moved(b, m)))


def unit(q):
    norm = q[0] * q[0] + q[1] * q[1] + q[2] * q[2] + q[3] * q[3]
    inv = lax.rsqrt(norm)
    return tuple(v * inv for v in q)


def scaled_add(a, b):
    return tuple(h + smear_weight * w for h, w in zip(a, b))


def combined(ld, m, s, leave=None):
    total = None
    here = ld(m, *s)
    for n in range(4):
        if n == m:
            continue
        u = mul_cr(mul(ld(n, *s), ld(m, *moved(s, n))), ld(n, *moved(s, m)))
        total = u if total is None else add(total, u)
        if n == 3:
            v = zroll(mul(mul_cl(ld(n, *s), here), ld(n, *moved(s, m))), 1)
            total = add(total, v)
        elif n != leave:
            total = add(total, lower(ld, m, n, s))
    return scaled_add(here, total)


def smear_link(ld, m, s):
    return unit(combined(ld, m, s))


def fill(own, par, xh, x_shared, eo, ep):
    for d in range(4):
        eo[d, :, :, BASE : BASE + 16, :] = own[d]
        ep[d, :, :, BASE : BASE + 16, :] = par[d]
        eo[d, :, :, BASE - 2 : BASE, :] = xh[3 + d]
    for slot, d in enumerate((0, 2, 3)):
        eo[d, :, :, BASE + 16 : BASE + 18, :] = xh[slot]
    if x_shared is not None:
        ep[2, :, :, BASE + 16 : BASE + 18, :] = x_shared[0]
        ep[1, :, :, BASE - 2 : BASE, :] = x_shared[1]
        if x_shared.shape[0] > 2:
            ep[2, :, :, BASE - 2 : BASE, :] = x_shared[2]


def interior_1(own, par, xh, x_shared, eo, ep, new):
    tl = own.shape[2]
    fill(own, par, xh, x_shared, eo, ep)
    for t in range(1, tl - 1):
        for y in range(2):
            ld = accessor(eo, ep, None, None)
            for d in range(4):
                q = smear_link(ld, d, (t, 0, y, 0))
                for c in range(4):
                    new[d, c, t, pl.ds(y, 8, stride=2), :] = q[c]


MAIN = slice(BASE, BASE + 16)
BEFORE = slice(BASE - 2, BASE)
AFTER = slice(BASE + 16, BASE + 18)


def first_1(eo, ep, t_below, t_shared, corner, t_dn, first, lo, lp):
    lo[:, :, MAIN, :] = t_below[...]
    lo[0, :, AFTER, :] = corner[0]
    lo[0:2, :, BEFORE, :] = corner[2:4]
    lp[0, :, MAIN, :] = t_shared[0]
    lp[2, :, MAIN, :] = t_shared[1]
    for y in range(2):
        ld = accessor(eo, ep, (lo, lp), None)
        for d in range(4):
            q = smear_link(ld, d, (0, 0, y, 0))
            for c in range(4):
                first[d, c, pl.ds(y, 8, stride=2), :] = q[c]
        q = smear_link(accessor(eo, ep, (lo, lp), None), 1, (0, -1, y, 0))
        for c in range(4):
            t_dn[224 + 2 * c + y : 225 + 2 * c + y, :] = q[c][0:1]
    q = smear_link(accessor(eo, ep, (lo, lp), None), 2, (0, 0, -1, 0))
    for c in range(4):
        t_dn[192 + 8 * c : 200 + 8 * c, :] = q[c]
    for d in range(3):
        for c in range(4):
            t_dn[64 * d + 16 * c : 64 * d + 16 * c + 16, :] = first[d + 1, c]


def rest_1(eo, ep, part, first, t_above, t_shared, corner, new, xs, ho, hp):
    tl = eo.shape[2]
    ho[1:4, :, MAIN, :] = t_above[...]
    ho[1, :, BEFORE, :] = corner[1]
    hp[2, :, MAIN, :] = t_shared[2]
    new[:, :, 0] = first[...]
    for t in range(1, tl - 1):
        new[:, :, t] = part[:, :, t]
    t = tl - 1
    for y in range(2):
        ld = accessor(eo, ep, None, (ho, hp))
        for d in range(4):
            q = smear_link(ld, d, (t, 0, y, 0))
            for c in range(4):
                new[d, c, t, pl.ds(y, 8, stride=2), :] = q[c]
    for slot, d in enumerate((0, 2, 3)):
        xs[slot] = new[d, :, :, 0:2, :]
    for d in range(4):
        xs[3 + d] = new[d, :, :, 14:16, :]


def pack_1(t_below, t_above, edges, shared):
    edges[0] = t_below[0, :, 0:2, :]
    edges[1] = t_above[0, :, 14:16, :]
    edges[2:4] = t_below[0:2, :, 14:16, :]
    shared[0] = t_below[0]
    shared[1] = t_below[2]
    shared[2] = t_above[1]


def unpack_above(t_above, ho):
    for d in range(3):
        for c in range(4):
            ho[d + 1, c, MAIN, :] = t_above[64 * d + 16 * c : 64 * d + 16 * c + 16, :]


def above_2(t_above, ho, hp):
    unpack_above(t_above, ho)
    for c in range(4):
        hp[2, c, pl.ds(BASE + 1, 8, stride=2), :] = t_above[192 + 8 * c : 200 + 8 * c, :]
        ho[1, c, BEFORE, :] = t_above[224 + 2 * c : 226 + 2 * c, :]


def temporal_2(own, par, xh, ho, hp, prefix, slab, eo, ep):
    tl = own.shape[2]
    fill(own, par, xh, None, eo, ep)
    for y in range(2):
        rows = pl.ds(y, 8, stride=2)
        one = jnp.ones((8, 128), F32)
        zero = jnp.zeros((8, 128), F32)
        state = (one, zero, zero, zero)
        for t in range(tl):
            for c in range(4):
                prefix[c, t, rows, :] = state[c]
            q = smear_link(accessor(eo, ep, None, (ho, hp)), 0, (t, 0, y, 0))
            state = q if t == 0 else mul(state, q)
        for c in range(4):
            slab[c, rows, :] = state[c]


def spatial_2(own, par, xh, x_shared, t_above, new, lows, eo, ep, ho):
    tl = own.shape[2]
    fill(own, par, xh, x_shared, eo, ep)
    unpack_above(t_above, ho)
    for t in range(tl):
        for y in range(2):
            ld = accessor(eo, ep, None, (ho, None))
            for d in range(1, 4):
                s = (t, 0, y, 0)
                q = combined(ld, d, s, leave=0) if t == 0 else smear_link(ld, d, s)
                for c in range(4):
                    new[d - 1, c, t, pl.ds(y, 8, stride=2), :] = q[c]
    for y in range(2):
        rows = pl.ds(y, 8, stride=2)
        ld = accessor(eo, ep, None, None)
        for d in range(1, 4):
            s = moved((tl - 1, 0, y, 0), 0)
            q = lower(ld, d, 0, s)
            for c in range(4):
                lows[d - 1, c, rows, :] = q[c]


def carry_kernel(n, prefix, slab_list, ready, gauge, gx, gy):
    tl = prefix.shape[1]
    place = lax.axis_index("tm")
    for half in range(2):
        rows = pl.ds(half * 8, 8)
        state = None
        for j in reversed(range(n - 1)):
            q = tuple(slab_list[j][c, rows, :] for c in range(4))
            there = place >= j + 1
            q = tuple(jnp.where(there, v, 1.0 if c == 0 else 0.0) for c, v in enumerate(q))
            state = q if state is None else mul(state, q)
        for t in range(tl):
            g = mul(state, tuple(prefix[c, t, rows, :] for c in range(4)))
            for c in range(4):
                gauge[c, t, rows, :] = g[c]
    gx[...] = gauge[:, :, 0:2, :]
    for c in range(4):
        for t in range(tl):
            gy[c, t] = gauge[c, t, pl.ds(0, 8, stride=2), :]


def rotate_kernel(gauge, nx, ny, links, lows, out, ext):
    tl = gauge.shape[1]
    ext[:, :, 0:16, :] = gauge[...]
    ext[:, :, 16:18, :] = nx[...]
    for t in range(tl):
        for y in range(2):
            rows = pl.ds(y, 8, stride=2)
            g = tuple(gauge[c, t, rows, :] for c in range(4))
            g1 = tuple(ext[c, t, pl.ds(2 + y, 8, stride=2), :] for c in range(4))
            if y == 0:
                g2 = tuple(gauge[c, t, pl.ds(1, 8, stride=2), :] for c in range(4))
            else:
                g2 = tuple(ny[c, t] for c in range(4))
            for d, other in enumerate((g1, g2, zroll(g, -1))):
                u = tuple(links[d, c, t, rows, :] for c in range(4))
                if t == 0:
                    u = unit(scaled_add(u, tuple(lows[d, c, rows, :] for c in range(4))))
                r = mul_cr(mul(g, u), other)
                for c in range(4):
                    out[d, c, t, rows, :] = r[c]


def boundary(links, t_up, t_dn, xs, copy):
    tl = links.shape[2]
    copy[...] = links[...]
    t_up[...] = links[:, :, tl - 1]
    t_dn[...] = links[1:4, :, 0]
    for slot, d in enumerate((0, 2, 3)):
        xs[slot] = links[d, :, :, 0:2, :]
    for d in range(4):
        xs[3 + d] = links[d, :, :, 14:16, :]


def call(kernel, outs, scratch, *args, weight=1):
    single = isinstance(outs[0], int)
    shapes = [jax.ShapeDtypeStruct(s, F32) for s in ([outs] if single else outs)]
    return pl.pallas_call(
        kernel,
        out_shape=shapes[0] if single else shapes,
        in_specs=[VMEM] * len(args),
        out_specs=VMEM if single else [VMEM] * len(shapes),
        scratch_shapes=[pltpu.VMEM(s, F32) for s in scratch],
        cost_estimate=pl.CostEstimate(flops=weight, bytes_accessed=1, transcendentals=0),
        compiler_params=pltpu.CompilerParams(vmem_limit_bytes=40 * 2**20),
    )(*args)


def rotated_by(x, axis, steps):
    n = lax.axis_size(axis)
    return lax.ppermute(x, axis, [(i, (i + steps) % n) for i in range(n)])


def x_exchange(xs, cut):
    if lax.axis_size("space") == 2:
        return rotated_by(xs, "space", 1)
    return jnp.concatenate(
        [rotated_by(xs[:cut], "space", -1), rotated_by(xs[cut:], "space", 1)]
    )


def to_rows(parts):
    return jnp.concatenate([p.reshape(-1, p.shape[-1]) for p in parts])


def after(value, other):
    return lax.optimization_barrier((value, other))[0]


def on_device(link_field):
    tl, xl, yl, z = link_field.shape[2:]
    rows = xl * yl
    links = link_field.reshape(4, 4, tl, rows, z)
    block = (4, 4, tl, rows, z)
    ext = (4, 4, tl, 32, z)
    layer = (4, 4, 32, z)
    t_up, t_dn, xs, links = call(
        boundary, [(4, 4, rows, z), (3, 4, rows, z), (7, 4, tl, 2, z), block], [], links
    )
    t_below = rotated_by(t_up, "tm", 1)
    t_above = rotated_by(t_dn, "tm", -1)
    xh = x_exchange(xs, 3)
    par = rotated_by(links, "pair", 1)
    edges, shared = call(
        pack_1, [(4, 4, yl, z), (3, 4, rows, z)], [], t_below, t_above, weight=LONG
    )
    corner = x_exchange(edges, 1)
    t_shared = rotated_by(shared, "pair", 1)
    x_shared = rotated_by(jnp.stack([xh[1], xh[4], xh[5]]), "pair", 1)
    eo, ep, part = call(interior_1, [ext, ext, block], [], links, par, xh, x_shared)
    t_dn, first = call(
        first_1, [(232, z), (4, 4, rows, z)], [layer] * 2, eo, ep, t_below, t_shared, corner
    )
    links, xs = call(
        rest_1,
        [block, (7, 4, tl, 2, z)],
        [layer] * 2,
        eo,
        ep,
        part,
        first,
        t_above,
        t_shared,
        corner,
    )
    t_above = rotated_by(t_dn, "tm", -1)
    xh = x_exchange(xs, 3)
    par = rotated_by(links, "pair", 1)
    layers = call(above_2, [layer, layer], [], t_above, weight=LONG)
    prefix, slab = call(
        temporal_2,
        [(4, tl, rows, z), (4, rows, z)],
        [ext, ext],
        links,
        par,
        xh,
        *layers,
    )
    n = lax.axis_size("tm")
    slabs = [rotated_by(slab, "tm", k) for k in range(1, n)]
    x_shared = rotated_by(after(jnp.stack([xh[1], xh[4]]), slab), "pair", 1)
    spatial = (3, 4, tl, rows, z)
    smeared, lows = call(
        spatial_2,
        [spatial, (3, 4, rows, z)],
        [ext, ext, layer],
        links,
        par,
        xh,
        x_shared,
        t_above,
    )
    lows = rotated_by(lows, "tm", 1)
    gauge, gx, gy = call(
        lambda p, *rest: carry_kernel(n, p, rest[: n - 1], *rest[n - 1 :]),
        [(4, tl, rows, z), (4, tl, 2, z), (4, tl, xl, z)],
        [],
        prefix,
        *slabs,
        smeared,
    )
    nx = rotated_by(gx, "space", -1)
    ny = rotated_by(gy, "pair", -1)
    out = call(
        rotate_kernel, spatial, [(4, tl, 24, z)], gauge, nx, ny, smeared, lows
    )
    return out.reshape(3, 4, tl, xl, yl, z)


def solution(mesh):
    spec = P(None, None, "tm", "space", "pair", "groups")
    return jax.shard_map(on_device, mesh=mesh, in_specs=(spec,), out_specs=spec, check_vma=False)
```

time: 42.6 us -> 38.4 us (0.901)
  waiting for transfers between devices: 16.7 us -> 12 us
  starting transfers between devices: 19.4 us -> 20 us
    ppermute x19 -> x17, waiting for transfers between devices: 16.7 us -> 12 us  [rotated_by(): return lax.ppermute(x, axis, [(i, (i + steps) % n) for i in range(n)])]
    ppermute x19 -> x17, starting transfers between devices: 19.4 us -> 20 us  [rotated_by(): return lax.ppermute(x, axis, [(i, (i + steps) % n) for i in range(n)])]
    pallas_call x8 -> x10, Pallas kernels: 4.97 us -> 5.01 us  [call(): pl.pallas_call(kernel, out_shape=shapes[0] if single else shapes, in_spec...]
  transfers between devices with their start and end apart: 19 -> 17, of which waited for: 9 -> 7; matrix products, arithmetic and copies ran while one was open for 0% -> 0% of each run, Pallas kernels for 7% -> 6%
where the time goes in v3:
time: 38.4 us; the launch traced here: 38.2 us
  starting transfers between devices  20 us (52%)
  waiting for transfers between devices  12 us (31%)
  Pallas kernels  5.01 us (13%)
  local copies, waits for them, and re-layouts  1.05 us (3%)
    ppermute x17, starting transfers between devices, rotated_by(): return lax.ppermute(x, axis, [(i, (i + steps) % n) for i in range(n)])  20 us
    ppermute x17, waiting for transfers between devices, rotated_by(): return lax.ppermute(x, axis, [(i, (i + steps) % n) for i in range(n)])  12 us
    pallas_call x10, Pallas kernels, call(): pl.pallas_call(kernel, out_shape=shapes[0] if single else shapes, in_spec...  5.01 us
    unnamed x2, local copies, waits for them, and re-layouts  1.04 us
  transfers between devices with their start and end apart: 17, of which 7 were waited for; matrix products, arithmetic and copies ran while one was open for 0% of the time, Pallas kernels for 6%

profile of v3, /device:TPU:0, one launch (start us, length us, event | category | flops | bytes accessed | tf_op | source)
XLA Modules:
  0.0 38.2 jit_solution(16632560228706695335)
XLA Ops:
  0.0 1.0 %copy-done = f32[4,4,4,8,2,128]{5,4,3,2,1,0:T(2,128)S(1)} copy-done((f32[4,4,4,8,2,128]{5,4,3,2,1,0:T(2,128)S(1)}, f32[4,4,4,8,2,128]{5,4,3,2,1,0:T(2,128)}, u32[]{:S(2)}) %copy-start) | copy-done | bytes 524312
  1.1 3.1 %collective-permute-start.3 = (f32[4,4,16,128]{3,2,1,0:T(8,128)S(1)}, f32[4,4,16,128]{3,2,1,0:T(8,128)S(1)}, u32[]{:S(2)}, u32[]{:S(2)}) collective-permute-start(f32[4,4,16,128]{3,2,1,0:T(8,128)S(1)} %get-tuple-element.33), channel_id=1, source_target_pairs={{0,4},{4,8},{8,12},{12,0},{1,5},{5,9},{9,13},{13,1},{2,6},{6,10},{... | collective-permute-start | bytes 393224 | tf_op jit(solution)/shard_map/ppermute | solution.py:318
  4.2 1.5 %collective-permute-start.1 = (f32[7,4,4,2,128]{4,3,2,1,0:T(2,128)S(1)}, f32[7,4,4,2,128]{4,3,2,1,0:T(2,128)S(1)}, u32[]{:S(2)}, u32[]{:S(2)}) collective-permute-start(f32[7,4,4,2,128]{4,3,2,1,0:T(2,128)S(1)} %get-tuple-element.29), channel_id=1, source_target_pairs={{0,2},{2,0},{1,3},{3,1},{4,6},{6,4},{5,7},{7,5},{8,10},{10,8},{9,1... | collective-permute-start | bytes 344072 | tf_op jit(solution)/shard_map/ppermute | solution.py:318
  5.7 2.2 %collective-permute-start.4 = (f32[3,4,16,128]{3,2,1,0:T(8,128)S(1)}, f32[3,4,16,128]{3,2,1,0:T(8,128)S(1)}, u32[]{:S(2)}, u32[]{:S(2)}) collective-permute-start(f32[3,4,16,128]{3,2,1,0:T(8,128)S(1)} %get-tuple-element.34), channel_id=1, source_target_pairs={{0,12},{4,0},{8,4},{12,8},{1,13},{5,1},{9,5},{13,9},{2,14},{6,2},{... | collective-permute-start | bytes 294920 | tf_op jit(solution)/shard_map/ppermute | solution.py:318
  7.9 1.0 %collective-permute-done.1.xh = f32[7,4,4,2,128]{4,3,2,1,0:T(2,128)S(1)} collective-permute-done((f32[7,4,4,2,128]{4,3,2,1,0:T(2,128)S(1)}, f32[7,4,4,2,128]{4,3,2,1,0:T(2,128)S(1)}, u32[]{:S(2)}, u32[]{:S(2)}) %collective-permute-start.1) | collective-permute-done | bytes 114720 | tf_op jit(solution)/shard_map/ppermute | solution.py:318
  9.0 2.8 %collective-permute-done.4.t_above = f32[3,4,16,128]{3,2,1,0:T(8,128)S(1)} collective-permute-done((f32[3,4,16,128]{3,2,1,0:T(8,128)S(1)}, f32[3,4,16,128]{3,2,1,0:T(8,128)S(1)}, u32[]{:S(2)}, u32[]{:S(2)}) %collective-permute-start.4) | collective-permute-done | bytes 98336 | tf_op jit(solution)/shard_map/ppermute | solution.py:318
  12.0 0.6 %collective-permute-start.2 = (f32[3,4,4,2,128]{4,3,2,1,0:T(2,128)S(1)}, f32[3,4,4,2,128]{4,3,2,1,0:T(2,128)S(1)}, u32[]{:S(2)}, u32[]{:S(2)}) collective-permute-start(f32[3,4,4,2,128]{4,3,2,1,0:T(2,128)S(1)} %pad_maximum_fusion), channel_id=1, source_target_pairs={{0,1},{1,0},{2,3},{3,2},{4,5},{5,4},{6,7},{7,6},{8,9},{9,8},{10,11... | collective-permute-start | bytes 147464 | tf_op jit(solution)/shard_map/ppermute | solution.py:318
  12.5 1.2 %collective-permute-start.6 = (f32[4,4,2,128]{3,2,1,0:T(2,128)S(1)}, f32[4,4,2,128]{3,2,1,0:T(2,128)S(1)}, u32[]{:S(2)}, u32[]{:S(2)}) collective-permute-start(f32[4,4,2,128]{3,2,1,0:T(2,128)S(1)} %get-tuple-element.36), channel_id=1, source_target_pairs={{0,2},{2,0},{1,3},{3,1},{4,6},{6,4},{5,7},{7,5},{8,10},{10,8},{9,1... | collective-permute-start | bytes 49160 | tf_op jit(solution)/shard_map/ppermute | solution.py:318
  13.7 0.9 %shard_map.18 = (f32[4,4,4,32,128]{4,3,2,1,0:T(8,128)S(1)}, f32[4,4,4,32,128]{4,3,2,1,0:T(8,128)S(1)}, f32[4,4,4,16,128]{4,3,2,1,0:T(8,128)S(1)}) custom-call(f32[4,4,4,16,128]{4,3,2,1,0:T(8,128)S(1)} %get-tuple-element.28.own, f32[4,4,4,16,128]{4,3,2,1,0:T(8,128)S(1)} %collective-permute-done.par, f32[7,4,4,2,128]{4,3,2,1,0:T(2,128)S(1)} %collective-permute-done.1.xh, ...), custom_call_target="tpu_custom_call" | custom-call | flops 1 | bytes 1 | tf_op jit(solution)/shard_map/pallas_call | solution.py:305
  14.6 1.6 %collective-permute-done.6.corner = f32[4,4,2,128]{3,2,1,0:T(2,128)S(1)} collective-permute-done((f32[4,4,2,128]{3,2,1,0:T(2,128)S(1)}, f32[4,4,2,128]{3,2,1,0:T(2,128)S(1)}, u32[]{:S(2)}, u32[]{:S(2)}) %collective-permute-start.6) | collective-permute-done | bytes 16416 | tf_op jit(solution)/shard_map/ppermute | solution.py:318
  16.3 0.6 %shard_map.20 = (f32[232,128]{1,0:T(8,128)S(1)}, f32[4,4,16,128]{3,2,1,0:T(8,128)S(1)}) custom-call(f32[4,4,4,32,128]{4,3,2,1,0:T(8,128)S(1)} %get-tuple-element.30.eo, f32[4,4,4,32,128]{4,3,2,1,0:T(8,128)S(1)} %get-tuple-element.31.ep, f32[4,4,16,128]{3,2,1,0:T(8,128)S(1)} %collective-permute-done.3.t_below, ...), custom_call_target="tpu_custom_call" | custom-call | flops 1 | bytes 1 | tf_op jit(solution)/shard_map/pallas_call | solution.py:305
  17.4 1.2 %collective-permute-start.8 = (f32[7,4,4,2,128]{4,3,2,1,0:T(2,128)S(1)}, f32[7,4,4,2,128]{4,3,2,1,0:T(2,128)S(1)}, u32[]{:S(2)}, u32[]{:S(2)}) collective-permute-start(f32[7,4,4,2,128]{4,3,2,1,0:T(2,128)S(1)} %get-tuple-element.39), channel_id=1, source_target_pairs={{0,2},{2,0},{1,3},{3,1},{4,6},{6,4},{5,7},{7,5},{8,10},{10,8},{9,1... | collective-permute-start | bytes 344072 | tf_op jit(solution)/shard_map/ppermute | solution.py:318
  18.6 2.0 %collective-permute-start.9 = (f32[232,128]{1,0:T(8,128)S(1)}, f32[232,128]{1,0:T(8,128)S(1)}, u32[]{:S(2)}, u32[]{:S(2)}) collective-permute-start(f32[232,128]{1,0:T(8,128)S(1)} %get-tuple-element.40), channel_id=1, source_target_pairs={{0,12},{4,0},{8,4},{12,8},{1,13},{5,1},{9,5},{13,9},{2,14},{6,2},{... | collective-permute-start | bytes 356360 | tf_op jit(solution)/shard_map/ppermute | solution.py:318
  20.7 1.6 %collective-permute-done.8.xh = f32[7,4,4,2,128]{4,3,2,1,0:T(2,128)S(1)} collective-permute-done((f32[7,4,4,2,128]{4,3,2,1,0:T(2,128)S(1)}, f32[7,4,4,2,128]{4,3,2,1,0:T(2,128)S(1)}, u32[]{:S(2)}, u32[]{:S(2)}) %collective-permute-start.8) | collective-permute-done | bytes 114720 | tf_op jit(solution)/shard_map/ppermute | solution.py:318
  22.3 2.0 %collective-permute-done.9.t_above = f32[232,128]{1,0:T(8,128)S(1)} collective-permute-done((f32[232,128]{1,0:T(8,128)S(1)}, f32[232,128]{1,0:T(8,128)S(1)}, u32[]{:S(2)}, u32[]{:S(2)}) %collective-permute-start.9) | collective-permute-done | bytes 118816 | tf_op jit(solution)/shard_map/ppermute | solution.py:318
  24.3 0.5 %shard_map.23 = (f32[4,4,16,128]{3,2,1,0:T(8,128)S(1)}, f32[4,16,128]{2,1,0:T(8,128)S(1)}) custom-call(f32[4,4,4,16,128]{4,3,2,1,0:T(8,128)S(1)} %get-tuple-element.38.own, f32[4,4,4,16,128]{4,3,2,1,0:T(8,128)S(1)} %collective-permute-done.7.par, f32[7,4,4,2,128]{4,3,2,1,0:T(2,128)S(1)} %collective-permute-done.8.xh, ...), custom_call_target="tpu_custom_call" | custom-call | flops 1 | bytes 1 | tf_op jit(solution)/shard_map/pallas_call | solution.py:305
  24.9 0.9 %collective-permute-start.10 = (f32[4,16,128]{2,1,0:T(8,128)S(1)}, f32[4,16,128]{2,1,0:T(8,128)S(1)}, u32[]{:S(2)}, u32[]{:S(2)}) collective-permute-start(f32[4,16,128]{2,1,0:T(8,128)S(1)} %get-tuple-element.44), channel_id=1, source_target_pairs={{0,4},{4,8},{8,12},{12,0},{1,5},{5,9},{9,13},{13,1},{2,6},{6,10},{... | collective-permute-start | bytes 98312 | tf_op jit(solution)/shard_map/ppermute | solution.py:318
  25.9 3.5 %collective-permute-start.11 = (f32[4,16,128]{2,1,0:T(8,128)S(1)}, f32[4,16,128]{2,1,0:T(8,128)S(1)}, u32[]{:S(2)}, u32[]{:S(2)}) collective-permute-start(f32[4,16,128]{2,1,0:T(8,128)S(1)} %get-tuple-element.44), channel_id=1, source_target_pairs={{0,8},{4,12},{8,0},{12,4},{1,9},{5,13},{9,1},{13,5},{2,10},{6,14},... | collective-permute-start | bytes 98312 | tf_op jit(solution)/shard_map/ppermute | solution.py:318
  29.4 1.3 %shard_map.24 = (f32[3,4,4,16,128]{4,3,2,1,0:T(8,128)S(1)}, f32[3,4,16,128]{3,2,1,0:T(8,128)S(1)}) custom-call(f32[4,4,4,16,128]{4,3,2,1,0:T(8,128)S(1)} %get-tuple-element.38.own, f32[4,4,4,16,128]{4,3,2,1,0:T(8,128)S(1)} %collective-permute-done.7.par, f32[7,4,4,2,128]{4,3,2,1,0:T(2,128)S(1)} %collective-permute-done.8.xh, ...), custom_call_target="tpu_custom_call" | custom-call | flops 1 | bytes 1 | tf_op jit(solution)/shard_map/pallas_call | solution.py:305
  30.7 2.1 %collective-permute-start.16 = (f32[3,4,16,128]{3,2,1,0:T(8,128)S(1)}, f32[3,4,16,128]{3,2,1,0:T(8,128)S(1)}, u32[]{:S(2)}, u32[]{:S(2)}) collective-permute-start(f32[3,4,16,128]{3,2,1,0:T(8,128)S(1)} %get-tuple-element.50), channel_id=1, source_target_pairs={{0,4},{4,8},{8,12},{12,0},{1,5},{5,9},{9,13},{13,1},{2,6},{6,10},{... | collective-permute-start | bytes 294920 | tf_op jit(solution)/shard_map/ppermute | solution.py:318
  32.8 0.5 %collective-permute-done.12.rest_2_ = f32[4,16,128]{2,1,0:T(8,128)S(1)} collective-permute-done((f32[4,16,128]{2,1,0:T(8,128)S(1)}, f32[4,16,128]{2,1,0:T(8,128)S(1)}, u32[]{:S(2)}, u32[]{:S(2)}) %collective-permute-start.12) | collective-permute-done | bytes 32800 | tf_op jit(solution)/shard_map/ppermute | solution.py:318
  33.5 1.4 %collective-permute-start.14 = (f32[4,4,2,128]{3,2,1,0:T(2,128)S(1)}, f32[4,4,2,128]{3,2,1,0:T(2,128)S(1)}, u32[]{:S(2)}, u32[]{:S(2)}) collective-permute-start(f32[4,4,2,128]{3,2,1,0:T(2,128)S(1)} %get-tuple-element.48), channel_id=1, source_target_pairs={{0,2},{2,0},{1,3},{3,1},{4,6},{6,4},{5,7},{7,5},{8,10},{10,8},{9,1... | collective-permute-start | bytes 49160 | tf_op jit(solution)/shard_map/ppermute | solution.py:318
  34.9 2.4 %collective-permute-done.14.nx = f32[4,4,2,128]{3,2,1,0:T(2,128)S(1)} collective-permute-done((f32[4,4,2,128]{3,2,1,0:T(2,128)S(1)}, f32[4,4,2,128]{3,2,1,0:T(2,128)S(1)}, u32[]{:S(2)}, u32[]{:S(2)}) %collective-permute-start.14) | collective-permute-done | bytes 16416 | tf_op jit(solution)/shard_map/ppermute | solution.py:318
  37.3 1.0 %shard_map.26 = f32[3,4,4,16,128]{4,3,2,1,0:T(8,128)} custom-call(f32[4,4,16,128]{3,2,1,0:T(8,128)S(1)} %get-tuple-element.47.gauge, f32[4,4,2,128]{3,2,1,0:T(2,128)S(1)} %collective-permute-done.14.nx, f32[4,4,8,128]{3,2,1,0:T(8,128)S(1)} %collective-permute-done.15.ny, f32[3,4,4,16,128]{4,3,2,1,0:T(8,128)S(1)} %get-tuple-element.46.rest_3_.links, ...), custom_call_target="tpu_custom_call" | custom-call | flops 1 | bytes 1 | tf_op jit(solution)/shard_map/pallas_call | solution.py:305
  (27 shorter events, 1.0 us)
Async XLA Ops:
  0.0 1.0 %copy-start = (f32[4,4,4,8,2,128]{5,4,3,2,1,0:T(2,128)S(1)}, f32[4,4,4,8,2,128]{5,4,3,2,1,0:T(2,128)}, u32[]{:S(2)}) copy-start(f32[4,4,4,8,2,128]{5,4,3,2,1,0:T(2,128)} %param.1) | copy-start | bytes 1572868
  1.1 10.7 %collective-permute-start.3 = (f32[4,4,16,128]{3,2,1,0:T(8,128)S(1)}, f32[4,4,16,128]{3,2,1,0:T(8,128)S(1)}, u32[]{:S(2)}, u32[]{:S(2)}) collective-permute-start(f32[4,4,16,128]{3,2,1,0:T(8,128)S(1)} %get-tuple-element.33), channel_id=1, source_target_pairs={{0,4},{4,8},{8,12},{12,0},{1,5},{5,9},{9,13},{13,1},{2,6},{6,10},{... | collective-permute-start | bytes 393224 | tf_op jit(solution)/shard_map/ppermute | solution.py:318
  4.2 4.8 %collective-permute-start.1 = (f32[7,4,4,2,128]{4,3,2,1,0:T(2,128)S(1)}, f32[7,4,4,2,128]{4,3,2,1,0:T(2,128)S(1)}, u32[]{:S(2)}, u32[]{:S(2)}) collective-permute-start(f32[7,4,4,2,128]{4,3,2,1,0:T(2,128)S(1)} %get-tuple-element.29), channel_id=1, source_target_pairs={{0,2},{2,0},{1,3},{3,1},{4,6},{6,4},{5,7},{7,5},{8,10},{10,8},{9,1... | collective-permute-start | bytes 344072 | tf_op jit(solution)/shard_map/ppermute | solution.py:318
  5.7 6.1 %collective-permute-start.4 = (f32[3,4,16,128]{3,2,1,0:T(8,128)S(1)}, f32[3,4,16,128]{3,2,1,0:T(8,128)S(1)}, u32[]{:S(2)}, u32[]{:S(2)}) collective-permute-start(f32[3,4,16,128]{3,2,1,0:T(8,128)S(1)} %get-tuple-element.34), channel_id=1, source_target_pairs={{0,12},{4,0},{8,4},{12,8},{1,13},{5,1},{9,5},{13,9},{2,14},{6,2},{... | collective-permute-start | bytes 294920 | tf_op jit(solution)/shard_map/ppermute | solution.py:318
  7.9 5.8 %collective-permute-start = (f32[4,4,4,16,128]{4,3,2,1,0:T(8,128)S(1)}, f32[4,4,4,16,128]{4,3,2,1,0:T(8,128)S(1)}, u32[]{:S(2)}, u32[]{:S(2)}) collective-permute-start(f32[4,4,4,16,128]{4,3,2,1,0:T(8,128)S(1)} %get-tuple-element.28.own), channel_id=1, source_target_pairs={{0,1},{1,0},{2,3},{3,2},{4,5},{5,4},{6,7},{7,6},{8,9},{9,8},{10,11... | collective-permute-start | bytes 1572872 | tf_op jit(solution)/shard_map/ppermute | solution.py:318
  11.9 4.4 %collective-permute-start.5 = (f32[3,4,16,128]{3,2,1,0:T(8,128)S(1)}, f32[3,4,16,128]{3,2,1,0:T(8,128)S(1)}, u32[]{:S(2)}, u32[]{:S(2)}) collective-permute-start(f32[3,4,16,128]{3,2,1,0:T(8,128)S(1)} %get-tuple-element.35), channel_id=1, source_target_pairs={{0,1},{1,0},{2,3},{3,2},{4,5},{5,4},{6,7},{7,6},{8,9},{9,8},{10,11... | collective-permute-start | bytes 294920 | tf_op jit(solution)/shard_map/ppermute | solution.py:318
  12.0 1.7 %collective-permute-start.2 = (f32[3,4,4,2,128]{4,3,2,1,0:T(2,128)S(1)}, f32[3,4,4,2,128]{4,3,2,1,0:T(2,128)S(1)}, u32[]{:S(2)}, u32[]{:S(2)}) collective-permute-start(f32[3,4,4,2,128]{4,3,2,1,0:T(2,128)S(1)} %pad_maximum_fusion), channel_id=1, source_target_pairs={{0,1},{1,0},{2,3},{3,2},{4,5},{5,4},{6,7},{7,6},{8,9},{9,8},{10,11... | collective-permute-start | bytes 147464 | tf_op jit(solution)/shard_map/ppermute | solution.py:318
  12.5 3.7 %collective-permute-start.6 = (f32[4,4,2,128]{3,2,1,0:T(2,128)S(1)}, f32[4,4,2,128]{3,2,1,0:T(2,128)S(1)}, u32[]{:S(2)}, u32[]{:S(2)}) collective-permute-start(f32[4,4,2,128]{3,2,1,0:T(2,128)S(1)} %get-tuple-element.36), channel_id=1, source_target_pairs={{0,2},{2,0},{1,3},{3,1},{4,6},{6,4},{5,7},{7,5},{8,10},{10,8},{9,1... | collective-permute-start | bytes 49160 | tf_op jit(solution)/shard_map/ppermute | solution.py:318
  17.4 4.9 %collective-permute-start.8 = (f32[7,4,4,2,128]{4,3,2,1,0:T(2,128)S(1)}, f32[7,4,4,2,128]{4,3,2,1,0:T(2,128)S(1)}, u32[]{:S(2)}, u32[]{:S(2)}) collective-permute-start(f32[7,4,4,2,128]{4,3,2,1,0:T(2,128)S(1)} %get-tuple-element.39), channel_id=1, source_target_pairs={{0,2},{2,0},{1,3},{3,1},{4,6},{6,4},{5,7},{7,5},{8,10},{10,8},{9,1... | collective-permute-start | bytes 344072 | tf_op jit(solution)/shard_map/ppermute | solution.py:318
  18.6 5.7 %collective-permute-start.7 = (f32[4,4,4,16,128]{4,3,2,1,0:T(8,128)S(1)}, f32[4,4,4,16,128]{4,3,2,1,0:T(8,128)S(1)}, u32[]{:S(2)}, u32[]{:S(2)}) collective-permute-start(f32[4,4,4,16,128]{4,3,2,1,0:T(8,128)S(1)} %get-tuple-element.38.own), channel_id=1, source_target_pairs={{0,1},{1,0},{2,3},{3,2},{4,5},{5,4},{6,7},{7,6},{8,9},{9,8},{10,11... | collective-permute-start | bytes 1572872 | tf_op jit(solution)/shard_map/ppermute | solution.py:318
  18.6 5.6 %collective-permute-start.9 = (f32[232,128]{1,0:T(8,128)S(1)}, f32[232,128]{1,0:T(8,128)S(1)}, u32[]{:S(2)}, u32[]{:S(2)}) collective-permute-start(f32[232,128]{1,0:T(8,128)S(1)} %get-tuple-element.40), channel_id=1, source_target_pairs={{0,12},{4,0},{8,4},{12,8},{1,13},{5,1},{9,5},{13,9},{2,14},{6,2},{... | collective-permute-start | bytes 356360 | tf_op jit(solution)/shard_map/ppermute | solution.py:318
  24.9 4.5 %collective-permute-start.13 = (f32[2,4,4,2,128]{4,3,2,1,0:T(2,128)S(1)}, f32[2,4,4,2,128]{4,3,2,1,0:T(2,128)S(1)}, u32[]{:S(2)}, u32[]{:S(2)}) collective-permute-start(f32[2,4,4,2,128]{4,3,2,1,0:T(2,128)S(1)} %pad_maximum_fusion.1), channel_id=1, source_target_pairs={{0,1},{1,0},{2,3},{3,2},{4,5},{5,4},{6,7},{7,6},{8,9},{9,8},{10,11... | collective-permute-start | bytes 98312 | tf_op jit(solution)/shard_map/ppermute | solution.py:318
  24.9 7.8 %collective-permute-start.10 = (f32[4,16,128]{2,1,0:T(8,128)S(1)}, f32[4,16,128]{2,1,0:T(8,128)S(1)}, u32[]{:S(2)}, u32[]{:S(2)}) collective-permute-start(f32[4,16,128]{2,1,0:T(8,128)S(1)} %get-tuple-element.44), channel_id=1, source_target_pairs={{0,4},{4,8},{8,12},{12,0},{1,5},{5,9},{9,13},{13,1},{2,6},{6,10},{... | collective-permute-start | bytes 98312 | tf_op jit(solution)/shard_map/ppermute | solution.py:318
  25.9 6.9 %collective-permute-start.11 = (f32[4,16,128]{2,1,0:T(8,128)S(1)}, f32[4,16,128]{2,1,0:T(8,128)S(1)}, u32[]{:S(2)}, u32[]{:S(2)}) collective-permute-start(f32[4,16,128]{2,1,0:T(8,128)S(1)} %get-tuple-element.44), channel_id=1, source_target_pairs={{0,8},{4,12},{8,0},{12,4},{1,9},{5,13},{9,1},{13,5},{2,10},{6,14},... | collective-permute-start | bytes 98312 | tf_op jit(solution)/shard_map/ppermute | solution.py:318
  29.4 3.9 %collective-permute-start.12 = (f32[4,16,128]{2,1,0:T(8,128)S(1)}, f32[4,16,128]{2,1,0:T(8,128)S(1)}, u32[]{:S(2)}, u32[]{:S(2)}) collective-permute-start(f32[4,16,128]{2,1,0:T(8,128)S(1)} %get-tuple-element.44), channel_id=1, source_target_pairs={{0,12},{4,0},{8,4},{12,8},{1,13},{5,1},{9,5},{13,9},{2,14},{6,2},{... | collective-permute-start | bytes 98312 | tf_op jit(solution)/shard_map/ppermute | solution.py:318
  30.7 6.6 %collective-permute-start.16 = (f32[3,4,16,128]{3,2,1,0:T(8,128)S(1)}, f32[3,4,16,128]{3,2,1,0:T(8,128)S(1)}, u32[]{:S(2)}, u32[]{:S(2)}) collective-permute-start(f32[3,4,16,128]{3,2,1,0:T(8,128)S(1)} %get-tuple-element.50), channel_id=1, source_target_pairs={{0,4},{4,8},{8,12},{12,0},{1,5},{5,9},{9,13},{13,1},{2,6},{6,10},{... | collective-permute-start | bytes 294920 | tf_op jit(solution)/shard_map/ppermute | solution.py:318
  33.4 3.9 %collective-permute-start.15 = (f32[4,4,8,128]{3,2,1,0:T(8,128)S(1)}, f32[4,4,8,128]{3,2,1,0:T(8,128)S(1)}, u32[]{:S(2)}, u32[]{:S(2)}) collective-permute-start(f32[4,4,8,128]{3,2,1,0:T(8,128)S(1)} %get-tuple-element.49), channel_id=1, source_target_pairs={{0,1},{1,0},{2,3},{3,2},{4,5},{5,4},{6,7},{7,6},{8,9},{9,8},{10,11... | collective-permute-start | bytes 196616 | tf_op jit(solution)/shard_map/ppermute | solution.py:318
  33.5 3.8 %collective-permute-start.14 = (f32[4,4,2,128]{3,2,1,0:T(2,128)S(1)}, f32[4,4,2,128]{3,2,1,0:T(2,128)S(1)}, u32[]{:S(2)}, u32[]{:S(2)}) collective-permute-start(f32[4,4,2,128]{3,2,1,0:T(2,128)S(1)} %get-tuple-element.48), channel_id=1, source_target_pairs={{0,2},{2,0},{1,3},{3,1},{4,6},{6,4},{5,7},{7,5},{8,10},{10,8},{9,1... | collective-permute-start | bytes 49160 | tf_op jit(solution)/shard_map/ppermute | solution.py:318

commit v4 on v3

--- a/solution.py
+++ b/solution.py
@@ -372,7 +372,7 @@
     )
     t_above = rotated_by(t_dn, "tm", -1)
     xh = x_exchange(xs, 3)
-    par = rotated_by(links, "pair", 1)
+    par = rotated_by(after(links, xh), "pair", 1)
     layers = call(above_2, [layer, layer], [], t_above, weight=LONG)
     prefix, slab = call(
         temporal_2,

time: 38.4 us -> 37.8 us (0.984)
  starting transfers between devices: 20 us -> 19.3 us
    ppermute x17, starting transfers between devices: 20 us -> 19.3 us  [rotated_by(): return lax.ppermute(x, axis, [(i, (i + steps) % n) for i in range(n)])]
  transfers between devices with their start and end apart: 17 -> 17, of which waited for: 7 -> 9; matrix products, arithmetic and copies ran while one was open for 0% -> 0% of each run, Pallas kernels for 6% -> 6%
where the time goes in v4:
time: 37.8 us; the launch traced here: 37.6 us
  starting transfers between devices  19.3 us (51%)
  waiting for transfers between devices  12.1 us (32%)
  Pallas kernels  5 us (13%)
  local copies, waits for them, and re-layouts  1.05 us (3%)
    ppermute x17, starting transfers between devices, rotated_by(): return lax.ppermute(x, axis, [(i, (i + steps) % n) for i in range(n)])  19.3 us
    ppermute x17, waiting for transfers between devices, rotated_by(): return lax.ppermute(x, axis, [(i, (i + steps) % n) for i in range(n)])  12.1 us
    pallas_call x10, Pallas kernels, call(): pl.pallas_call(kernel, out_shape=shapes[0] if single else shapes, in_spec...  5 us
    unnamed x2, local copies, waits for them, and re-layouts  1.04 us
  transfers between devices with their start and end apart: 17, of which 9 were waited for; matrix products, arithmetic and copies ran while one was open for 0% of the time, Pallas kernels for 6%

profile of v4, /device:TPU:0, one launch (start us, length us, event | category | flops | bytes accessed | tf_op | source)
XLA Modules:
  0.0 37.6 jit_solution(11676281934378424528)
XLA Ops:
  0.0 1.0 %copy-done = f32[4,4,4,8,2,128]{5,4,3,2,1,0:T(2,128)S(1)} copy-done((f32[4,4,4,8,2,128]{5,4,3,2,1,0:T(2,128)S(1)}, f32[4,4,4,8,2,128]{5,4,3,2,1,0:T(2,128)}, u32[]{:S(2)}) %copy-start) | copy-done | bytes 524312
  1.1 3.1 %collective-permute-start.3 = (f32[4,4,16,128]{3,2,1,0:T(8,128)S(1)}, f32[4,4,16,128]{3,2,1,0:T(8,128)S(1)}, u32[]{:S(2)}, u32[]{:S(2)}) collective-permute-start(f32[4,4,16,128]{3,2,1,0:T(8,128)S(1)} %get-tuple-element.34), channel_id=1, source_target_pairs={{0,4},{4,8},{8,12},{12,0},{1,5},{5,9},{9,13},{13,1},{2,6},{6,10},{... | collective-permute-start | bytes 393224 | tf_op jit(solution)/shard_map/ppermute | solution.py:318
  4.2 1.5 %collective-permute-start.1 = (f32[7,4,4,2,128]{4,3,2,1,0:T(2,128)S(1)}, f32[7,4,4,2,128]{4,3,2,1,0:T(2,128)S(1)}, u32[]{:S(2)}, u32[]{:S(2)}) collective-permute-start(f32[7,4,4,2,128]{4,3,2,1,0:T(2,128)S(1)} %get-tuple-element.30), channel_id=1, source_target_pairs={{0,2},{2,0},{1,3},{3,1},{4,6},{6,4},{5,7},{7,5},{8,10},{10,8},{9,1... | collective-permute-start | bytes 344072 | tf_op jit(solution)/shard_map/ppermute | solution.py:318
  5.7 2.2 %collective-permute-start.4 = (f32[3,4,16,128]{3,2,1,0:T(8,128)S(1)}, f32[3,4,16,128]{3,2,1,0:T(8,128)S(1)}, u32[]{:S(2)}, u32[]{:S(2)}) collective-permute-start(f32[3,4,16,128]{3,2,1,0:T(8,128)S(1)} %get-tuple-element.35), channel_id=1, source_target_pairs={{0,12},{4,0},{8,4},{12,8},{1,13},{5,1},{9,5},{13,9},{2,14},{6,2},{... | collective-permute-start | bytes 294920 | tf_op jit(solution)/shard_map/ppermute | solution.py:318
  7.9 1.0 %collective-permute-done.1.xh = f32[7,4,4,2,128]{4,3,2,1,0:T(2,128)S(1)} collective-permute-done((f32[7,4,4,2,128]{4,3,2,1,0:T(2,128)S(1)}, f32[7,4,4,2,128]{4,3,2,1,0:T(2,128)S(1)}, u32[]{:S(2)}, u32[]{:S(2)}) %collective-permute-start.1) | collective-permute-done | bytes 114720 | tf_op jit(solution)/shard_map/ppermute | solution.py:318
  9.0 2.8 %collective-permute-done.4.t_above = f32[3,4,16,128]{3,2,1,0:T(8,128)S(1)} collective-permute-done((f32[3,4,16,128]{3,2,1,0:T(8,128)S(1)}, f32[3,4,16,128]{3,2,1,0:T(8,128)S(1)}, u32[]{:S(2)}, u32[]{:S(2)}) %collective-permute-start.4) | collective-permute-done | bytes 98336 | tf_op jit(solution)/shard_map/ppermute | solution.py:318
  12.0 0.6 %collective-permute-start.2 = (f32[3,4,4,2,128]{4,3,2,1,0:T(2,128)S(1)}, f32[3,4,4,2,128]{4,3,2,1,0:T(2,128)S(1)}, u32[]{:S(2)}, u32[]{:S(2)}) collective-permute-start(f32[3,4,4,2,128]{4,3,2,1,0:T(2,128)S(1)} %pad_maximum_fusion), channel_id=1, source_target_pairs={{0,1},{1,0},{2,3},{3,2},{4,5},{5,4},{6,7},{7,6},{8,9},{9,8},{10,11... | collective-permute-start | bytes 147464 | tf_op jit(solution)/shard_map/ppermute | solution.py:318
  12.5 1.2 %collective-permute-start.6 = (f32[4,4,2,128]{3,2,1,0:T(2,128)S(1)}, f32[4,4,2,128]{3,2,1,0:T(2,128)S(1)}, u32[]{:S(2)}, u32[]{:S(2)}) collective-permute-start(f32[4,4,2,128]{3,2,1,0:T(2,128)S(1)} %get-tuple-element.37), channel_id=1, source_target_pairs={{0,2},{2,0},{1,3},{3,1},{4,6},{6,4},{5,7},{7,5},{8,10},{10,8},{9,1... | collective-permute-start | bytes 49160 | tf_op jit(solution)/shard_map/ppermute | solution.py:318
  13.7 0.9 %shard_map.18 = (f32[4,4,4,32,128]{4,3,2,1,0:T(8,128)S(1)}, f32[4,4,4,32,128]{4,3,2,1,0:T(8,128)S(1)}, f32[4,4,4,16,128]{4,3,2,1,0:T(8,128)S(1)}) custom-call(f32[4,4,4,16,128]{4,3,2,1,0:T(8,128)S(1)} %get-tuple-element.29.own, f32[4,4,4,16,128]{4,3,2,1,0:T(8,128)S(1)} %collective-permute-done.par, f32[7,4,4,2,128]{4,3,2,1,0:T(2,128)S(1)} %collective-permute-done.1.xh, ...), custom_call_target="tpu_custom_call" | custom-call | flops 1 | bytes 1 | tf_op jit(solution)/shard_map/pallas_call | solution.py:305
  14.6 1.6 %collective-permute-done.6.corner = f32[4,4,2,128]{3,2,1,0:T(2,128)S(1)} collective-permute-done((f32[4,4,2,128]{3,2,1,0:T(2,128)S(1)}, f32[4,4,2,128]{3,2,1,0:T(2,128)S(1)}, u32[]{:S(2)}, u32[]{:S(2)}) %collective-permute-start.6) | collective-permute-done | bytes 16416 | tf_op jit(solution)/shard_map/ppermute | solution.py:318
  16.3 0.6 %shard_map.20 = (f32[232,128]{1,0:T(8,128)S(1)}, f32[4,4,16,128]{3,2,1,0:T(8,128)S(1)}) custom-call(f32[4,4,4,32,128]{4,3,2,1,0:T(8,128)S(1)} %get-tuple-element.31.eo, f32[4,4,4,32,128]{4,3,2,1,0:T(8,128)S(1)} %get-tuple-element.32.ep, f32[4,4,16,128]{3,2,1,0:T(8,128)S(1)} %collective-permute-done.3.t_below, ...), custom_call_target="tpu_custom_call" | custom-call | flops 1 | bytes 1 | tf_op jit(solution)/shard_map/pallas_call | solution.py:305
  17.4 1.2 %collective-permute-start.7 = (f32[7,4,4,2,128]{4,3,2,1,0:T(2,128)S(1)}, f32[7,4,4,2,128]{4,3,2,1,0:T(2,128)S(1)}, u32[]{:S(2)}, u32[]{:S(2)}) collective-permute-start(f32[7,4,4,2,128]{4,3,2,1,0:T(2,128)S(1)} %get-tuple-element.40), channel_id=1, source_target_pairs={{0,2},{2,0},{1,3},{3,1},{4,6},{6,4},{5,7},{7,5},{8,10},{10,8},{9,1... | collective-permute-start | bytes 344072 | tf_op jit(solution)/shard_map/ppermute | solution.py:318
  18.6 2.0 %collective-permute-start.9 = (f32[232,128]{1,0:T(8,128)S(1)}, f32[232,128]{1,0:T(8,128)S(1)}, u32[]{:S(2)}, u32[]{:S(2)}) collective-permute-start(f32[232,128]{1,0:T(8,128)S(1)} %get-tuple-element.42), channel_id=1, source_target_pairs={{0,12},{4,0},{8,4},{12,8},{1,13},{5,1},{9,5},{13,9},{2,14},{6,2},{... | collective-permute-start | bytes 356360 | tf_op jit(solution)/shard_map/ppermute | solution.py:318
  20.7 1.6 %collective-permute-done.7.xh = f32[7,4,4,2,128]{4,3,2,1,0:T(2,128)S(1)} collective-permute-done((f32[7,4,4,2,128]{4,3,2,1,0:T(2,128)S(1)}, f32[7,4,4,2,128]{4,3,2,1,0:T(2,128)S(1)}, u32[]{:S(2)}, u32[]{:S(2)}) %collective-permute-start.7) | collective-permute-done | bytes 114720 | tf_op jit(solution)/shard_map/ppermute | solution.py:318
  22.3 1.2 %collective-permute-done.9.t_above = f32[232,128]{1,0:T(8,128)S(1)} collective-permute-done((f32[232,128]{1,0:T(8,128)S(1)}, f32[232,128]{1,0:T(8,128)S(1)}, u32[]{:S(2)}, u32[]{:S(2)}) %collective-permute-start.9) | collective-permute-done | bytes 118816 | tf_op jit(solution)/shard_map/ppermute | solution.py:318
  23.5 0.7 %collective-permute-done.8.par = f32[4,4,4,16,128]{4,3,2,1,0:T(8,128)S(1)} collective-permute-done((f32[4,4,4,16,128]{4,3,2,1,0:T(8,128)S(1)}, f32[4,4,4,16,128]{4,3,2,1,0:T(8,128)S(1)}, u32[]{:S(2)}, u32[]{:S(2)}) %collective-permute-start.8) | collective-permute-done | bytes 524320 | tf_op jit(solution)/shard_map/ppermute | solution.py:318
  24.9 0.6 %collective-permute-start.10 = (f32[4,16,128]{2,1,0:T(8,128)S(1)}, f32[4,16,128]{2,1,0:T(8,128)S(1)}, u32[]{:S(2)}, u32[]{:S(2)}) collective-permute-start(f32[4,16,128]{2,1,0:T(8,128)S(1)} %get-tuple-element.46), channel_id=1, source_target_pairs={{0,4},{4,8},{8,12},{12,0},{1,5},{5,9},{9,13},{13,1},{2,6},{6,10},{... | collective-permute-start | bytes 98312 | tf_op jit(solution)/shard_map/ppermute | solution.py:318
  25.5 3.1 %collective-permute-start.11 = (f32[4,16,128]{2,1,0:T(8,128)S(1)}, f32[4,16,128]{2,1,0:T(8,128)S(1)}, u32[]{:S(2)}, u32[]{:S(2)}) collective-permute-start(f32[4,16,128]{2,1,0:T(8,128)S(1)} %get-tuple-element.46), channel_id=1, source_target_pairs={{0,8},{4,12},{8,0},{12,4},{1,9},{5,13},{9,1},{13,5},{2,10},{6,14},... | collective-permute-start | bytes 98312 | tf_op jit(solution)/shard_map/ppermute | solution.py:318
  28.9 1.3 %shard_map.24 = (f32[3,4,4,16,128]{4,3,2,1,0:T(8,128)S(1)}, f32[3,4,16,128]{3,2,1,0:T(8,128)S(1)}) custom-call(f32[4,4,4,16,128]{4,3,2,1,0:T(8,128)S(1)} %get-tuple-element.41.own, f32[4,4,4,16,128]{4,3,2,1,0:T(8,128)S(1)} %collective-permute-done.8.par, f32[7,4,4,2,128]{4,3,2,1,0:T(2,128)S(1)} %collective-permute-done.7.xh, ...), custom_call_target="tpu_custom_call" | custom-call | flops 1 | bytes 1 | tf_op jit(solution)/shard_map/pallas_call | solution.py:305
  30.2 1.7 %collective-permute-start.16 = (f32[3,4,16,128]{3,2,1,0:T(8,128)S(1)}, f32[3,4,16,128]{3,2,1,0:T(8,128)S(1)}, u32[]{:S(2)}, u32[]{:S(2)}) collective-permute-start(f32[3,4,16,128]{3,2,1,0:T(8,128)S(1)} %get-tuple-element.52), channel_id=1, source_target_pairs={{0,4},{4,8},{8,12},{12,0},{1,5},{5,9},{9,13},{13,1},{2,6},{6,10},{... | collective-permute-start | bytes 294920 | tf_op jit(solution)/shard_map/ppermute | solution.py:318
  32.0 0.5 %collective-permute-done.12.rest_2_ = f32[4,16,128]{2,1,0:T(8,128)S(1)} collective-permute-done((f32[4,16,128]{2,1,0:T(8,128)S(1)}, f32[4,16,128]{2,1,0:T(8,128)S(1)}, u32[]{:S(2)}, u32[]{:S(2)}) %collective-permute-start.12) | collective-permute-done | bytes 32800 | tf_op jit(solution)/shard_map/ppermute | solution.py:318
  32.7 1.4 %collective-permute-start.14 = (f32[4,4,2,128]{3,2,1,0:T(2,128)S(1)}, f32[4,4,2,128]{3,2,1,0:T(2,128)S(1)}, u32[]{:S(2)}, u32[]{:S(2)}) collective-permute-start(f32[4,4,2,128]{3,2,1,0:T(2,128)S(1)} %get-tuple-element.50), channel_id=1, source_target_pairs={{0,2},{2,0},{1,3},{3,1},{4,6},{6,4},{5,7},{7,5},{8,10},{10,8},{9,1... | collective-permute-start | bytes 49160 | tf_op jit(solution)/shard_map/ppermute | solution.py:318
  34.0 2.4 %collective-permute-done.14.nx = f32[4,4,2,128]{3,2,1,0:T(2,128)S(1)} collective-permute-done((f32[4,4,2,128]{3,2,1,0:T(2,128)S(1)}, f32[4,4,2,128]{3,2,1,0:T(2,128)S(1)}, u32[]{:S(2)}, u32[]{:S(2)}) %collective-permute-start.14) | collective-permute-done | bytes 16416 | tf_op jit(solution)/shard_map/ppermute | solution.py:318
  36.7 1.0 %shard_map.26 = f32[3,4,4,16,128]{4,3,2,1,0:T(8,128)} custom-call(f32[4,4,16,128]{3,2,1,0:T(8,128)S(1)} %get-tuple-element.49.gauge, f32[4,4,2,128]{3,2,1,0:T(2,128)S(1)} %collective-permute-done.14.nx, f32[4,4,8,128]{3,2,1,0:T(8,128)S(1)} %collective-permute-done.15.ny, f32[3,4,4,16,128]{4,3,2,1,0:T(8,128)S(1)} %get-tuple-element.48.rest_3_.links, ...), custom_call_target="tpu_custom_call" | custom-call | flops 1 | bytes 1 | tf_op jit(solution)/shard_map/pallas_call | solution.py:305
  (27 shorter events, 2.2 us)
Async XLA Ops:
  0.0 1.0 %copy-start = (f32[4,4,4,8,2,128]{5,4,3,2,1,0:T(2,128)S(1)}, f32[4,4,4,8,2,128]{5,4,3,2,1,0:T(2,128)}, u32[]{:S(2)}) copy-start(f32[4,4,4,8,2,128]{5,4,3,2,1,0:T(2,128)} %param.1) | copy-start | bytes 1572868
  1.1 10.7 %collective-permute-start.3 = (f32[4,4,16,128]{3,2,1,0:T(8,128)S(1)}, f32[4,4,16,128]{3,2,1,0:T(8,128)S(1)}, u32[]{:S(2)}, u32[]{:S(2)}) collective-permute-start(f32[4,4,16,128]{3,2,1,0:T(8,128)S(1)} %get-tuple-element.34), channel_id=1, source_target_pairs={{0,4},{4,8},{8,12},{12,0},{1,5},{5,9},{9,13},{13,1},{2,6},{6,10},{... | collective-permute-start | bytes 393224 | tf_op jit(solution)/shard_map/ppermute | solution.py:318
  4.2 4.8 %collective-permute-start.1 = (f32[7,4,4,2,128]{4,3,2,1,0:T(2,128)S(1)}, f32[7,4,4,2,128]{4,3,2,1,0:T(2,128)S(1)}, u32[]{:S(2)}, u32[]{:S(2)}) collective-permute-start(f32[7,4,4,2,128]{4,3,2,1,0:T(2,128)S(1)} %get-tuple-element.30), channel_id=1, source_target_pairs={{0,2},{2,0},{1,3},{3,1},{4,6},{6,4},{5,7},{7,5},{8,10},{10,8},{9,1... | collective-permute-start | bytes 344072 | tf_op jit(solution)/shard_map/ppermute | solution.py:318
  5.7 6.1 %collective-permute-start.4 = (f32[3,4,16,128]{3,2,1,0:T(8,128)S(1)}, f32[3,4,16,128]{3,2,1,0:T(8,128)S(1)}, u32[]{:S(2)}, u32[]{:S(2)}) collective-permute-start(f32[3,4,16,128]{3,2,1,0:T(8,128)S(1)} %get-tuple-element.35), channel_id=1, source_target_pairs={{0,12},{4,0},{8,4},{12,8},{1,13},{5,1},{9,5},{13,9},{2,14},{6,2},{... | collective-permute-start | bytes 294920 | tf_op jit(solution)/shard_map/ppermute | solution.py:318
  7.9 5.8 %collective-permute-start = (f32[4,4,4,16,128]{4,3,2,1,0:T(8,128)S(1)}, f32[4,4,4,16,128]{4,3,2,1,0:T(8,128)S(1)}, u32[]{:S(2)}, u32[]{:S(2)}) collective-permute-start(f32[4,4,4,16,128]{4,3,2,1,0:T(8,128)S(1)} %get-tuple-element.29.own), channel_id=1, source_target_pairs={{0,1},{1,0},{2,3},{3,2},{4,5},{5,4},{6,7},{7,6},{8,9},{9,8},{10,11... | collective-permute-start | bytes 1572872 | tf_op jit(solution)/shard_map/ppermute | solution.py:318
  11.9 4.4 %collective-permute-start.5 = (f32[3,4,16,128]{3,2,1,0:T(8,128)S(1)}, f32[3,4,16,128]{3,2,1,0:T(8,128)S(1)}, u32[]{:S(2)}, u32[]{:S(2)}) collective-permute-start(f32[3,4,16,128]{3,2,1,0:T(8,128)S(1)} %get-tuple-element.36), channel_id=1, source_target_pairs={{0,1},{1,0},{2,3},{3,2},{4,5},{5,4},{6,7},{7,6},{8,9},{9,8},{10,11... | collective-permute-start | bytes 294920 | tf_op jit(solution)/shard_map/ppermute | solution.py:318
  12.0 1.7 %collective-permute-start.2 = (f32[3,4,4,2,128]{4,3,2,1,0:T(2,128)S(1)}, f32[3,4,4,2,128]{4,3,2,1,0:T(2,128)S(1)}, u32[]{:S(2)}, u32[]{:S(2)}) collective-permute-start(f32[3,4,4,2,128]{4,3,2,1,0:T(2,128)S(1)} %pad_maximum_fusion), channel_id=1, source_target_pairs={{0,1},{1,0},{2,3},{3,2},{4,5},{5,4},{6,7},{7,6},{8,9},{9,8},{10,11... | collective-permute-start | bytes 147464 | tf_op jit(solution)/shard_map/ppermute | solution.py:318
  12.5 3.7 %collective-permute-start.6 = (f32[4,4,2,128]{3,2,1,0:T(2,128)S(1)}, f32[4,4,2,128]{3,2,1,0:T(2,128)S(1)}, u32[]{:S(2)}, u32[]{:S(2)}) collective-permute-start(f32[4,4,2,128]{3,2,1,0:T(2,128)S(1)} %get-tuple-element.37), channel_id=1, source_target_pairs={{0,2},{2,0},{1,3},{3,1},{4,6},{6,4},{5,7},{7,5},{8,10},{10,8},{9,1... | collective-permute-start | bytes 49160 | tf_op jit(solution)/shard_map/ppermute | solution.py:318
  17.4 4.9 %collective-permute-start.7 = (f32[7,4,4,2,128]{4,3,2,1,0:T(2,128)S(1)}, f32[7,4,4,2,128]{4,3,2,1,0:T(2,128)S(1)}, u32[]{:S(2)}, u32[]{:S(2)}) collective-permute-start(f32[7,4,4,2,128]{4,3,2,1,0:T(2,128)S(1)} %get-tuple-element.40), channel_id=1, source_target_pairs={{0,2},{2,0},{1,3},{3,1},{4,6},{6,4},{5,7},{7,5},{8,10},{10,8},{9,1... | collective-permute-start | bytes 344072 | tf_op jit(solution)/shard_map/ppermute | solution.py:318
  18.6 4.8 %collective-permute-start.9 = (f32[232,128]{1,0:T(8,128)S(1)}, f32[232,128]{1,0:T(8,128)S(1)}, u32[]{:S(2)}, u32[]{:S(2)}) collective-permute-start(f32[232,128]{1,0:T(8,128)S(1)} %get-tuple-element.42), channel_id=1, source_target_pairs={{0,12},{4,0},{8,4},{12,8},{1,13},{5,1},{9,5},{13,9},{2,14},{6,2},{... | collective-permute-start | bytes 356360 | tf_op jit(solution)/shard_map/ppermute | solution.py:318
  22.3 1.9 %collective-permute-start.8 = (f32[4,4,4,16,128]{4,3,2,1,0:T(8,128)S(1)}, f32[4,4,4,16,128]{4,3,2,1,0:T(8,128)S(1)}, u32[]{:S(2)}, u32[]{:S(2)}) collective-permute-start(f32[4,4,4,16,128]{4,3,2,1,0:T(8,128)S(1)} %get-tuple-element.41.own), channel_id=1, source_target_pairs={{0,1},{1,0},{2,3},{3,2},{4,5},{5,4},{6,7},{7,6},{8,9},{9,8},{10,11... | collective-permute-start | bytes 1572872 | tf_op jit(solution)/shard_map/ppermute | solution.py:318
  24.7 4.2 %collective-permute-start.13 = (f32[2,4,4,2,128]{4,3,2,1,0:T(2,128)S(1)}, f32[2,4,4,2,128]{4,3,2,1,0:T(2,128)S(1)}, u32[]{:S(2)}, u32[]{:S(2)}) collective-permute-start(f32[2,4,4,2,128]{4,3,2,1,0:T(2,128)S(1)} %pad_maximum_fusion.1), channel_id=1, source_target_pairs={{0,1},{1,0},{2,3},{3,2},{4,5},{5,4},{6,7},{7,6},{8,9},{9,8},{10,11... | collective-permute-start | bytes 98312 | tf_op jit(solution)/shard_map/ppermute | solution.py:318
  24.9 7.1 %collective-permute-start.10 = (f32[4,16,128]{2,1,0:T(8,128)S(1)}, f32[4,16,128]{2,1,0:T(8,128)S(1)}, u32[]{:S(2)}, u32[]{:S(2)}) collective-permute-start(f32[4,16,128]{2,1,0:T(8,128)S(1)} %get-tuple-element.46), channel_id=1, source_target_pairs={{0,4},{4,8},{8,12},{12,0},{1,5},{5,9},{9,13},{13,1},{2,6},{6,10},{... | collective-permute-start | bytes 98312 | tf_op jit(solution)/shard_map/ppermute | solution.py:318
  25.5 6.5 %collective-permute-start.11 = (f32[4,16,128]{2,1,0:T(8,128)S(1)}, f32[4,16,128]{2,1,0:T(8,128)S(1)}, u32[]{:S(2)}, u32[]{:S(2)}) collective-permute-start(f32[4,16,128]{2,1,0:T(8,128)S(1)} %get-tuple-element.46), channel_id=1, source_target_pairs={{0,8},{4,12},{8,0},{12,4},{1,9},{5,13},{9,1},{13,5},{2,10},{6,14},... | collective-permute-start | bytes 98312 | tf_op jit(solution)/shard_map/ppermute | solution.py:318
  28.6 3.9 %collective-permute-start.12 = (f32[4,16,128]{2,1,0:T(8,128)S(1)}, f32[4,16,128]{2,1,0:T(8,128)S(1)}, u32[]{:S(2)}, u32[]{:S(2)}) collective-permute-start(f32[4,16,128]{2,1,0:T(8,128)S(1)} %get-tuple-element.46), channel_id=1, source_target_pairs={{0,12},{4,0},{8,4},{12,8},{1,13},{5,1},{9,5},{13,9},{2,14},{6,2},{... | collective-permute-start | bytes 98312 | tf_op jit(solution)/shard_map/ppermute | solution.py:318
  30.2 6.5 %collective-permute-start.16 = (f32[3,4,16,128]{3,2,1,0:T(8,128)S(1)}, f32[3,4,16,128]{3,2,1,0:T(8,128)S(1)}, u32[]{:S(2)}, u32[]{:S(2)}) collective-permute-start(f32[3,4,16,128]{3,2,1,0:T(8,128)S(1)} %get-tuple-element.52), channel_id=1, source_target_pairs={{0,4},{4,8},{8,12},{12,0},{1,5},{5,9},{9,13},{13,1},{2,6},{6,10},{... | collective-permute-start | bytes 294920 | tf_op jit(solution)/shard_map/ppermute | solution.py:318
  32.6 3.9 %collective-permute-start.15 = (f32[4,4,8,128]{3,2,1,0:T(8,128)S(1)}, f32[4,4,8,128]{3,2,1,0:T(8,128)S(1)}, u32[]{:S(2)}, u32[]{:S(2)}) collective-permute-start(f32[4,4,8,128]{3,2,1,0:T(8,128)S(1)} %get-tuple-element.51), channel_id=1, source_target_pairs={{0,1},{1,0},{2,3},{3,2},{4,5},{5,4},{6,7},{7,6},{8,9},{9,8},{10,11... | collective-permute-start | bytes 196616 | tf_op jit(solution)/shard_map/ppermute | solution.py:318
  32.7 3.8 %collective-permute-start.14 = (f32[4,4,2,128]{3,2,1,0:T(2,128)S(1)}, f32[4,4,2,128]{3,2,1,0:T(2,128)S(1)}, u32[]{:S(2)}, u32[]{:S(2)}) collective-permute-start(f32[4,4,2,128]{3,2,1,0:T(2,128)S(1)} %get-tuple-element.50), channel_id=1, source_target_pairs={{0,2},{2,0},{1,3},{3,1},{4,6},{6,4},{5,7},{7,5},{8,10},{10,8},{9,1... | collective-permute-start | bytes 49160 | tf_op jit(solution)/shard_map/ppermute | solution.py:318

commit v5 on v4

--- a/solution.py
+++ b/solution.py
@@ -385,7 +385,7 @@
     )
     n = lax.axis_size("tm")
     slabs = [rotated_by(slab, "tm", k) for k in range(1, n)]
-    x_shared = rotated_by(after(jnp.stack([xh[1], xh[4]]), slab), "pair", 1)
+    x_shared = rotated_by(jnp.stack([xh[1], xh[4]]), "pair", 1)
     spatial = (3, 4, tl, rows, z)
     smeared, lows = call(
         spatial_2,

time: 37.8 us -> 37.9 us (level)
  transfers between devices with their start and end apart: 17 -> 17, of which waited for: 9 -> 9; matrix products, arithmetic and copies ran while one was open for 0% -> 0% of each run, Pallas kernels for 6% -> 8%
where the time goes in v5:
time: 37.9 us; the launch traced here: 37.7 us
  starting transfers between devices  19.6 us (52%)
  waiting for transfers between devices  11.9 us (31%)
  Pallas kernels  5 us (13%)
  local copies, waits for them, and re-layouts  1.05 us (3%)
    ppermute x17, starting transfers between devices, rotated_by(): return lax.ppermute(x, axis, [(i, (i + steps) % n) for i in range(n)])  19.6 us
    ppermute x17, waiting for transfers between devices, rotated_by(): return lax.ppermute(x, axis, [(i, (i + steps) % n) for i in range(n)])  11.9 us
    pallas_call x10, Pallas kernels, call(): pl.pallas_call(kernel, out_shape=shapes[0] if single else shapes, in_spec...  5 us
    unnamed x2, local copies, waits for them, and re-layouts  1.04 us
  transfers between devices with their start and end apart: 17, of which 9 were waited for; matrix products, arithmetic and copies ran while one was open for 0% of the time, Pallas kernels for 8%

profile of v5, /device:TPU:0, one launch (start us, length us, event | category | flops | bytes accessed | tf_op | source)
XLA Modules:
  0.0 37.7 jit_solution(16488036571715384909)
XLA Ops:
  0.0 1.0 %copy-done = f32[4,4,4,8,2,128]{5,4,3,2,1,0:T(2,128)S(1)} copy-done((f32[4,4,4,8,2,128]{5,4,3,2,1,0:T(2,128)S(1)}, f32[4,4,4,8,2,128]{5,4,3,2,1,0:T(2,128)}, u32[]{:S(2)}) %copy-start) | copy-done | bytes 524312
  1.1 3.1 %collective-permute-start.3 = (f32[4,4,16,128]{3,2,1,0:T(8,128)S(1)}, f32[4,4,16,128]{3,2,1,0:T(8,128)S(1)}, u32[]{:S(2)}, u32[]{:S(2)}) collective-permute-start(f32[4,4,16,128]{3,2,1,0:T(8,128)S(1)} %get-tuple-element.33), channel_id=1, source_target_pairs={{0,4},{4,8},{8,12},{12,0},{1,5},{5,9},{9,13},{13,1},{2,6},{6,10},{... | collective-permute-start | bytes 393224 | tf_op jit(solution)/shard_map/ppermute | solution.py:318
  4.2 1.5 %collective-permute-start.1 = (f32[7,4,4,2,128]{4,3,2,1,0:T(2,128)S(1)}, f32[7,4,4,2,128]{4,3,2,1,0:T(2,128)S(1)}, u32[]{:S(2)}, u32[]{:S(2)}) collective-permute-start(f32[7,4,4,2,128]{4,3,2,1,0:T(2,128)S(1)} %get-tuple-element.29), channel_id=1, source_target_pairs={{0,2},{2,0},{1,3},{3,1},{4,6},{6,4},{5,7},{7,5},{8,10},{10,8},{9,1... | collective-permute-start | bytes 344072 | tf_op jit(solution)/shard_map/ppermute | solution.py:318
  5.7 2.2 %collective-permute-start.4 = (f32[3,4,16,128]{3,2,1,0:T(8,128)S(1)}, f32[3,4,16,128]{3,2,1,0:T(8,128)S(1)}, u32[]{:S(2)}, u32[]{:S(2)}) collective-permute-start(f32[3,4,16,128]{3,2,1,0:T(8,128)S(1)} %get-tuple-element.34), channel_id=1, source_target_pairs={{0,12},{4,0},{8,4},{12,8},{1,13},{5,1},{9,5},{13,9},{2,14},{6,2},{... | collective-permute-start | bytes 294920 | tf_op jit(solution)/shard_map/ppermute | solution.py:318
  7.9 1.0 %collective-permute-done.1.xh = f32[7,4,4,2,128]{4,3,2,1,0:T(2,128)S(1)} collective-permute-done((f32[7,4,4,2,128]{4,3,2,1,0:T(2,128)S(1)}, f32[7,4,4,2,128]{4,3,2,1,0:T(2,128)S(1)}, u32[]{:S(2)}, u32[]{:S(2)}) %collective-permute-start.1) | collective-permute-done | bytes 114720 | tf_op jit(solution)/shard_map/ppermute | solution.py:318
  9.0 2.8 %collective-permute-done.4.t_above = f32[3,4,16,128]{3,2,1,0:T(8,128)S(1)} collective-permute-done((f32[3,4,16,128]{3,2,1,0:T(8,128)S(1)}, f32[3,4,16,128]{3,2,1,0:T(8,128)S(1)}, u32[]{:S(2)}, u32[]{:S(2)}) %collective-permute-start.4) | collective-permute-done | bytes 98336 | tf_op jit(solution)/shard_map/ppermute | solution.py:318
  12.0 0.6 %collective-permute-start.2 = (f32[3,4,4,2,128]{4,3,2,1,0:T(2,128)S(1)}, f32[3,4,4,2,128]{4,3,2,1,0:T(2,128)S(1)}, u32[]{:S(2)}, u32[]{:S(2)}) collective-permute-start(f32[3,4,4,2,128]{4,3,2,1,0:T(2,128)S(1)} %pad_maximum_fusion), channel_id=1, source_target_pairs={{0,1},{1,0},{2,3},{3,2},{4,5},{5,4},{6,7},{7,6},{8,9},{9,8},{10,11... | collective-permute-start | bytes 147464 | tf_op jit(solution)/shard_map/ppermute | solution.py:318
  12.5 1.2 %collective-permute-start.6 = (f32[4,4,2,128]{3,2,1,0:T(2,128)S(1)}, f32[4,4,2,128]{3,2,1,0:T(2,128)S(1)}, u32[]{:S(2)}, u32[]{:S(2)}) collective-permute-start(f32[4,4,2,128]{3,2,1,0:T(2,128)S(1)} %get-tuple-element.36), channel_id=1, source_target_pairs={{0,2},{2,0},{1,3},{3,1},{4,6},{6,4},{5,7},{7,5},{8,10},{10,8},{9,1... | collective-permute-start | bytes 49160 | tf_op jit(solution)/shard_map/ppermute | solution.py:318
  13.7 0.9 %shard_map.18 = (f32[4,4,4,32,128]{4,3,2,1,0:T(8,128)S(1)}, f32[4,4,4,32,128]{4,3,2,1,0:T(8,128)S(1)}, f32[4,4,4,16,128]{4,3,2,1,0:T(8,128)S(1)}) custom-call(f32[4,4,4,16,128]{4,3,2,1,0:T(8,128)S(1)} %get-tuple-element.28.own, f32[4,4,4,16,128]{4,3,2,1,0:T(8,128)S(1)} %collective-permute-done.par, f32[7,4,4,2,128]{4,3,2,1,0:T(2,128)S(1)} %collective-permute-done.1.xh, ...), custom_call_target="tpu_custom_call" | custom-call | flops 1 | bytes 1 | tf_op jit(solution)/shard_map/pallas_call | solution.py:305
  14.6 1.6 %collective-permute-done.6.corner = f32[4,4,2,128]{3,2,1,0:T(2,128)S(1)} collective-permute-done((f32[4,4,2,128]{3,2,1,0:T(2,128)S(1)}, f32[4,4,2,128]{3,2,1,0:T(2,128)S(1)}, u32[]{:S(2)}, u32[]{:S(2)}) %collective-permute-start.6) | collective-permute-done | bytes 16416 | tf_op jit(solution)/shard_map/ppermute | solution.py:318
  16.3 0.6 %shard_map.20 = (f32[232,128]{1,0:T(8,128)S(1)}, f32[4,4,16,128]{3,2,1,0:T(8,128)S(1)}) custom-call(f32[4,4,4,32,128]{4,3,2,1,0:T(8,128)S(1)} %get-tuple-element.30.eo, f32[4,4,4,32,128]{4,3,2,1,0:T(8,128)S(1)} %get-tuple-element.31.ep, f32[4,4,16,128]{3,2,1,0:T(8,128)S(1)} %collective-permute-done.3.t_below, ...), custom_call_target="tpu_custom_call" | custom-call | flops 1 | bytes 1 | tf_op jit(solution)/shard_map/pallas_call | solution.py:305
  17.4 1.2 %collective-permute-start.7 = (f32[7,4,4,2,128]{4,3,2,1,0:T(2,128)S(1)}, f32[7,4,4,2,128]{4,3,2,1,0:T(2,128)S(1)}, u32[]{:S(2)}, u32[]{:S(2)}) collective-permute-start(f32[7,4,4,2,128]{4,3,2,1,0:T(2,128)S(1)} %get-tuple-element.39), channel_id=1, source_target_pairs={{0,2},{2,0},{1,3},{3,1},{4,6},{6,4},{5,7},{7,5},{8,10},{10,8},{9,1... | collective-permute-start | bytes 344072 | tf_op jit(solution)/shard_map/ppermute | solution.py:318
  18.6 2.0 %collective-permute-start.9 = (f32[232,128]{1,0:T(8,128)S(1)}, f32[232,128]{1,0:T(8,128)S(1)}, u32[]{:S(2)}, u32[]{:S(2)}) collective-permute-start(f32[232,128]{1,0:T(8,128)S(1)} %get-tuple-element.41), channel_id=1, source_target_pairs={{0,12},{4,0},{8,4},{12,8},{1,13},{5,1},{9,5},{13,9},{2,14},{6,2},{... | collective-permute-start | bytes 356360 | tf_op jit(solution)/shard_map/ppermute | solution.py:318
  20.7 1.6 %collective-permute-done.7.xh = f32[7,4,4,2,128]{4,3,2,1,0:T(2,128)S(1)} collective-permute-done((f32[7,4,4,2,128]{4,3,2,1,0:T(2,128)S(1)}, f32[7,4,4,2,128]{4,3,2,1,0:T(2,128)S(1)}, u32[]{:S(2)}, u32[]{:S(2)}) %collective-permute-start.7) | collective-permute-done | bytes 114720 | tf_op jit(solution)/shard_map/ppermute | solution.py:318
  22.9 0.6 %collective-permute-done.9.t_above = f32[232,128]{1,0:T(8,128)S(1)} collective-permute-done((f32[232,128]{1,0:T(8,128)S(1)}, f32[232,128]{1,0:T(8,128)S(1)}, u32[]{:S(2)}, u32[]{:S(2)}) %collective-permute-start.9) | collective-permute-done | bytes 118816 | tf_op jit(solution)/shard_map/ppermute | solution.py:318
  23.5 0.9 %collective-permute-done.8.par = f32[4,4,4,16,128]{4,3,2,1,0:T(8,128)S(1)} collective-permute-done((f32[4,4,4,16,128]{4,3,2,1,0:T(8,128)S(1)}, f32[4,4,4,16,128]{4,3,2,1,0:T(8,128)S(1)}, u32[]{:S(2)}, u32[]{:S(2)}) %collective-permute-start.8) | collective-permute-done | bytes 524320 | tf_op jit(solution)/shard_map/ppermute | solution.py:318
  24.9 0.6 %collective-permute-start.10 = (f32[4,16,128]{2,1,0:T(8,128)S(1)}, f32[4,16,128]{2,1,0:T(8,128)S(1)}, u32[]{:S(2)}, u32[]{:S(2)}) collective-permute-start(f32[4,16,128]{2,1,0:T(8,128)S(1)} %get-tuple-element.45), channel_id=1, source_target_pairs={{0,4},{4,8},{8,12},{12,0},{1,5},{5,9},{9,13},{13,1},{2,6},{6,10},{... | collective-permute-start | bytes 98312 | tf_op jit(solution)/shard_map/ppermute | solution.py:318
  25.6 2.9 %collective-permute-start.11 = (f32[4,16,128]{2,1,0:T(8,128)S(1)}, f32[4,16,128]{2,1,0:T(8,128)S(1)}, u32[]{:S(2)}, u32[]{:S(2)}) collective-permute-start(f32[4,16,128]{2,1,0:T(8,128)S(1)} %get-tuple-element.45), channel_id=1, source_target_pairs={{0,8},{4,12},{8,0},{12,4},{1,9},{5,13},{9,1},{13,5},{2,10},{6,14},... | collective-permute-start | bytes 98312 | tf_op jit(solution)/shard_map/ppermute | solution.py:318
  29.0 1.3 %shard_map.24 = (f32[3,4,4,16,128]{4,3,2,1,0:T(8,128)S(1)}, f32[3,4,16,128]{3,2,1,0:T(8,128)S(1)}) custom-call(f32[4,4,4,16,128]{4,3,2,1,0:T(8,128)S(1)} %get-tuple-element.40.own, f32[4,4,4,16,128]{4,3,2,1,0:T(8,128)S(1)} %collective-permute-done.8.par, f32[7,4,4,2,128]{4,3,2,1,0:T(2,128)S(1)} %collective-permute-done.7.xh, ...), custom_call_target="tpu_custom_call" | custom-call | flops 1 | bytes 1 | tf_op jit(solution)/shard_map/pallas_call | solution.py:305
  30.3 1.6 %collective-permute-start.16 = (f32[3,4,16,128]{3,2,1,0:T(8,128)S(1)}, f32[3,4,16,128]{3,2,1,0:T(8,128)S(1)}, u32[]{:S(2)}, u32[]{:S(2)}) collective-permute-start(f32[3,4,16,128]{3,2,1,0:T(8,128)S(1)} %get-tuple-element.50), channel_id=1, source_target_pairs={{0,4},{4,8},{8,12},{12,0},{1,5},{5,9},{9,13},{13,1},{2,6},{6,10},{... | collective-permute-start | bytes 294920 | tf_op jit(solution)/shard_map/ppermute | solution.py:318
  31.9 0.5 %collective-permute-done.12.rest_2_ = f32[4,16,128]{2,1,0:T(8,128)S(1)} collective-permute-done((f32[4,16,128]{2,1,0:T(8,128)S(1)}, f32[4,16,128]{2,1,0:T(8,128)S(1)}, u32[]{:S(2)}, u32[]{:S(2)}) %collective-permute-start.12) | collective-permute-done | bytes 32800 | tf_op jit(solution)/shard_map/ppermute | solution.py:318
  32.6 1.4 %collective-permute-start.14 = (f32[4,4,2,128]{3,2,1,0:T(2,128)S(1)}, f32[4,4,2,128]{3,2,1,0:T(2,128)S(1)}, u32[]{:S(2)}, u32[]{:S(2)}) collective-permute-start(f32[4,4,2,128]{3,2,1,0:T(2,128)S(1)} %get-tuple-element.48), channel_id=1, source_target_pairs={{0,2},{2,0},{1,3},{3,1},{4,6},{6,4},{5,7},{7,5},{8,10},{10,8},{9,1... | collective-permute-start | bytes 49160 | tf_op jit(solution)/shard_map/ppermute | solution.py:318
  34.0 2.4 %collective-permute-done.14.nx = f32[4,4,2,128]{3,2,1,0:T(2,128)S(1)} collective-permute-done((f32[4,4,2,128]{3,2,1,0:T(2,128)S(1)}, f32[4,4,2,128]{3,2,1,0:T(2,128)S(1)}, u32[]{:S(2)}, u32[]{:S(2)}) %collective-permute-start.14) | collective-permute-done | bytes 16416 | tf_op jit(solution)/shard_map/ppermute | solution.py:318
  36.8 1.0 %shard_map.26 = f32[3,4,4,16,128]{4,3,2,1,0:T(8,128)} custom-call(f32[4,4,16,128]{3,2,1,0:T(8,128)S(1)} %get-tuple-element.47.gauge, f32[4,4,2,128]{3,2,1,0:T(2,128)S(1)} %collective-permute-done.14.nx, f32[4,4,8,128]{3,2,1,0:T(8,128)S(1)} %collective-permute-done.15.ny, f32[3,4,4,16,128]{4,3,2,1,0:T(8,128)S(1)} %get-tuple-element.46.rest_3_.links, ...), custom_call_target="tpu_custom_call" | custom-call | flops 1 | bytes 1 | tf_op jit(solution)/shard_map/pallas_call | solution.py:305
  (27 shorter events, 2.9 us)
Async XLA Ops:
  0.0 1.0 %copy-start = (f32[4,4,4,8,2,128]{5,4,3,2,1,0:T(2,128)S(1)}, f32[4,4,4,8,2,128]{5,4,3,2,1,0:T(2,128)}, u32[]{:S(2)}) copy-start(f32[4,4,4,8,2,128]{5,4,3,2,1,0:T(2,128)} %param.1) | copy-start | bytes 1572868
  1.1 10.7 %collective-permute-start.3 = (f32[4,4,16,128]{3,2,1,0:T(8,128)S(1)}, f32[4,4,16,128]{3,2,1,0:T(8,128)S(1)}, u32[]{:S(2)}, u32[]{:S(2)}) collective-permute-start(f32[4,4,16,128]{3,2,1,0:T(8,128)S(1)} %get-tuple-element.33), channel_id=1, source_target_pairs={{0,4},{4,8},{8,12},{12,0},{1,5},{5,9},{9,13},{13,1},{2,6},{6,10},{... | collective-permute-start | bytes 393224 | tf_op jit(solution)/shard_map/ppermute | solution.py:318
  4.2 4.8 %collective-permute-start.1 = (f32[7,4,4,2,128]{4,3,2,1,0:T(2,128)S(1)}, f32[7,4,4,2,128]{4,3,2,1,0:T(2,128)S(1)}, u32[]{:S(2)}, u32[]{:S(2)}) collective-permute-start(f32[7,4,4,2,128]{4,3,2,1,0:T(2,128)S(1)} %get-tuple-element.29), channel_id=1, source_target_pairs={{0,2},{2,0},{1,3},{3,1},{4,6},{6,4},{5,7},{7,5},{8,10},{10,8},{9,1... | collective-permute-start | bytes 344072 | tf_op jit(solution)/shard_map/ppermute | solution.py:318
  5.7 6.1 %collective-permute-start.4 = (f32[3,4,16,128]{3,2,1,0:T(8,128)S(1)}, f32[3,4,16,128]{3,2,1,0:T(8,128)S(1)}, u32[]{:S(2)}, u32[]{:S(2)}) collective-permute-start(f32[3,4,16,128]{3,2,1,0:T(8,128)S(1)} %get-tuple-element.34), channel_id=1, source_target_pairs={{0,12},{4,0},{8,4},{12,8},{1,13},{5,1},{9,5},{13,9},{2,14},{6,2},{... | collective-permute-start | bytes 294920 | tf_op jit(solution)/shard_map/ppermute | solution.py:318
  7.9 5.8 %collective-permute-start = (f32[4,4,4,16,128]{4,3,2,1,0:T(8,128)S(1)}, f32[4,4,4,16,128]{4,3,2,1,0:T(8,128)S(1)}, u32[]{:S(2)}, u32[]{:S(2)}) collective-permute-start(f32[4,4,4,16,128]{4,3,2,1,0:T(8,128)S(1)} %get-tuple-element.28.own), channel_id=1, source_target_pairs={{0,1},{1,0},{2,3},{3,2},{4,5},{5,4},{6,7},{7,6},{8,9},{9,8},{10,11... | collective-permute-start | bytes 1572872 | tf_op jit(solution)/shard_map/ppermute | solution.py:318
  11.9 4.4 %collective-permute-start.5 = (f32[3,4,16,128]{3,2,1,0:T(8,128)S(1)}, f32[3,4,16,128]{3,2,1,0:T(8,128)S(1)}, u32[]{:S(2)}, u32[]{:S(2)}) collective-permute-start(f32[3,4,16,128]{3,2,1,0:T(8,128)S(1)} %get-tuple-element.35), channel_id=1, source_target_pairs={{0,1},{1,0},{2,3},{3,2},{4,5},{5,4},{6,7},{7,6},{8,9},{9,8},{10,11... | collective-permute-start | bytes 294920 | tf_op jit(solution)/shard_map/ppermute | solution.py:318
  12.0 1.7 %collective-permute-start.2 = (f32[3,4,4,2,128]{4,3,2,1,0:T(2,128)S(1)}, f32[3,4,4,2,128]{4,3,2,1,0:T(2,128)S(1)}, u32[]{:S(2)}, u32[]{:S(2)}) collective-permute-start(f32[3,4,4,2,128]{4,3,2,1,0:T(2,128)S(1)} %pad_maximum_fusion), channel_id=1, source_target_pairs={{0,1},{1,0},{2,3},{3,2},{4,5},{5,4},{6,7},{7,6},{8,9},{9,8},{10,11... | collective-permute-start | bytes 147464 | tf_op jit(solution)/shard_map/ppermute | solution.py:318
  12.5 3.7 %collective-permute-start.6 = (f32[4,4,2,128]{3,2,1,0:T(2,128)S(1)}, f32[4,4,2,128]{3,2,1,0:T(2,128)S(1)}, u32[]{:S(2)}, u32[]{:S(2)}) collective-permute-start(f32[4,4,2,128]{3,2,1,0:T(2,128)S(1)} %get-tuple-element.36), channel_id=1, source_target_pairs={{0,2},{2,0},{1,3},{3,1},{4,6},{6,4},{5,7},{7,5},{8,10},{10,8},{9,1... | collective-permute-start | bytes 49160 | tf_op jit(solution)/shard_map/ppermute | solution.py:318
  17.4 4.9 %collective-permute-start.7 = (f32[7,4,4,2,128]{4,3,2,1,0:T(2,128)S(1)}, f32[7,4,4,2,128]{4,3,2,1,0:T(2,128)S(1)}, u32[]{:S(2)}, u32[]{:S(2)}) collective-permute-start(f32[7,4,4,2,128]{4,3,2,1,0:T(2,128)S(1)} %get-tuple-element.39), channel_id=1, source_target_pairs={{0,2},{2,0},{1,3},{3,1},{4,6},{6,4},{5,7},{7,5},{8,10},{10,8},{9,1... | collective-permute-start | bytes 344072 | tf_op jit(solution)/shard_map/ppermute | solution.py:318
  18.6 4.8 %collective-permute-start.9 = (f32[232,128]{1,0:T(8,128)S(1)}, f32[232,128]{1,0:T(8,128)S(1)}, u32[]{:S(2)}, u32[]{:S(2)}) collective-permute-start(f32[232,128]{1,0:T(8,128)S(1)} %get-tuple-element.41), channel_id=1, source_target_pairs={{0,12},{4,0},{8,4},{12,8},{1,13},{5,1},{9,5},{13,9},{2,14},{6,2},{... | collective-permute-start | bytes 356360 | tf_op jit(solution)/shard_map/ppermute | solution.py:318
  22.3 6.7 %collective-permute-start.13 = (f32[2,4,4,2,128]{4,3,2,1,0:T(2,128)S(1)}, f32[2,4,4,2,128]{4,3,2,1,0:T(2,128)S(1)}, u32[]{:S(2)}, u32[]{:S(2)}) collective-permute-start(f32[2,4,4,2,128]{4,3,2,1,0:T(2,128)S(1)} %pad_maximum_fusion.1), channel_id=1, source_target_pairs={{0,1},{1,0},{2,3},{3,2},{4,5},{5,4},{6,7},{7,6},{8,9},{9,8},{10,11... | collective-permute-start | bytes 98312 | tf_op jit(solution)/shard_map/ppermute | solution.py:318
  22.4 2.0 %collective-permute-start.8 = (f32[4,4,4,16,128]{4,3,2,1,0:T(8,128)S(1)}, f32[4,4,4,16,128]{4,3,2,1,0:T(8,128)S(1)}, u32[]{:S(2)}, u32[]{:S(2)}) collective-permute-start(f32[4,4,4,16,128]{4,3,2,1,0:T(8,128)S(1)} %get-tuple-element.40.own), channel_id=1, source_target_pairs={{0,1},{1,0},{2,3},{3,2},{4,5},{5,4},{6,7},{7,6},{8,9},{9,8},{10,11... | collective-permute-start | bytes 1572872 | tf_op jit(solution)/shard_map/ppermute | solution.py:318
  24.9 6.9 %collective-permute-start.10 = (f32[4,16,128]{2,1,0:T(8,128)S(1)}, f32[4,16,128]{2,1,0:T(8,128)S(1)}, u32[]{:S(2)}, u32[]{:S(2)}) collective-permute-start(f32[4,16,128]{2,1,0:T(8,128)S(1)} %get-tuple-element.45), channel_id=1, source_target_pairs={{0,4},{4,8},{8,12},{12,0},{1,5},{5,9},{9,13},{13,1},{2,6},{6,10},{... | collective-permute-start | bytes 98312 | tf_op jit(solution)/shard_map/ppermute | solution.py:318
  25.6 6.3 %collective-permute-start.11 = (f32[4,16,128]{2,1,0:T(8,128)S(1)}, f32[4,16,128]{2,1,0:T(8,128)S(1)}, u32[]{:S(2)}, u32[]{:S(2)}) collective-permute-start(f32[4,16,128]{2,1,0:T(8,128)S(1)} %get-tuple-element.45), channel_id=1, source_target_pairs={{0,8},{4,12},{8,0},{12,4},{1,9},{5,13},{9,1},{13,5},{2,10},{6,14},... | collective-permute-start | bytes 98312 | tf_op jit(solution)/shard_map/ppermute | solution.py:318
  28.5 3.9 %collective-permute-start.12 = (f32[4,16,128]{2,1,0:T(8,128)S(1)}, f32[4,16,128]{2,1,0:T(8,128)S(1)}, u32[]{:S(2)}, u32[]{:S(2)}) collective-permute-start(f32[4,16,128]{2,1,0:T(8,128)S(1)} %get-tuple-element.45), channel_id=1, source_target_pairs={{0,12},{4,0},{8,4},{12,8},{1,13},{5,1},{9,5},{13,9},{2,14},{6,2},{... | collective-permute-start | bytes 98312 | tf_op jit(solution)/shard_map/ppermute | solution.py:318
  30.3 6.5 %collective-permute-start.16 = (f32[3,4,16,128]{3,2,1,0:T(8,128)S(1)}, f32[3,4,16,128]{3,2,1,0:T(8,128)S(1)}, u32[]{:S(2)}, u32[]{:S(2)}) collective-permute-start(f32[3,4,16,128]{3,2,1,0:T(8,128)S(1)} %get-tuple-element.50), channel_id=1, source_target_pairs={{0,4},{4,8},{8,12},{12,0},{1,5},{5,9},{9,13},{13,1},{2,6},{6,10},{... | collective-permute-start | bytes 294920 | tf_op jit(solution)/shard_map/ppermute | solution.py:318
  32.5 3.9 %collective-permute-start.15 = (f32[4,4,8,128]{3,2,1,0:T(8,128)S(1)}, f32[4,4,8,128]{3,2,1,0:T(8,128)S(1)}, u32[]{:S(2)}, u32[]{:S(2)}) collective-permute-start(f32[4,4,8,128]{3,2,1,0:T(8,128)S(1)} %get-tuple-element.49), channel_id=1, source_target_pairs={{0,1},{1,0},{2,3},{3,2},{4,5},{5,4},{6,7},{7,6},{8,9},{9,8},{10,11... | collective-permute-start | bytes 196616 | tf_op jit(solution)/shard_map/ppermute | solution.py:318
  32.6 3.8 %collective-permute-start.14 = (f32[4,4,2,128]{3,2,1,0:T(2,128)S(1)}, f32[4,4,2,128]{3,2,1,0:T(2,128)S(1)}, u32[]{:S(2)}, u32[]{:S(2)}) collective-permute-start(f32[4,4,2,128]{3,2,1,0:T(2,128)S(1)} %get-tuple-element.48), channel_id=1, source_target_pairs={{0,2},{2,0},{1,3},{3,1},{4,6},{6,4},{5,7},{7,5},{8,10},{10,8},{9,1... | collective-permute-start | bytes 49160 | tf_op jit(solution)/shard_map/ppermute | solution.py:318
